TPU v7x, 128 devices: a whole 4x4x4 slice. The times are simulated.
128 devices in a mesh: chan: 16 (over x, y_hi, core), tm: 8 (over y_lo, z).
Axes of the slice: x: 4, y: 4 (y_hi: 2, y_lo: 2; y = y_hi * 2 + y_lo), z: 4, core: 2. Of those that a mesh axis runs over, the one named last changes fastest.
Arguments:
- record: bfloat16 [10240, 16384], P('chan', 'tm'), may hold values from -6 to 6
- channel_ok: int32 [10240], P('chan'), may hold values 0 or 1
- fan_bounds: int32 [2, 8193], replicated, may hold values from 0 to 5120, as said below
Outputs:
- slowness: float32 [10240, 16384], P('chan', 'tm')
Inputs may be any that keep to these rules, and one draw needn't show every extreme that they name: fan_bounds[0, g] <= fan_bounds[1, g] for every g; fan_bounds[0, 0] is 0 and fan_bounds[1, 8192] is 5120.
All inputs are finite; a program needn't handle non-finite values. No bound on the sum of `channel_ok` on one device may be relied on, other than what follows from the above.
Results may differ from a plain program's by a relative error of at most 0.0063.
Values may be sent and summed in bfloat16 or wider, within the bound.
No kernel may reach another device: no remote copies, remote signals or barrier semaphores. Data moves between devices by JAX's collectives and lax.ppermute only.
A program may use at most 128 MiB of HBM per device.

v0:
```python
import math

import jax
import jax.numpy as jnp
from jax import lax
from jax.sharding import PartitionSpec as P

NC = 10240
NT = 16384
TF = 128
R = 4


def padded_2(cells, sides, width):
    for axis, dim in sides:
        count = lax.axis_size(axis)
        ends = count - 1
        head = lax.slice_in_dim(cells, 0, width, axis=dim)
        tail = lax.slice_in_dim(cells, cells.shape[dim] - width, cells.shape[dim], axis=dim)
        cells = jnp.concatenate(
            [
                lax.ppermute(tail, axis, [(i, (i + 1) % count) for i in range(ends)]),
                cells,
                lax.ppermute(head, axis, [((i + 1) % count, i) for i in range(ends)]),
            ],
            axis=dim,
        )
    return cells


def contract(pattern, left_arg, right_arg):
    return jnp.einsum(
        pattern,
        left_arg,
        right_arg,
        precision=lax.Precision.HIGH,
        preferred_element_type=jnp.float32,
    )


def rotations(row_digits, col_digits, length):
    phase_int = row_digits[:, None] * col_digits[None, :] % length
    angles = phase_int.astype(jnp.float32) * (2.0 * math.pi / length)
    return (jnp.cos(angles), jnp.sin(angles))


def time_forward(samples, keep):
    row_count = samples.shape[0]
    signal = samples.astype(jnp.float32).reshape(row_count, TF, TF)
    digits = jnp.arange(TF, dtype=jnp.int32)
    cos_w, sin_w = rotations(digits, digits, TF)
    tw_cos, tw_sin = rotations(digits, digits, TF * TF)
    first_re = contract("rmn,km->rkn", signal, cos_w)
    first_im = -contract("rmn,km->rkn", signal, sin_w)
    turned_re = first_re * tw_cos + first_im * tw_sin
    turned_im = first_im * tw_cos - first_re * tw_sin
    spec_re = contract("rkn,jn->rkj", turned_re, cos_w) + contract("rkn,jn->rkj", turned_im, sin_w)
    spec_im = contract("rkn,jn->rkj", turned_im, cos_w) - contract("rkn,jn->rkj", turned_re, sin_w)
    return (
        spec_re.reshape(row_count, TF * keep).astype(jnp.bfloat16),
        spec_im.reshape(row_count, TF * keep).astype(jnp.bfloat16),
    )


def time_inverse(back_re, back_im):
    row_count = back_re.shape[0]
    part_re = back_re.astype(jnp.float32).reshape(row_count, TF, TF)
    part_im = back_im.astype(jnp.float32).reshape(row_count, TF, TF)
    digits = jnp.arange(TF, dtype=jnp.int32)
    cos_w, sin_w = rotations(digits, digits, TF)
    tw_cos, tw_sin = rotations(digits, digits, TF * TF)
    mixed_re = contract("rkj,jn->rkn", part_re, cos_w) - contract("rkj,jn->rkn", part_im, sin_w)
    mixed_im = contract("rkj,jn->rkn", part_im, cos_w) + contract("rkj,jn->rkn", part_re, sin_w)
    turned_re = mixed_re * tw_cos - mixed_im * tw_sin
    turned_im = mixed_im * tw_cos + mixed_re * tw_sin
    result = contract("rkn,km->rmn", turned_re, cos_w) - contract("rkn,km->rmn", turned_im, sin_w)
    return (result / NT).reshape(row_count, NT).astype(jnp.bfloat16)


def reversed_waves(values):
    along_outer = jnp.roll(jnp.flip(values, 0), 1, axis=0)
    along_inner = jnp.flip(along_outer, 1)
    first_row = jnp.roll(along_inner[0:1], 1, axis=1)
    return jnp.concatenate([first_row, along_inner[1:]], axis=0)


def channel_filter(
    pencil_re, pencil_im, position, lower_bound, upper_bound, top_low, top_high, packed
):
    devices = position.shape[0]
    row_depth = NC // devices
    columns = pencil_re.shape[1]
    part_re = pencil_re.astype(jnp.float32).reshape(devices, row_depth, columns)
    part_im = pencil_im.astype(jnp.float32).reshape(devices, row_depth, columns)
    outer_digits = jnp.arange(devices, dtype=jnp.int32)
    inner_digits = jnp.arange(row_depth, dtype=jnp.int32)
    cos_a, sin_a = rotations(outer_digits, position, devices)
    cos_b, sin_b = rotations(inner_digits, inner_digits, row_depth)
    tw_cos, tw_sin = rotations(outer_digits, inner_digits, NC)
    tw_cos = tw_cos[:, :, None]
    tw_sin = tw_sin[:, :, None]
    first_re = contract("pbf,kp->kbf", part_re, cos_a) + contract("pbf,kp->kbf", part_im, sin_a)
    first_im = contract("pbf,kp->kbf", part_im, cos_a) - contract("pbf,kp->kbf", part_re, sin_a)
    turned_re = first_re * tw_cos + first_im * tw_sin
    turned_im = first_im * tw_cos - first_re * tw_sin
    wave_re = contract("kbf,jb->kjf", turned_re, cos_b) + contract("kbf,jb->kjf", turned_im, sin_b)
    wave_im = contract("kbf,jb->kjf", turned_im, cos_b) - contract("kbf,jb->kjf", turned_re, sin_b)
    number = outer_digits[:, None] + devices * inner_digits[None, :]
    folded = jnp.minimum(number, NC - number)
    passing = (
        (folded[:, :, None] >= lower_bound[None, None, :])
        & (folded[:, :, None] <= upper_bound[None, None, :])
    ).astype(jnp.float32)
    top_pass = ((folded >= top_low) & (folded <= top_high)).astype(jnp.float32)
    first_pass = passing[:, :, 0]
    column_re = wave_re[:, :, 0]
    column_im = wave_im[:, :, 0]
    mirror_re = reversed_waves(column_re)
    mirror_im = reversed_waves(column_im)
    even_part = (first_pass + top_pass) * 0.5
    odd_part = (first_pass - top_pass) * 0.5
    split_re = even_part * column_re + odd_part * mirror_re
    split_im = even_part * column_im - odd_part * mirror_im
    wave_re = wave_re * passing
    wave_im = wave_im * passing
    wave_re = wave_re.at[:, :, 0].set(packed * split_re + (1.0 - packed) * wave_re[:, :, 0])
    wave_im = wave_im.at[:, :, 0].set(packed * split_im + (1.0 - packed) * wave_im[:, :, 0])
    back_re = contract("kjf,jb->kbf", wave_re, cos_b) - contract("kjf,jb->kbf", wave_im, sin_b)
    back_im = contract("kjf,jb->kbf", wave_im, cos_b) + contract("kjf,jb->kbf", wave_re, sin_b)
    untwist_re = back_re * tw_cos - back_im * tw_sin
    untwist_im = back_im * tw_cos + back_re * tw_sin
    out_re = contract("kbf,kp->pbf", untwist_re, cos_a) - contract("kbf,kp->pbf", untwist_im, sin_a)
    out_im = contract("kbf,kp->pbf", untwist_im, cos_a) + contract("kbf,kp->pbf", untwist_re, sin_a)
    return (
        (out_re / NC).reshape(NC, columns).astype(jnp.bfloat16),
        (out_im / NC).reshape(NC, columns).astype(jnp.bfloat16),
    )


def box_sum(values, dim_index, radius):
    length = values.shape[dim_index] - 2 * radius
    running = lax.slice_in_dim(values, 0, length, axis=dim_index)
    for offset in range(1, 2 * radius + 1):
        running = running + lax.slice_in_dim(values, offset, offset + length, axis=dim_index)
    return running


def gradients(padded):
    grad_chan = (padded[2:, 1:-1] - padded[:-2, 1:-1]) * 0.5
    grad_time = (padded[1:-1, 2:] - padded[1:-1, :-2]) * 0.5
    return (grad_chan, grad_time)


def per_device(record, channel_ok, fan_bounds):
    chan_count = lax.axis_size("chan")
    time_count = lax.axis_size("tm")
    devices = chan_count * time_count
    tile_chan, tile_time = record.shape
    radius = R
    tiles = record * channel_ok.astype(jnp.bfloat16)[:, None]
    series = lax.all_to_all(tiles, "tm", split_axis=0, concat_axis=1, tiled=True)
    block_index = lax.axis_index("chan") * time_count + lax.axis_index("tm")
    top_low = fan_bounds[0, NT // 2]
    top_high = fan_bounds[1, NT // 2]
    spec_re, spec_im = time_forward(series, TF)
    columns = NT // devices
    folded_table = jnp.concatenate([fan_bounds, fan_bounds[:, 1 : NT // 2][:, ::-1]], axis=1)
    ordered = folded_table.reshape(2, TF, TF).transpose(0, 2, 1).reshape(2, NT)
    packed = jnp.float32(0.0)
    window = lax.dynamic_slice_in_dim(ordered, block_index * columns, columns, 1)
    slot_index = jnp.arange(devices, dtype=jnp.int32)
    pencil_re, pencil_im = (
        lax.all_to_all(spec_re, ("chan", "tm"), split_axis=1, concat_axis=0, tiled=True),
        lax.all_to_all(spec_im, ("chan", "tm"), split_axis=1, concat_axis=0, tiled=True),
    )
    filt_re, filt_im = channel_filter(
        pencil_re, pencil_im, slot_index, window[0], window[1], top_low, top_high, packed
    )
    back_re, back_im = (
        lax.all_to_all(filt_re, ("chan", "tm"), split_axis=0, concat_axis=1, tiled=True),
        lax.all_to_all(filt_im, ("chan", "tm"), split_axis=0, concat_axis=1, tiled=True),
    )
    filtered_rows = time_inverse(back_re, back_im)
    filtered = lax.all_to_all(filtered_rows, "tm", split_axis=1, concat_axis=0, tiled=True)
    padded = padded_2(filtered, (("chan", 0), ("tm", 1)), radius + 1).astype(jnp.float32)
    grad_chan, grad_time = gradients(padded)
    chan_pos = (
        lax.axis_index("chan") * tile_chan
        - radius
        + jnp.arange(tile_chan + 2 * radius, dtype=jnp.int32)
    )
    time_pos = (
        lax.axis_index("tm") * tile_time
        - radius
        + jnp.arange(tile_time + 2 * radius, dtype=jnp.int32)
    )
    chan_in = (chan_pos >= 0) & (chan_pos < NC)
    time_in = (time_pos >= 0) & (time_pos < NT)
    weight = (chan_in[:, None] & time_in[None, :]).astype(jnp.float32)
    products = jnp.stack([grad_chan * grad_time * weight, grad_time * grad_time * weight])
    summed = box_sum(box_sum(products, 1, radius), 2, radius)
    window_area = (2 * radius + 1) * (2 * radius + 1)
    cross_mean = summed[0] / window_area
    along_mean = summed[1] / window_area
    return -cross_mean / (along_mean + 1e-05)


def solution(mesh):
    in_specs = (P("chan", "tm"), P("chan"), P())
    out_specs = P("chan", "tm")
    return jax.shard_map(
        per_device, mesh=mesh, in_specs=in_specs, out_specs=out_specs, check_vma=False
    )
```

profile of v0, /device:TPU:1, one launch (start us, length us, event | category | flops | bytes accessed | tf_op | source)
XLA Modules:
  0.0 542.5 jit_solution(2788104700288146665)
XLA Ops:
  0.7 3.5 broadcast_multiply_fusion
  4.2 6.9 %all-to-all-start = ((bf16[8,80,2048]{2,1,0:T(8,128)(2,1)}), bf16[8,80,2048]{2,1,0:T(8,128)(2,1)S(1)}, u32[]{:S(2)}, u32[]{:S(2)}) async-start(bf16[8,80,2048]{2,1,0:T(8,128)(2,1)} %bitcast.217), calls=%async_computation | async-start | bytes 5242880 | tf_op jit(solution)/shard_map/all_to_all | solution.py:161
  11.8 31.0 %all-to-all-done = bf16[8,80,2048]{2,1,0:T(8,128)(2,1)S(1)} async-done(((bf16[8,80,2048]{2,1,0:T(8,128)(2,1)}), bf16[8,80,2048]{2,1,0:T(8,128)(2,1)S(1)}, u32[]{:S(2)}, u32[]{:S(2)}) %all-to-all-start) | async-done | bytes 2621472 | tf_op jit(solution)/shard_map/all_to_all | solution.py:161
  45.7 3.9 reshape.263
  56.0 3.7 subtract_convert_fusion
  63.0 8.8 %all-to-all-start.2 = ((bf16[80,128,128]{2,0,1:T(8,128)(2,1)}), bf16[80,128,128]{2,0,1:T(8,128)(2,1)}, u32[]{:S(2)}, u32[]{:S(2)}) async-start(bf16[80,128,128]{2,0,1:T(8,128)(2,1)} %copy.289), calls=%async_computation.2 | async-start | bytes 5242880 | tf_op jit(solution)/shard_map/all_to_all | solution.py:174
  71.8 5.9 %fusion.29 = f32[80,128,128]{2,1,0:T(8,128)S(1)} fusion(f32[128,80,128]{2,0,1:T(8,128)} %copy-done.1, f32[128,80,128]{2,0,1:T(8,128)} %copy-done, f32[128,128]{1,0:T(8,128)S(1)} %copy.281, f32[128,128]{1,0:T(8,128)S(1)} %copy.279), kind=kOutput, calls=%fused_computation.64 | convolution fusion | flops 1012105216 | bytes 15859712 | tf_op jit(solution)/shard_map/rkn,jn->rkj/dot_general | solution.py:32
  77.8 5.3 add_convert_fusion
  86.3 20.9 %all-to-all-done.2 = bf16[80,128,128]{2,0,1:T(8,128)(2,1)} async-done(((bf16[80,128,128]{2,0,1:T(8,128)(2,1)}), bf16[80,128,128]{2,0,1:T(8,128)(2,1)}, u32[]{:S(2)}, u32[]{:S(2)}) %all-to-all-start.2) | async-done | bytes 2621472 | tf_op jit(solution)/shard_map/all_to_all | solution.py:174
  107.2 5.1 all-to-all-start.1
  112.5 5.6 %reverse.16 = s32[2,8192]{1,0:T(2,128)S(1)} reverse(s32[2,8192]{1,0:T(2,128)S(1)} %bitcast.220), dimensions={1} | reverse | bytes 131072
  121.7 5.9 %fusion.54 = f32[128,80,128]{2,0,1:T(8,128)} fusion(bf16[80,128,128]{2,0,1:T(8,128)(2,1)} %all-to-all-done.2), kind=kOutput, calls=%fused_computation.104 | convolution fusion | flops 1006862336 | bytes 7864320 | tf_op jit(solution)/shard_map/pbf,kp->kbf/dot_general | solution.py:32
  127.6 5.9 %fusion.52 = f32[128,80,128]{2,0,1:T(8,128)} fusion(bf16[80,128,128]{2,0,1:T(8,128)(2,1)} %all-to-all-done.2), kind=kOutput, calls=%fused_computation.102 | convolution fusion | flops 1006862336 | bytes 7864320 | tf_op jit(solution)/shard_map/pbf,kp->kbf/dot_general | solution.py:32
  133.5 14.6 %all-to-all-done.1 = bf16[80,128,128]{2,0,1:T(8,128)(2,1)S(1)} async-done(((bf16[80,128,128]{2,0,1:T(8,128)(2,1)}), bf16[80,128,128]{2,0,1:T(8,128)(2,1)S(1)}, u32[]{:S(2)}, u32[]{:S(2)}) %all-to-all-start.1) | async-done | bytes 2621472 | tf_op jit(solution)/shard_map/all_to_all | solution.py:173
  148.1 4.6 fusion.64
  152.7 8.0 %multiply_add_fusion = (f32[128,80,128]{2,0,1:T(8,128)}, f32[128,80,128]{2,0,1:T(8,128)}) fusion(f32[128,80,128]{2,0,1:T(8,128)S(1)} %fusion.64, f32[128,80]{0,1:T(8,128)S(1)} %get-tuple-element.48, f32[128,80]{0,1:T(8,128)S(1)} %get-tuple-element.49, f32[128,80,128]{2,0,1:T(8,128)S(1)} %copy-done.8, bf16[80,128,128]{2,0,1:T(8,128)(2,1)S(1)} %all-to-all-done.1), kind=kOutput, calls=%fused_computation.86 | convolution fusion | flops 1016037376 | bytes 23674880 | tf_op jit(solution)/shard_map/pbf,kp->kbf/dot_general | solution.py:32
  160.6 6.4 %copy.341 = f32[128,80,128]{0,1,2:T(8,128)} copy(f32[128,80,128]{2,0,1:T(8,128)} %get-tuple-element.32) | data formatting | bytes 10485760 | tf_op jit(solution)/shard_map/sub | solution.py:105
  167.0 7.4 %fusion.149 = f32[80,128,128]{1,0,2:T(8,128)} fusion(f32[128,80,128]{0,1,2:T(8,128)} %copy.341), kind=kOutput, calls=%fused_computation.207 | convolution fusion | flops 629203200 | bytes 10485760 | tf_op jit(solution)/shard_map/kbf,jb->kjf/dot_general | solution.py:32
  174.4 6.5 %copy.338 = f32[128,80,128]{0,1,2:T(8,128)} copy(f32[128,80,128]{2,0,1:T(8,128)} %get-tuple-element.31) | data formatting | bytes 10485760 | tf_op jit(solution)/shard_map/add | solution.py:104
  180.9 5.3 fusion.151
  186.2 5.5 %subtract_bitcast_fusion = f32[128,80,128]{0,1,2:T(8,128)S(1)} fusion(f32[80,128,128]{1,0,2:T(8,128)} %fusion.149, f32[128,80,128]{0,1,2:T(8,128)S(1)} %copy-done.6), kind=kOutput, calls=%fused_computation.83 | convolution fusion | flops 630513920 | bytes 15728640 | tf_op jit(solution)/shard_map/kbf,jb->kjf/dot_general | solution.py:32
  191.9 6.8 %broadcast_select_fusion.1 = (f32[128,80,128]{0,1,2:T(8,128)}, f32[128,80,128]{0,1,2:T(8,128)}, f32[128,80,128]{0,1,2:T(8,128)S(1)}) fusion(s32[128]{0:T(128)S(1)} %get-tuple-element.46, s32[128]{0:T(128)S(1)} %get-tuple-element.45, s32[128,80]{0,1:T(8,128)S(1)} %subtract_minimum_fusion.1, f32[128,80,128]{0,1,2:T(8,128)S(1)} %subtract_bitcast_fusion, ...), kind=kOutput, calls=%fused_computation.115 | convolution fusion | flops 637067520 | bytes 31499264 | tf_op jit(solution)/shard_map/kbf,jb->kjf/dot_general | solution.py:32
  204.7 6.7 %copy.309 = f32[128,80,128]{2,1,0:T(8,128)} copy(f32[128,80,128]{0,1,2:T(8,128)} %get-tuple-element.40) | data formatting | bytes 10485760 | tf_op jit(solution)/shard_map/scatter | solution.py:127
  211.4 7.5 %fusion.146 = f32[80,128,128]{2,0,1:T(8,128)} fusion(f32[128,80,128]{2,1,0:T(8,128)} %copy.309), kind=kOutput, calls=%fused_computation.204 | convolution fusion | flops 629203200 | bytes 10485760 | tf_op jit(solution)/shard_map/kjf,jb->kbf/dot_general | solution.py:32
  218.9 5.1 fusion.153
  224.0 6.3 %copy.301 = f32[128,80,128]{2,1,0:T(8,128)} copy(f32[128,80,128]{0,1,2:T(8,128)} %get-tuple-element.39) | data formatting | bytes 10485760 | tf_op jit(solution)/shard_map/scatter | solution.py:126
  230.3 5.3 fusion.144
  238.5 12.1 %fusion.25 = (f32[128,80,128]{2,0,1:T(8,128)S(1)}, f32[128,80,128]{2,0,1:T(8,128)S(1)}) fusion(f32[128,80]{0,1:T(8,128)S(1)} %get-tuple-element.48, f32[128,80]{0,1:T(8,128)S(1)} %get-tuple-element.49, f32[80,128,128]{2,0,1:T(8,128)S(1)} %bitcast.211, f32[80,128,128]{2,0,1:T(8,128)S(1)} %fusion.155, f32[80,128,128]{2,0,1:T(8,128)S(1)} %fusion.144, ...), kind=kLoop, calls=%fused_computation.58 | loop fusion | flops 10485760 | bytes 31539200 | tf_op jit(solution)/shard_map/sub | solution.py:130
  254.7 3.8 multiply_convert_fusion.1
  261.7 6.6 %all-to-all-start.4 = ((bf16[128,80,128]{2,1,0:T(8,128)(2,1)}), bf16[128,80,128]{2,1,0:T(8,128)(2,1)}, u32[]{:S(2)}, u32[]{:S(2)}) async-start(bf16[128,80,128]{2,1,0:T(8,128)(2,1)} %copy.319), calls=%async_computation.4 | async-start | bytes 5242880 | tf_op jit(solution)/shard_map/all_to_all | solution.py:181
  268.3 5.5 %fusion.116 = f32[128,80,128]{2,0,1:T(8,128)S(1)} fusion(f32[128,80,128]{2,0,1:T(8,128)} %copy-done.3), kind=kOutput, calls=%fused_computation.163 | convolution fusion | flops 1006862336 | bytes 10485760 | tf_op jit(solution)/shard_map/kbf,kp->pbf/dot_general | solution.py:32
  273.8 3.5 multiply_convert_fusion.2
  280.7 23.0 %all-to-all-done.4 = bf16[128,80,128]{2,1,0:T(8,128)(2,1)} async-done(((bf16[128,80,128]{2,1,0:T(8,128)(2,1)}), bf16[128,80,128]{2,1,0:T(8,128)(2,1)}, u32[]{:S(2)}, u32[]{:S(2)}) %all-to-all-start.4) | async-done | bytes 2621472 | tf_op jit(solution)/shard_map/all_to_all | solution.py:181
  303.7 4.8 all-to-all-start.3
  308.5 5.8 %fusion.44 = f32[80,128,128]{2,1,0:T(8,128)} fusion(bf16[128,80,128]{2,1,0:T(8,128)(2,1)} %all-to-all-done.4), kind=kOutput, calls=%fused_computation.94 | convolution fusion | flops 1006862336 | bytes 7864320 | tf_op jit(solution)/shard_map/rkj,jn->rkn/dot_general | solution.py:32
  314.4 5.9 %fusion.46 = f32[80,128,128]{2,1,0:T(8,128)} fusion(bf16[128,80,128]{2,1,0:T(8,128)(2,1)} %all-to-all-done.4), kind=kOutput, calls=%fused_computation.96 | convolution fusion | flops 1006862336 | bytes 7864320 | tf_op jit(solution)/shard_map/rkj,jn->rkn/dot_general | solution.py:32
  320.2 24.1 %all-to-all-done.3 = bf16[128,80,128]{2,1,0:T(8,128)(2,1)S(1)} async-done(((bf16[128,80,128]{2,1,0:T(8,128)(2,1)}), bf16[128,80,128]{2,1,0:T(8,128)(2,1)S(1)}, u32[]{:S(2)}, u32[]{:S(2)}) %all-to-all-start.3) | async-done | bytes 2621472 | tf_op jit(solution)/shard_map/all_to_all | solution.py:180
  344.3 4.3 fusion.73
  359.4 4.7 copy.326
  364.0 3.6 all-to-all-start.5
  367.7 31.7 %all-to-all-done.5 = bf16[80,8,2048]{2,0,1:T(8,128)(2,1)S(1)} async-done(((bf16[80,8,2048]{2,0,1:T(8,128)(2,1)}), bf16[80,8,2048]{2,0,1:T(8,128)(2,1)S(1)}, u32[]{:S(2)}, u32[]{:S(2)}) %all-to-all-start.5) | async-done | bytes 2621472 | tf_op jit(solution)/shard_map/all_to_all | solution.py:184
  404.5 4.8 collective-permute-done.1
  416.6 3.8 collective-permute-done.3
  420.4 4.6 concatenate.49
  427.2 7.4 %fusion.17 = (f32[1,648,2056]{2,1,0:T(8,128)}, f32[1,648,2056]{2,1,0:T(8,128)}) fusion(pred[2056]{0:T(1024)(128)(4,1)S(1)} %fusion.228, pred[648]{0:T(1024)(128)(4,1)S(1)} %fusion.231, f32[650,2058]{1,0:T(8,128)S(1)} %convert_element_type.170), kind=kLoop, calls=%fused_computation.44 | loop fusion | flops 11990592 | bytes 31977616 | tf_op jit(solution)/shard_map/stack | solution.py:200
  434.7 48.1 %fusion.2 = f32[2,640,2056]{2,1,0:T(8,128)} fusion(f32[1,648,2056]{2,1,0:T(8,128)} %get-tuple-element.34, f32[1,648,2056]{2,1,0:T(8,128)} %get-tuple-element.33), kind=kLoop, calls=%fused_computation.18 | loop fusion | flops 44738560 | bytes 21185024 | tf_op jit(solution)/shard_map/add | solution.py:144
  482.7 51.4 %slice_add_fusion = f32[2,640,2048]{2,1,0:T(8,128)} fusion(f32[2,640,2056]{2,1,0:T(8,128)} %fusion.2), kind=kLoop, calls=%fused_computation.33 | loop fusion | flops 20971520 | bytes 104857600 | tf_op jit(solution)/shard_map/add | solution.py:144
  534.1 8.2 %fusion.23 = f32[640,2048]{1,0:T(8,128)} fusion(f32[2,640,2048]{2,1,0:T(8,128)} %slice_add_fusion), kind=kLoop, calls=%fused_computation.53 | loop fusion | flops 6553600 | bytes 15728640 | tf_op jit(solution)/shard_map/div | solution.py:205
  (110 shorter events, 65.8 us)
Async XLA Ops:
  4.2 38.6 %all-to-all-start = ((bf16[8,80,2048]{2,1,0:T(8,128)(2,1)}), bf16[8,80,2048]{2,1,0:T(8,128)(2,1)S(1)}, u32[]{:S(2)}, u32[]{:S(2)}) async-start(bf16[8,80,2048]{2,1,0:T(8,128)(2,1)} %bitcast.217), calls=%async_computation | async-start | bytes 5242880 | tf_op jit(solution)/shard_map/all_to_all | solution.py:161
  51.4 4.6 copy-start
  53.2 2.8 copy-start.1
  63.0 14.7 %slice-start = ((s8[5242880]{0:T(1024)(128)(4,1)}), s8[1048576]{0:T(1024)(128)(4,1)S(1)}, s32[]{:S(2)}) async-start(s8[5242880]{0:T(1024)(128)(4,1)} %bitcast.204), calls=%async_computation.6 | async-start | bytes 2097152
  63.0 44.2 %all-to-all-start.2 = ((bf16[80,128,128]{2,0,1:T(8,128)(2,1)}), bf16[80,128,128]{2,0,1:T(8,128)(2,1)}, u32[]{:S(2)}, u32[]{:S(2)}) async-start(bf16[80,128,128]{2,0,1:T(8,128)(2,1)} %copy.289), calls=%async_computation.2 | async-start | bytes 5242880 | tf_op jit(solution)/shard_map/all_to_all | solution.py:174
  71.8 5.9 %slice-start.1 = ((s8[5242880]{0:T(1024)(128)(4,1)}), s8[4194304]{0:T(1024)(128)(4,1)S(1)}, s32[]{:S(2)}) async-start(s8[5242880]{0:T(1024)(128)(4,1)} %bitcast.204), calls=%async_computation.7 | async-start | bytes 8388608
  83.0 29.3 %copy-start.12 = (s32[2,8193]{1,0:T(2,128)S(1)}, s32[2,8193]{1,0:T(2,128)}, u32[]{:S(2)}) copy-start(s32[2,8193]{1,0:T(2,128)} %param.9) | copy-start | bytes 196636
  107.2 40.9 %all-to-all-start.1 = ((bf16[80,128,128]{2,0,1:T(8,128)(2,1)}), bf16[80,128,128]{2,0,1:T(8,128)(2,1)S(1)}, u32[]{:S(2)}, u32[]{:S(2)}) async-start(bf16[80,128,128]{2,0,1:T(8,128)(2,1)} %copy.284), calls=%async_computation.1 | async-start | bytes 5242880 | tf_op jit(solution)/shard_map/all_to_all | solution.py:173
  148.1 4.6 copy-start.8
  180.9 5.4 copy-start.6
  180.9 11.0 %slice-start.4 = ((s8[5242880]{0:T(1024)(128)(4,1)}), s8[4194304]{0:T(1024)(128)(4,1)S(1)}, s32[]{:S(2)}) async-start(s8[5242880]{0:T(1024)(128)(4,1)} %bitcast.208), calls=%async_computation.10 | async-start | bytes 8388608
  186.2 5.6 %slice-start.5 = ((s8[5242880]{0:T(1024)(128)(4,1)}), s8[1048576]{0:T(1024)(128)(4,1)S(1)}, s32[]{:S(2)}) async-start(s8[5242880]{0:T(1024)(128)(4,1)} %bitcast.208), calls=%async_computation.11 | async-start | bytes 2097152
  191.7 7.1 %copy-start.7 = (f32[128,80,128]{0,1,2:T(8,128)}, f32[128,80,128]{0,1,2:T(8,128)S(1)}, u32[]{:S(2)}) copy-start(f32[128,80,128]{0,1,2:T(8,128)S(1)} %subtract_bitcast_fusion) | copy-start | bytes 15728644
  198.6 2.3 copy-start.11
  211.4 7.5 %copy-start.4 = (f32[128,80,128]{2,1,0:T(8,128)S(1)}, f32[128,80,128]{2,1,0:T(8,128)}, u32[]{:S(2)}) copy-start(f32[128,80,128]{2,1,0:T(8,128)} %copy.309) | copy-start | bytes 15728644
  230.3 5.3 copy-start.5
  230.3 8.1 %slice-start.6 = ((s8[5242880]{0:T(1024)(128)(4,1)}), s8[4194304]{0:T(1024)(128)(4,1)S(1)}, s32[]{:S(2)}) async-start(s8[5242880]{0:T(1024)(128)(4,1)} %bitcast.210), calls=%async_computation.12 | async-start | bytes 8388608
  230.3 8.1 %slice-start.8 = ((s8[5242880]{0:T(1024)(128)(4,1)}), s8[4194304]{0:T(1024)(128)(4,1)S(1)}, s32[]{:S(2)}) async-start(s8[5242880]{0:T(1024)(128)(4,1)} %bitcast.212), calls=%async_computation.14 | async-start | bytes 8388608
  235.6 2.9 slice-start.7
  235.6 2.9 slice-start.9
  250.6 3.0 copy-start.2
  250.6 4.1 copy-start.3
  261.7 12.1 %slice-start.2 = ((s8[5242880]{0:T(1024)(128)(4,1)}), s8[1048576]{0:T(1024)(128)(4,1)S(1)}, s32[]{:S(2)}) async-start(s8[5242880]{0:T(1024)(128)(4,1)} %bitcast.206), calls=%async_computation.8 | async-start | bytes 2097152
  261.7 41.9 %all-to-all-start.4 = ((bf16[128,80,128]{2,1,0:T(8,128)(2,1)}), bf16[128,80,128]{2,1,0:T(8,128)(2,1)}, u32[]{:S(2)}, u32[]{:S(2)}) async-start(bf16[128,80,128]{2,1,0:T(8,128)(2,1)} %copy.319), calls=%async_computation.4 | async-start | bytes 5242880 | tf_op jit(solution)/shard_map/all_to_all | solution.py:181
  268.3 5.5 %slice-start.3 = ((s8[5242880]{0:T(1024)(128)(4,1)}), s8[4194304]{0:T(1024)(128)(4,1)S(1)}, s32[]{:S(2)}) async-start(s8[5242880]{0:T(1024)(128)(4,1)} %bitcast.206), calls=%async_computation.9 | async-start | bytes 8388608
  303.7 40.7 %all-to-all-start.3 = ((bf16[128,80,128]{2,1,0:T(8,128)(2,1)}), bf16[128,80,128]{2,1,0:T(8,128)(2,1)S(1)}, u32[]{:S(2)}, u32[]{:S(2)}) async-start(bf16[128,80,128]{2,1,0:T(8,128)(2,1)} %copy.316), calls=%async_computation.3 | async-start | bytes 5242880 | tf_op jit(solution)/shard_map/all_to_all | solution.py:180
  344.3 4.3 copy-start.9
  364.0 35.3 %all-to-all-start.5 = ((bf16[80,8,2048]{2,0,1:T(8,128)(2,1)}), bf16[80,8,2048]{2,0,1:T(8,128)(2,1)S(1)}, u32[]{:S(2)}, u32[]{:S(2)}) async-start(bf16[80,8,2048]{2,0,1:T(8,128)(2,1)} %copy.326), calls=%async_computation.5 | async-start | bytes 5242880 | tf_op jit(solution)/shard_map/all_to_all | solution.py:184
  399.3 5.1 copy-start.10
  399.4 5.1 collective-permute-start
  402.5 6.7 %collective-permute-start.1 = (bf16[5,2048]{1,0:T(8,128)(2,1)S(1)}, bf16[5,2048]{1,0:T(8,128)(2,1)S(1)}, u32[]{:S(2)}, u32[]{:S(2)}) collective-permute-start(bf16[5,2048]{1,0:T(8,128)(2,1)S(1)} %get-tuple-element.38), channel_id=1, source_target_pairs={{8,0},{16,8},{24,16},{32,24},{40,32},{48,40},{56,48},{64,56},{72,6... | collective-permute-start | bytes 61448 | tf_op jit(solution)/shard_map/ppermute | solution.py:24
  411.8 4.8 collective-permute-start.2
  414.3 6.1 %collective-permute-start.3 = (bf16[650,5]{1,0:T(8,128)(2,1)S(1)}, bf16[650,5]{1,0:T(8,128)(2,1)S(1)}, u32[]{:S(2)}, u32[]{:S(2)}) collective-permute-start(bf16[650,5]{1,0:T(8,128)(2,1)S(1)} %get-tuple-element.35), channel_id=1, source_target_pairs={{1,0},{2,1},{3,2},{4,3},{5,4},{6,5},{7,6},{9,8},{10,9},{11,10},{12... | collective-permute-start | bytes 19508 | tf_op jit(solution)/shard_map/ppermute | solution.py:24
where the time goes:
time: 553 us; the launch traced here: 543 us
  waiting for transfers between devices  155 us (28%)
  other arithmetic  142 us (26%)
  matrix products  130 us (24%)
  local copies, waits for them, and re-layouts  69.4 us (13%)
  starting transfers between devices  44.7 us (8%)
    dot_general x28, matrix products, contract(): jnp.einsum(pattern, left_arg, right_arg, precision=lax.Precision.HIGH, pr...  130 us
    add x2, other arithmetic, box_sum(): running + lax.slice_in_dim(values, offset, offset + length, axis=dim_index)  99.4 us
    all_to_all x1, waiting for transfers between devices, per_device(): lax.all_to_all(filtered_rows, 'tm', split_axis=1, concat_axis=0, tiled=True)  31.7 us
    all_to_all x1, waiting for transfers between devices, per_device(): lax.all_to_all(tiles, 'tm', split_axis=0, concat_axis=1, tiled=True)  31 us
    all_to_all x1, waiting for transfers between devices, per_device(): lax.all_to_all(filt_re, ('chan', 'tm'), split_axis=0, concat_axis=1, tile...  24.1 us
    all_to_all x1, waiting for transfers between devices, per_device(): lax.all_to_all(filt_im, ('chan', 'tm'), split_axis=0, concat_axis=1, tile...  23 us
    all_to_all x1, waiting for transfers between devices, per_device(): lax.all_to_all(spec_im, ('chan', 'tm'), split_axis=1, concat_axis=0, tile...  20.9 us
    all_to_all x1, waiting for transfers between devices, per_device(): lax.all_to_all(spec_re, ('chan', 'tm'), split_axis=1, concat_axis=0, tile...  14.6 us
  transfers between devices with their start and end apart: 10, of which 9 were waited for; matrix products, arithmetic and copies ran while one was open for 11% of the time, Pallas kernels for 0%

commit v1 on v0

v1 whole, which is shorter than its diff:
```python
import functools
import math

import jax
import jax.numpy as jnp
import ml_dtypes
import numpy as np
from jax import lax
from jax.experimental import pallas as pl
from jax.experimental.pallas import tpu as pltpu
from jax.sharding import PartitionSpec as P

NC = 10240
NT = 16384
TF = 128
R = 4
ROWS = 80
HALF = 64
WIDE = 2176
BF = jnp.bfloat16
F32 = jnp.float32
VMEM = pl.BlockSpec(memory_space=pltpu.VMEM)
SMEM = pl.BlockSpec(memory_space=pltpu.SMEM)

WAVES = [0] + [8 * n for n in range(1, 8)] + [4 + 8 * n for n in range(8)]
WAVES += [q + 8 * n for q in (1, 2, 3) for n in range(16)]


def two_parts(matrix):
    high = matrix.astype(ml_dtypes.bfloat16)
    low = (matrix - high.astype(np.float64)).astype(ml_dtypes.bfloat16)
    return high, low


def turn(numbers, length):
    angle = (numbers % length) * (2.0 * np.pi / length)
    return np.cos(angle), np.sin(angle)


def time_tables():
    n = np.arange(128)[:, None]
    j = np.concatenate([np.arange(64), 127 - np.arange(64)])[None, :]
    cos, sin = turn(n * j, 128)

    def halves(re, im):
        return np.concatenate([re[:, :64], im[:, :64], re[:, 64:], im[:, 64:]], axis=1)

    forward = np.concatenate([halves(cos, -sin), halves(sin, cos)], axis=0)
    backward = np.concatenate(
        [halves(cos, -sin).T, halves(sin, cos).T], axis=1
    ) / NT
    jj = np.arange(64)[None, :]
    c0, s0 = turn(n * 128 * jj, NT)
    c1, s1 = turn(n * (64 + 128 * jj), NT)
    zero = np.zeros((128, 128))
    even = np.concatenate([c0, -s0], axis=1)
    even[:, 64] = 1.0 - 2.0 * (np.arange(128) % 2)
    odd = np.concatenate([c1, -s1], axis=1)
    first = np.concatenate(
        [np.concatenate([even, zero], axis=1), np.concatenate([zero, odd], axis=1)], axis=0
    )
    weight = np.full(256, 2.0)
    weight[0] = 1.0
    weight[64] = 1.0
    last = (first * weight[None, :]).T / NT
    k = np.array(WAVES)[:, None]
    tw_cos, tw_sin = turn(k * np.arange(128)[None, :], NT)
    return forward, backward, first, last, tw_cos, tw_sin


def chan_tables():
    cos, sin = turn(np.arange(128)[:, None] * np.arange(128)[None, :], 128)
    forward = np.block([[cos, -sin], [sin, cos]])
    backward = np.block([[cos, sin], [-sin, cos]])
    tw_cos, tw_sin = turn(np.arange(ROWS)[:, None] * np.arange(128)[None, :], NC)
    return forward, backward, tw_cos, tw_sin


def plus(a, b):
    if a is None:
        return b
    if b is None:
        return a
    return a + b


def minus(a, b):
    if b is None:
        return a
    if a is None:
        return -b
    return a - b


def times(value, number):
    if value is None or number == 0.0:
        return None
    if number == 1.0:
        return value
    if number == -1.0:
        return -value
    return value * number


def cadd(x, y):
    return plus(x[0], y[0]), plus(x[1], y[1])


def csub(x, y):
    return minus(x[0], y[0]), minus(x[1], y[1])


def spun(x, step, length, sign):
    step = step % length
    if 4 * step % length == 0:
        quarter = 4 * step // length
        c = (1.0, 0.0, -1.0, 0.0)[quarter]
        s = (0.0, 1.0, 0.0, -1.0)[quarter]
    else:
        c = math.cos(2.0 * math.pi * step / length)
        s = math.sin(2.0 * math.pi * step / length)
    s = sign * s
    re, im = x
    if 8 * step % length == 0 and 4 * step % length != 0 and re is not None and im is not None:
        a = abs(c)
        u = re if c > 0 else -re
        v = im if c > 0 else -im
        if c * s > 0:
            return (u - v) * a, (v + u) * a
        return (u + v) * a, (v - u) * a
    return minus(times(re, c), times(im, s)), plus(times(im, c), times(re, s))


def fft_list(xs, sign):
    count = len(xs)
    if count == 1:
        return xs
    even = fft_list(xs[0::2], sign)
    odd = fft_list(xs[1::2], sign)
    head, tail = [], []
    for k in range(count // 2):
        t = spun(odd[k], k, count, sign)
        head.append(cadd(even[k], t))
        tail.append(csub(even[k], t))
    return head + tail


def rfft_list(xs):
    count = len(xs)
    if count == 2:
        return [(xs[0] + xs[1], None), (xs[0] - xs[1], None)]
    even = rfft_list(xs[0::2])
    odd = rfft_list(xs[1::2])
    out = [None] * (count // 2 + 1)
    for k in range(count // 4 + 1):
        t = spun(odd[k], k, count, -1.0)
        out[k] = cadd(even[k], t)
        if k < count // 4:
            re, im = csub(even[k], t)
            out[count // 2 - k] = (re, minus(None, im) if im is not None else None)
    return out


def irfft_list(ys):
    half = len(ys) - 1
    count = 2 * half
    if count == 2:
        return [ys[0][0] + ys[1][0], ys[0][0] - ys[1][0]]
    evens, odds = [], []
    for k in range(count // 4 + 1):
        mirror = (ys[half - k][0], minus(None, ys[half - k][1]) if ys[half - k][1] is not None else None)
        if 2 * k == half:
            evens.append((ys[k][0] * 2.0, None))
            re, _ = spun(ys[k], k, count, 1.0)
            odds.append((re * 2.0, None))
        else:
            both = cadd(ys[k], mirror)
            gap = spun(csub(ys[k], mirror), k, count, 1.0)
            if k == 0:
                both = (both[0], None)
                gap = (gap[0], None)
            evens.append(both)
            odds.append(gap)
    even = irfft_list(evens)
    odd = irfft_list(odds)
    out = []
    for e, o in zip(even, odd):
        out += [e, o]
    return out


def fft5(xs, sign):
    c1, c2 = math.cos(2 * math.pi / 5), math.cos(4 * math.pi / 5)
    s1, s2 = math.sin(2 * math.pi / 5), math.sin(4 * math.pi / 5)
    out = [[None, None] for _ in range(5)]
    pairs = []
    for part in range(2):
        x = [v[part] for v in xs]
        t1, t2, t3, t4 = x[1] + x[4], x[2] + x[3], x[1] - x[4], x[2] - x[3]
        out[0][part] = x[0] + t1 + t2
        pairs.append(
            (
                x[0] + c1 * t1 + c2 * t2,
                x[0] + c2 * t1 + c1 * t2,
                s1 * t3 + s2 * t4,
                s2 * t3 - s1 * t4,
            )
        )
    (ra, rb, rc, rd), (ia, ib, ic, idd) = pairs
    if sign > 0:
        out[1] = [ra - ic, ia + rc]
        out[4] = [ra + ic, ia - rc]
        out[2] = [rb - idd, ib + rd]
        out[3] = [rb + idd, ib - rd]
    else:
        out[1] = [ra + ic, ia - rc]
        out[4] = [ra - ic, ia + rc]
        out[2] = [rb + idd, ib - rd]
        out[3] = [rb - idd, ib + rd]
    return [tuple(v) for v in out]


def dot(a, b):
    return lax.dot_general(a, b, (((1,), (0,)), ((), ())), preferred_element_type=F32)


def parted(value):
    high = value.astype(BF)
    low = (value - high.astype(F32)).astype(BF)
    return high, low


def forward_kernel(x_ref, ok_ref, tc_ref, ts_ref, w_ref, w0_ref, out_ref, stage, hi_ref, lo_ref):
    def tile_body(tile, carry):
        rows = pl.ds(pl.multiple_of(tile * 16, 16), 16)
        good = ok_ref[rows, :]
        for a in range(16):
            xs = [x_ref[s, rows, a * 128 : (a + 1) * 128].astype(F32) * good for s in range(8)]
            ys = rfft_list(xs)
            stage[a, 0] = ys[0][0]
            for q in (1, 2, 3):
                re, im = spun(ys[q], a * q, 128, -1.0)
                stage[a, 2 * q] = re
                stage[a, 2 * q + 1] = im
            stage[a, 1] = ys[4][0]

        def put(slot, re, im):
            base = pl.ds(pl.multiple_of(slot * ROWS + tile * 16, 16), 16)
            for part, value in enumerate((re, im)):
                high, low = parted(value)
                hi_ref[base, part * 128 : (part + 1) * 128] = high
                lo_ref[base, part * 128 : (part + 1) * 128] = low

        def twist(slot, value):
            re, im = value
            c = tc_ref[slot : slot + 1, :]
            s = ts_ref[slot : slot + 1, :]
            put(slot, re * c + im * s, im * c - re * s)

        ys = rfft_list([stage[a, 0] for a in range(16)])
        put(0, ys[0][0], ys[8][0])
        for n in range(1, 8):
            twist(n, ys[n])
        ys = fft_list([spun((stage[a, 1], None), a, 32, -1.0) for a in range(16)], -1.0)
        for n in range(8):
            twist(8 + n, ys[n])
        for q in (1, 2, 3):
            ys = fft_list([(stage[a, 2 * q], stage[a, 2 * q + 1]) for a in range(16)], -1.0)
            for n in range(16):
                twist(16 * q + n, ys[n])
        return carry

    lax.fori_loop(0, 5, tile_body, 0)

    def mixed(rows, w):
        high, low = hi_ref[rows, :], lo_ref[rows, :]
        return dot(high, w[0]) + dot(low, w[0]) + dot(high, w[1])

    first = mixed(pl.ds(0, ROWS), w0_ref).astype(BF)
    out_ref[0] = first[:, :128]
    out_ref[1] = first[:, 128:]

    def wave_body(step, carry):
        res = mixed(pl.ds(pl.multiple_of(ROWS + step * 7 * ROWS, 16), 7 * ROWS), w_ref).astype(BF)
        for n in range(7):
            out_ref[2 + 14 * step + 2 * n] = res[n * ROWS : (n + 1) * ROWS, :128]
            out_ref[3 + 14 * step + 2 * n] = res[n * ROWS : (n + 1) * ROWS, 128:]
        return carry

    lax.fori_loop(0, 9, wave_body, 0)


def backward_kernel(in_ref, tc_ref, ts_ref, w_ref, w0_ref, out_ref, stage, mid_ref):
    def joined(slot):
        return jnp.concatenate([in_ref[2 * slot], in_ref[2 * slot + 1]], axis=1)

    first = joined(0)
    mid_ref[pl.ds(0, ROWS), :] = dot(first, w0_ref[0]) + dot(first, w0_ref[1])

    def wave_body(step, carry):
        data = jnp.concatenate([joined(1 + step * 7 + n) for n in range(7)], axis=0)
        mid_ref[pl.ds(pl.multiple_of(ROWS + step * 7 * ROWS, 16), 7 * ROWS), :] = dot(
            data, w_ref[0]
        ) + dot(data, w_ref[1])
        return carry

    lax.fori_loop(0, 9, wave_body, 0)
    lane = lax.broadcasted_iota(jnp.int32, (16, 128), 1)

    def tile_body(tile, carry):
        def get(slot):
            base = pl.ds(pl.multiple_of(slot * ROWS + tile * 16, 16), 16)
            return mid_ref[base, :128], mid_ref[base, 128:]

        def twisted(slot):
            re, im = get(slot)
            c = tc_ref[slot : slot + 1, :]
            s = ts_ref[slot : slot + 1, :]
            return re * c - im * s, im * c + re * s

        mean, top = get(0)
        ys = irfft_list([(mean, None)] + [twisted(n) for n in range(1, 8)] + [(top, None)])
        for a in range(16):
            stage[a, 0] = ys[a]
        ys = fft_list([twisted(8 + n) for n in range(8)] + [(None, None)] * 8, 1.0)
        for a in range(16):
            stage[a, 1] = 2.0 * spun(ys[a], a, 32, 1.0)[0]
        for q in (1, 2, 3):
            ys = fft_list([twisted(16 * q + n) for n in range(16)], 1.0)
            for a in range(16):
                re, im = spun(ys[a], a * q, 128, 1.0)
                stage[a, 2 * q] = re
                stage[a, 2 * q + 1] = im
        rows = pl.ds(pl.multiple_of(tile * 16, 16), 16)

        def series(a):
            parts = [(stage[a, 0], None)]
            parts += [(stage[a, 2 * q], stage[a, 2 * q + 1]) for q in (1, 2, 3)]
            return [y.astype(BF) for y in irfft_list(parts + [(stage[a, 1], None)])]

        ends = {}
        for a in range(16):
            ys = series(a)
            for s in range(8):
                out_ref[s, rows, a * 128 : (a + 1) * 128] = ys[s]
            if a in (0, 15):
                ends[a] = ys
        blank = jnp.zeros((16, 128), BF)
        for s in range(8):
            after = ends[0][s + 1] if s < 7 else blank
            before = ends[15][s - 1] if s > 0 else blank
            out_ref[s, rows, 2048:] = jnp.where(
                lane < 64, after.astype(F32), before.astype(F32)
            ).astype(BF)
        return carry

    lax.fori_loop(0, 5, tile_body, 0)


STEP = 8


def channel_kernel(
    in_ref, low_ref, high_ref, first_ref, tc_ref, ts_ref, w_ref, v_ref, out_ref, flat, u_re, u_im, a_re, a_im
):
    def load_body(p, carry):
        flat[pl.ds(pl.multiple_of(p * ROWS, 8), ROWS), :] = in_ref[p].astype(F32)
        return carry

    lax.fori_loop(0, 128, load_body, 0, unroll=4)
    packed = first_ref[...]
    blank = jnp.zeros((8, 128), F32)

    def in_body(step, carry):
        parts = []
        for n in range(STEP):
            turned = flat[pl.ds(step * STEP + n, 128, stride=ROWS), :].T
            re, im = turned[:64], turned[64:]
            im = jnp.concatenate([im[:8] * (1.0 - packed), im[8:], im[:8] * packed], axis=0)
            re = jnp.concatenate([re, blank], axis=0)
            parts.append(jnp.concatenate([re, im], axis=1).astype(BF))
        data = jnp.concatenate(parts, axis=0)
        res = dot(data, w_ref[0]) + dot(data, w_ref[1])
        for n in range(STEP):
            r = step * STEP + n
            re = res[n * 72 : (n + 1) * 72, :128]
            im = res[n * 72 : (n + 1) * 72, 128:]
            c = tc_ref[pl.ds(r, 1), :]
            s = ts_ref[pl.ds(r, 1), :]
            u_re[r] = re * c + im * s
            u_im[r] = im * c - re * s
        return carry

    lax.fori_loop(0, ROWS // STEP, in_body, 0)
    lane = lax.broadcasted_iota(jnp.int32, (8, 128), 1)

    def fan_body(tile, carry):
        rows = pl.ds(pl.multiple_of(tile * 8, 8), 8)
        low = low_ref[rows, :]
        high = high_ref[rows, :]
        for n2 in range(5):
            spots = [(5 * n1 + 16 * n2) % ROWS for n1 in range(16)]
            ys = fft_list([(u_re[r, rows, :], u_im[r, rows, :]) for r in spots], -1.0)
            for k1 in range(16):
                a_re[n2 * 16 + k1] = ys[k1][0]
                a_im[n2 * 16 + k1] = ys[k1][1]
        for k1 in range(16):
            ys = fft5([(a_re[n2 * 16 + k1], a_im[n2 * 16 + k1]) for n2 in range(5)], -1.0)
            kept = []
            for k2 in range(5):
                outer = next(k for k in range(ROWS) if k % 16 == k1 and k % 5 == k2)
                if outer < ROWS // 2:
                    fold = lane + outer * 128
                else:
                    fold = (NC - outer * 128) - lane
                keep = (fold >= low) & (fold <= high)
                kept.append(tuple(jnp.where(keep, v, 0.0) for v in ys[k2]))
            ys = fft5(kept, 1.0)
            for n2 in range(5):
                a_re[n2 * 16 + k1] = ys[n2][0]
                a_im[n2 * 16 + k1] = ys[n2][1]
        for n2 in range(5):
            spots = [(5 * n1 + 16 * n2) % ROWS for n1 in range(16)]
            ys = fft_list([(a_re[n2 * 16 + k1], a_im[n2 * 16 + k1]) for k1 in range(16)], 1.0)
            for n1 in range(16):
                u_re[spots[n1], rows, :] = ys[n1][0]
                u_im[spots[n1], rows, :] = ys[n1][1]
        return carry

    lax.fori_loop(0, 9, fan_body, 0)

    def out_body(step, carry):
        highs, lows = [], []
        for n in range(STEP):
            r = step * STEP + n
            re, im = u_re[r], u_im[r]
            re = jnp.concatenate([re[:8] + re[64:], re[8:64]], axis=0)
            im = jnp.concatenate([im[:8] + im[64:], im[8:64]], axis=0)
            c = tc_ref[pl.ds(r, 1), :]
            s = ts_ref[pl.ds(r, 1), :]
            high, low = parted(jnp.concatenate([re * c - im * s, im * c + re * s], axis=1))
            highs.append(high)
            lows.append(low)
        high = jnp.concatenate(highs, axis=0)
        low = jnp.concatenate(lows, axis=0)
        res = (dot(high, v_ref[0]) + dot(low, v_ref[0]) + dot(high, v_ref[1])) * (1.0 / NC)
        for n in range(STEP):
            block = res[n * 64 : (n + 1) * 64]
            both = jnp.concatenate([block[:, :128], block[:, 128:]], axis=0)
            flat[pl.ds(step * STEP + n, 128, stride=ROWS), :] = both.T
        return carry

    lax.fori_loop(0, ROWS // STEP, out_body, 0)

    def store_body(p, carry):
        out_ref[p] = flat[pl.ds(pl.multiple_of(p * ROWS, 8), ROWS), :].astype(BF)
        return carry

    lax.fori_loop(0, 128, store_body, 0, unroll=4)


def tensor_kernel(place_ref, x_ref, above_ref, below_ref, out_ref, wide, prod):
    chan, part = place_ref[0], place_ref[1]
    lane = lax.broadcasted_iota(jnp.int32, (16, 128), 1)

    def spread(start, block):
        block = block.astype(F32)
        side = block[:, 2048:]
        rows = pl.ds(start, 16)
        wide[rows, 128:2176] = block[:, :2048]
        wide[rows, :128] = side
        wide[rows, 2176:] = side

    spread(0, above_ref[...])
    spread(656, below_ref[...])

    def spread_body(step, carry):
        start = pl.multiple_of(step * 16, 16)
        spread(pl.multiple_of(start + 16, 16), x_ref[pl.ds(start, 16), :])
        return carry

    lax.fori_loop(0, 40, spread_body, 0)
    time = lax.broadcasted_iota(jnp.int32, (8, 2304), 1) - 128
    time_in = ((time >= 0) | (part > 0)) & ((time < 2048) | (part < 7))
    sub = lax.broadcasted_iota(jnp.int32, (8, 2304), 0)

    def down(a, b, count):
        return jnp.where(
            sub < 8 - count, pltpu.roll(a, 8 - count, 0), pltpu.roll(b, 8 - count, 0)
        )

    def prod_body(step, carry):
        start = pl.multiple_of(step * 8 + 8, 8)
        here = wide[pl.ds(start, 8), :]
        prev = wide[pl.ds(pl.multiple_of(start - 8, 8), 8), :]
        nxt = wide[pl.ds(pl.multiple_of(start + 8, 8), 8), :]
        grad_chan = (down(here, nxt, 1) - down(prev, here, 7)) * 0.5
        grad_time = (pltpu.roll(here, 2303, 1) - pltpu.roll(here, 1, 1)) * 0.5
        row = sub + (start - 16)
        inside = time_in & ((row >= 0) | (chan > 0)) & ((row < 640) | (chan < 15))
        grad_time_in = jnp.where(inside, grad_time, 0.0)
        prod[0, pl.ds(start, 8), :] = grad_chan * grad_time_in
        prod[1, pl.ds(start, 8), :] = grad_time * grad_time_in
        return carry

    lax.fori_loop(0, 82, prod_body, 0)

    def sum_body(step, carry):
        start = pl.multiple_of(step * 8 + 8, 8)
        sums = []
        for n in range(2):
            a = prod[n, pl.ds(start, 8), :]
            b = prod[n, pl.ds(pl.multiple_of(start + 8, 8), 8), :]
            c = prod[n, pl.ds(pl.multiple_of(start + 16, 8), 8), :]
            p = down(a, b, 4)
            q = down(b, c, 4)
            acc = p + q
            for d in range(1, 8):
                acc = acc + down(p, q, d)
            s2 = acc + pltpu.roll(acc, 2303, 1)
            s4 = s2 + pltpu.roll(s2, 2302, 1)
            s8 = s4 + pltpu.roll(s4, 2300, 1)
            s9 = s8 + pltpu.roll(acc, 2296, 1)
            sums.append(pltpu.roll(s9, 4, 1)[:, 128:2176])
        cross = sums[0] * (1.0 / 81.0)
        along = sums[1] * (1.0 / 81.0)
        out_ref[pl.ds(pl.multiple_of(step * 8, 8), 8), :] = -cross / (along + 1e-05)
        return carry

    lax.fori_loop(0, 80, sum_body, 0)


def call(kernel, out, scratch, flops, *args, smem=0):
    nbytes = sum(a.size * a.dtype.itemsize for a in args) + out.size * out.dtype.itemsize
    return pl.pallas_call(
        kernel,
        out_shape=out,
        in_specs=[SMEM] * smem + [VMEM] * (len(args) - smem),
        out_specs=VMEM,
        scratch_shapes=scratch,
        compiler_params=pltpu.CompilerParams(vmem_limit_bytes=48 * 2**20),
        cost_estimate=pl.CostEstimate(flops=flops, bytes_accessed=nbytes, transcendentals=0),
    )(*args)


def pair(matrix):
    return jnp.asarray(np.stack(two_parts(matrix)))


def single(table):
    return jnp.asarray(table.astype(np.float32))


def forward(series, good):
    fwd, _, first, _, tc, ts = time_tables()
    scratch = [
        pltpu.VMEM((16, 8, 16, 128), F32),
        pltpu.VMEM((64 * ROWS, 256), BF),
        pltpu.VMEM((64 * ROWS, 256), BF),
    ]
    out = jax.ShapeDtypeStruct((128, ROWS, 128), BF)
    return call(
        forward_kernel, out, scratch, 4 * 10**9, series, good, single(tc), single(ts), pair(fwd), pair(first)
    )


def backward(spectra):
    _, bwd, _, last, tc, ts = time_tables()
    scratch = [pltpu.VMEM((16, 8, 16, 128), F32), pltpu.VMEM((64 * ROWS, 256), F32)]
    out = jax.ShapeDtypeStruct((8, ROWS, WIDE), BF)
    return call(
        backward_kernel, out, scratch, 4 * 10**9, spectra, single(tc), single(ts), pair(bwd), pair(last)
    )


def channels(pencil, low, high, packed):
    fwd, bwd, tc, ts = chan_tables()
    scratch = [
        pltpu.VMEM((128 * ROWS, 128), F32),
        pltpu.VMEM((ROWS, 72, 128), F32),
        pltpu.VMEM((ROWS, 72, 128), F32),
        pltpu.VMEM((ROWS, 8, 128), F32),
        pltpu.VMEM((ROWS, 8, 128), F32),
    ]
    out = jax.ShapeDtypeStruct((128, ROWS, 128), BF)
    return call(
        channel_kernel,
        out,
        scratch,
        8 * 10**9,
        pencil,
        low,
        high,
        packed,
        single(tc),
        single(ts),
        pair(fwd),
        pair(bwd),
    )


def tensor(place, cells, above, below):
    scratch = [pltpu.VMEM((672, 2304), F32), pltpu.VMEM((2, 672, 2304), F32)]
    out = jax.ShapeDtypeStruct((640, 2048), F32)
    return call(tensor_kernel, out, scratch, 10**9, place, cells, above, below, smem=1)


def window_bounds(fan_bounds, block):
    column = []
    for slot, k in enumerate(WAVES):
        column += [0, 64] if slot == 0 else [k, 128 - k]
    pick = jnp.asarray(np.array(column, np.int32))[block]
    table = fan_bounds[:, : NT // 2].reshape(2, 64, 128)
    mine = lax.dynamic_slice(table, (0, 0, pick), (2, 64, 1))
    top = jnp.broadcast_to(fan_bounds[:, NT // 2].reshape(2, 1, 1), (2, 8, 1))
    both = jnp.broadcast_to(jnp.concatenate([mine, top], axis=1), (2, 72, 128))
    return both[0], both[1]


def per_device(record, channel_ok, fan_bounds):
    chan, part = lax.axis_index("chan"), lax.axis_index("tm")
    block = chan * 8 + part
    series = lax.all_to_all(record.reshape(8, ROWS, 2048), "tm", 0, 0, tiled=True)
    good = lax.dynamic_slice(channel_ok, (part * ROWS,), (ROWS,)).astype(F32)
    good = jnp.broadcast_to(good[:, None], (ROWS, 128))
    spectra = forward(series, good)
    low, high = window_bounds(fan_bounds, block)
    corner = lax.broadcasted_iota(jnp.int32, (8, 128), 0) == 0
    packed = (corner & (block == 0)).astype(F32)
    pencil = lax.all_to_all(spectra, ("chan", "tm"), 0, 0, tiled=True)
    passed = channels(pencil, low, high, packed)
    back = lax.all_to_all(passed, ("chan", "tm"), 0, 0, tiled=True)
    rows = backward(back)
    cells = lax.all_to_all(rows, "tm", 0, 0, tiled=True).reshape(640, WIDE)
    above = lax.ppermute(cells[624:], "chan", [(i, i + 1) for i in range(15)])
    below = lax.ppermute(cells[:16], "chan", [(i + 1, i) for i in range(15)])
    place = jnp.stack([chan, part]).astype(jnp.int32)
    return tensor(place, cells, above, below)


def solution(mesh):
    in_specs = (P("chan", "tm"), P("chan"), P())
    out_specs = P("chan", "tm")
    return jax.shard_map(
        per_device, mesh=mesh, in_specs=in_specs, out_specs=out_specs, check_vma=False
    )
```

time: 553 us -> 251 us (0.45); the launches traced: 543 us -> 249 us
  other arithmetic: 142 us -> 0.92 us
  matrix products: 130 us -> 0 us
  waiting for transfers between devices: 155 us -> 65.2 us
  Pallas kernels: 0 us -> 80.4 us
  blocking collectives: 0 us -> 74.8 us
  local copies, waits for them, and re-layouts: 69.4 us -> 2.8 us
  starting transfers between devices: 44.7 us -> 23.5 us
    dot_general x28 -> x0, matrix products: 130 us -> none  [contract(): jnp.einsum(pattern, left_arg, right_arg, precision=lax.Precision.HIGH, pr...]
    add x2 -> x0, other arithmetic: 99.4 us -> none  [box_sum(): running + lax.slice_in_dim(values, offset, offset + length, axis=dim_index)]
    all_to_all x6 -> x2, waiting for transfers between devices: 145 us -> 63.9 us  [the longest x1 32.9 us: per_device(): pencil = lax.all_to_all(spectra, ('chan', 'tm'), 0, 0, tiled=True)]
    pallas_call x0 -> x4, Pallas kernels: none -> 80.4 us  [call(): pl.pallas_call(kernel, out_shape=out, in_specs=[SMEM] * smem + [VMEM] * (...]
    all_to_all x0 -> x2, blocking collectives: none -> 74.8 us  [the longest x1 40.2 us: per_device(): back = lax.all_to_all(passed, ('chan', 'tm'), 0, 0, tiled=True)]
    convert_element_type x6 -> x0, local copies, waits for them, and re-layouts: 20.9 us -> none  [the longest x2 7.74 us: time_inverse(): return (result / NT).reshape(row_count, NT).astype(jnp.bfloat16)]
    all_to_all x6 -> x2, starting transfers between devices: 35.8 us -> 15.4 us  [the longest x1 8.41 us: per_device(): pencil = lax.all_to_all(spectra, ('chan', 'tm'), 0, 0, tiled=True)]
    scatter x2 -> x0, local copies, waits for them, and re-layouts: 13 us -> none  [the longest x1 6.71 us: channel_filter(): wave_im.at[:, :, 0]]
  transfers between devices with their start and end apart: 10 -> 4, of which waited for: 9 -> 3; matrix products, arithmetic and copies ran while one was open for 11% -> 1% of each run, Pallas kernels for 0% -> 0%
where the time goes in v1:
time: 251 us; the launch traced here: 249 us
  Pallas kernels  80.4 us (32%)
  blocking collectives  74.8 us (30%)
  waiting for transfers between devices  65.2 us (26%)
  starting transfers between devices  23.5 us (9%)
  local copies, waits for them, and re-layouts  2.8 us (1%)
    pallas_call x4, Pallas kernels, call(): pl.pallas_call(kernel, out_shape=out, in_specs=[SMEM] * smem + [VMEM] * (...  80.4 us
    all_to_all x1, blocking collectives, per_device(): back = lax.all_to_all(passed, ('chan', 'tm'), 0, 0, tiled=True)  40.2 us
    all_to_all x1, blocking collectives, per_device(): cells = lax.all_to_all(rows, 'tm', 0, 0, tiled=True).reshape(640, WIDE)  34.7 us
    all_to_all x1, waiting for transfers between devices, per_device(): pencil = lax.all_to_all(spectra, ('chan', 'tm'), 0, 0, tiled=True)  32.9 us
    all_to_all x1, waiting for transfers between devices, per_device(): lax.all_to_all(record.reshape(8, ROWS, 2048), 'tm', 0, 0, tiled=True)  31 us
    all_to_all x1, starting transfers between devices, per_device(): pencil = lax.all_to_all(spectra, ('chan', 'tm'), 0, 0, tiled=True)  8.41 us
    all_to_all x1, starting transfers between devices, per_device(): lax.all_to_all(record.reshape(8, ROWS, 2048), 'tm', 0, 0, tiled=True)  7.02 us
  transfers between devices with their start and end apart: 4, of which 3 were waited for; matrix products, arithmetic and copies ran while one was open for 1% of the time, Pallas kernels for 0%

profile of v1, /device:TPU:1, one launch (start us, length us, event | category | flops | bytes accessed | tf_op | source)
XLA Modules:
  0.0 249.5 jit_solution(16155746499668855610)
XLA Ops:
  0.0 0.0 copy-start.5
  0.0 0.0 copy-start.6
  0.0 0.0 copy-start.9
  0.0 0.0 copy-start.10
  0.0 7.0 %all-to-all-start = ((bf16[8,80,2048]{2,1,0:T(8,128)(2,1)}), bf16[8,80,2048]{2,1,0:T(8,128)(2,1)S(1)}, u32[]{:S(2)}, u32[]{:S(2)}) async-start(bf16[8,80,2048]{2,1,0:T(8,128)(2,1)} %bitcast.16), calls=%async_computation | async-start | bytes 5242880 | tf_op jit(solution)/shard_map/all_to_all | solution.py:623
  7.0 0.8 dynamic-slice_convert_fusion
  7.8 31.0 %all-to-all-done.x_ref = bf16[8,80,2048]{2,1,0:T(8,128)(2,1)S(1)} async-done(((bf16[8,80,2048]{2,1,0:T(8,128)(2,1)}), bf16[8,80,2048]{2,1,0:T(8,128)(2,1)S(1)}, u32[]{:S(2)}, u32[]{:S(2)}) %all-to-all-start) | async-done | bytes 2621472 | tf_op jit(solution)/shard_map/all_to_all | solution.py:623
  38.8 0.1 broadcast_in_dim.24.ok_ref
  38.9 0.0 copy-done.5
  38.9 0.0 copy-done.6
  38.9 0.0 copy-done.9
  38.9 0.0 copy-done.10
  38.9 8.1 %shard_map.154 = bf16[128,80,128]{2,1,0:T(8,128)(2,1)S(1)} custom-call(bf16[8,80,2048]{2,1,0:T(8,128)(2,1)S(1)} %all-to-all-done.x_ref, f32[80,128]{1,0:T(8,128)S(1)} %broadcast_in_dim.24.ok_ref, f32[64,128]{1,0:T(8,128)S(1)} %copy-done.10, f32[64,128]{1,0:T(8,128)S(1)} %copy-done.9, bf16[2,256,256]{2,1,0:T(8,128)(2,1)S(1)} %copy-done.6, ...), custom_call_target="tpu_custom_call" | custom-call | flops 4000000000 | bytes 5873664 | tf_op jit(solution)/shard_map/pallas_call | solution.py:535
  47.0 0.0 copy-start
  47.0 1.5 copy-done
  48.5 0.0 copy-start.7
  48.5 0.0 copy-start.8
  48.5 8.4 %all-to-all-start.1 = ((bf16[128,80,128]{2,1,0:T(8,128)(2,1)}), bf16[128,80,128]{2,1,0:T(8,128)(2,1)S(1)}, u32[]{:S(2)}, u32[]{:S(2)}) async-start(bf16[128,80,128]{2,1,0:T(8,128)(2,1)} %copy-done), calls=%async_computation.1 | async-start | bytes 5242880 | tf_op jit(solution)/shard_map/all_to_all | solution.py:630
  57.0 0.0 copy-done.12
  57.0 0.6 dynamic_slice.10
  58.7 0.0 copy-done.11
  59.3 0.1 constant_dynamic-slice_fusion
  59.4 0.1 copy.18
  59.5 0.1 slice_reduce_fusion
  59.6 0.1 broadcast_in_dim.26
  59.6 0.1 fusion.2
  59.7 32.9 %all-to-all-done.1.in_ref = bf16[128,80,128]{2,1,0:T(8,128)(2,1)S(1)} async-done(((bf16[128,80,128]{2,1,0:T(8,128)(2,1)}), bf16[128,80,128]{2,1,0:T(8,128)(2,1)S(1)}, u32[]{:S(2)}, u32[]{:S(2)}) %all-to-all-start.1) | async-done | bytes 2621472 | tf_op jit(solution)/shard_map/all_to_all | solution.py:630
  92.6 0.1 iota.7.first_ref
  92.7 0.1 broadcast_in_dim.30.high_ref
  92.8 0.1 broadcast_in_dim.28.low_ref
  92.9 0.0 copy-done.3
  92.9 0.0 copy-done.4
  92.9 0.0 copy-done.7
  92.9 0.0 copy-done.8
  92.9 15.4 %shard_map.155 = bf16[128,80,128]{2,1,0:T(8,128)(2,1)S(1)} custom-call(bf16[128,80,128]{2,1,0:T(8,128)(2,1)S(1)} %all-to-all-done.1.in_ref, s32[72,128]{1,0:T(8,128)S(1)} %broadcast_in_dim.28.low_ref, s32[72,128]{1,0:T(8,128)S(1)} %broadcast_in_dim.30.high_ref, f32[8,128]{1,0:T(8,128)S(1)} %iota.7.first_ref, f32[80,128]{1,0:T(8,128)S(1)} %copy-done.8, ...), custom_call_target="tpu_custom_call" | custom-call | flops 8000000000 | bytes 5926912 | tf_op jit(solution)/shard_map/pallas_call | solution.py:535
  108.3 0.0 copy-start.1
  108.3 0.0 copy-start.2
  108.3 40.2 %all_to_all.20.in_ref = bf16[128,80,128]{2,1,0:T(8,128)(2,1)S(1)} all-to-all(bf16[128,80,128]{2,1,0:T(8,128)(2,1)S(1)} %shard_map.155), channel_id=1, replica_groups=mesh['chan'=16,'tm'=8] {'chan','tm'}, dimensions={0} | all-to-all | bytes 5242880 | tf_op jit(solution)/shard_map/all_to_all | solution.py:632
  148.5 0.0 copy-done.1
  148.5 0.0 copy-done.2
  148.5 6.5 %shard_map.156 = bf16[8,80,2176]{2,1,0:T(8,128)(2,1)S(1)} custom-call(bf16[128,80,128]{2,1,0:T(8,128)(2,1)S(1)} %all_to_all.20.in_ref, f32[64,128]{1,0:T(8,128)S(1)} %copy-done.10, f32[64,128]{1,0:T(8,128)S(1)} %copy-done.9, bf16[2,256,256]{2,1,0:T(8,128)(2,1)S(1)} %copy-done.2, bf16[2,256,256]{2,1,0:T(8,128)(2,1)S(1)} %copy-done.1), custom_call_target="tpu_custom_call" | custom-call | flops 4000000000 | bytes 5996544 | tf_op jit(solution)/shard_map/pallas_call | solution.py:535
  155.0 34.7 %all_to_all.21 = bf16[8,80,2176]{2,1,0:T(8,128)(2,1)S(1)} all-to-all(bf16[8,80,2176]{2,1,0:T(8,128)(2,1)S(1)} %shard_map.156), channel_id=1, replica_groups=mesh['chan'=16,'tm'=8] {'tm'}, dimensions={0} | all-to-all | bytes 5570560 | tf_op jit(solution)/shard_map/all_to_all | solution.py:634
  189.7 5.0 %collective-permute-start.1 = (bf16[16,2176]{1,0:T(8,128)(2,1)S(1)}, bf16[16,2176]{1,0:T(8,128)(2,1)S(1)}, u32[]{:S(2)}, u32[]{:S(2)}) collective-permute-start(bf16[16,2176]{1,0:T(8,128)(2,1)S(1)} %get-tuple-element.5), channel_id=1, source_target_pairs={{8,0},{16,8},{24,16},{32,24},{40,32},{48,40},{56,48},{64,56},{72,6... | collective-permute-start | bytes 208904 | tf_op jit(solution)/shard_map/ppermute | solution.py:636
  194.6 3.1 %collective-permute-start = (bf16[16,2176]{1,0:T(8,128)(2,1)S(1)}, bf16[16,2176]{1,0:T(8,128)(2,1)S(1)}, u32[]{:S(2)}, u32[]{:S(2)}) collective-permute-start(bf16[16,2176]{1,0:T(8,128)(2,1)S(1)} %get-tuple-element.6), channel_id=1, source_target_pairs={{0,8},{8,16},{16,24},{24,32},{32,40},{40,48},{48,56},{56,64},{64,7... | collective-permute-start | bytes 208904 | tf_op jit(solution)/shard_map/ppermute | solution.py:635
  197.7 0.1 pad_add_fusion.1.place_ref
  197.8 0.0 collective-permute-done.1.below_ref
  197.8 1.3 collective-permute-done.above_ref
  199.1 50.4 %shard_map.157 = f32[640,2048]{1,0:T(8,128)} custom-call(s32[2]{0:T(128)S(1)} %pad_add_fusion.1.place_ref, bf16[640,2176]{1,0:T(8,128)(2,1)S(1)} %bitcast.15, bf16[16,2176]{1,0:T(8,128)(2,1)S(1)} %collective-permute-done.above_ref, bf16[16,2176]{1,0:T(8,128)(2,1)S(1)} %collective-permute-done.1.below_ref), custom_call_target="tpu_custom_call" | custom-call | flops 1000000000 | bytes 8167432 | tf_op jit(solution)/shard_map/pallas_call | solution.py:535
  (8 shorter events, 0.0 us)
Async XLA Ops:
  0.0 38.9 %copy-start.5 = (bf16[2,256,256]{2,1,0:T(8,128)(2,1)S(1)}, bf16[2,256,256]{2,1,0:T(8,128)(2,1)}, u32[]{:S(2)}) copy-start(bf16[2,256,256]{2,1,0:T(8,128)(2,1)} %constant.45.clone.w0_ref) | copy-start | bytes 786436
  0.0 38.9 %copy-start.6 = (bf16[2,256,256]{2,1,0:T(8,128)(2,1)S(1)}, bf16[2,256,256]{2,1,0:T(8,128)(2,1)}, u32[]{:S(2)}) copy-start(bf16[2,256,256]{2,1,0:T(8,128)(2,1)} %constant.44.clone.w_ref) | copy-start | bytes 786436
  0.0 38.9 %copy-start.9 = (f32[64,128]{1,0:T(8,128)S(1)}, f32[64,128]{1,0:T(8,128)}, u32[]{:S(2)}) copy-start(f32[64,128]{1,0:T(8,128)} %constant.43.clone.ts_ref) | copy-start | bytes 98308
  0.0 38.9 %copy-start.10 = (f32[64,128]{1,0:T(8,128)S(1)}, f32[64,128]{1,0:T(8,128)}, u32[]{:S(2)}) copy-start(f32[64,128]{1,0:T(8,128)} %constant.42.clone.tc_ref) | copy-start | bytes 98308
  0.0 38.8 %all-to-all-start = ((bf16[8,80,2048]{2,1,0:T(8,128)(2,1)}), bf16[8,80,2048]{2,1,0:T(8,128)(2,1)S(1)}, u32[]{:S(2)}, u32[]{:S(2)}) async-start(bf16[8,80,2048]{2,1,0:T(8,128)(2,1)} %bitcast.16), calls=%async_computation | async-start | bytes 5242880 | tf_op jit(solution)/shard_map/all_to_all | solution.py:623
  47.0 1.5 copy-start
  48.5 8.5 %copy-start.12 = (s32[128]{0:T(128)S(1)}, s32[128]{0:T(128)}, u32[]{:S(2)}) copy-start(s32[128]{0:T(128)} %constant.46.clone) | copy-start | bytes 1540
  48.5 10.2 %copy-start.11 = (s32[2,8193]{1,0:T(2,128)S(1)}, s32[2,8193]{1,0:T(2,128)}, u32[]{:S(2)}) copy-start(s32[2,8193]{1,0:T(2,128)} %param.18) | copy-start | bytes 196636
  48.5 44.4 %copy-start.3 = (bf16[2,256,256]{2,1,0:T(8,128)(2,1)S(1)}, bf16[2,256,256]{2,1,0:T(8,128)(2,1)}, u32[]{:S(2)}) copy-start(bf16[2,256,256]{2,1,0:T(8,128)(2,1)} %constant.50.clone.v_ref) | copy-start | bytes 786436
  48.5 44.4 %copy-start.4 = (bf16[2,256,256]{2,1,0:T(8,128)(2,1)S(1)}, bf16[2,256,256]{2,1,0:T(8,128)(2,1)}, u32[]{:S(2)}) copy-start(bf16[2,256,256]{2,1,0:T(8,128)(2,1)} %constant.49.clone.w_ref) | copy-start | bytes 786436
  48.5 44.4 %copy-start.7 = (f32[80,128]{1,0:T(8,128)S(1)}, f32[80,128]{1,0:T(8,128)}, u32[]{:S(2)}) copy-start(f32[80,128]{1,0:T(8,128)} %constant.48.clone.ts_ref) | copy-start | bytes 122884
  48.5 44.4 %copy-start.8 = (f32[80,128]{1,0:T(8,128)S(1)}, f32[80,128]{1,0:T(8,128)}, u32[]{:S(2)}) copy-start(f32[80,128]{1,0:T(8,128)} %constant.47.clone.tc_ref) | copy-start | bytes 122884
  48.5 44.1 %all-to-all-start.1 = ((bf16[128,80,128]{2,1,0:T(8,128)(2,1)}), bf16[128,80,128]{2,1,0:T(8,128)(2,1)S(1)}, u32[]{:S(2)}, u32[]{:S(2)}) async-start(bf16[128,80,128]{2,1,0:T(8,128)(2,1)} %copy-done), calls=%async_computation.1 | async-start | bytes 5242880 | tf_op jit(solution)/shard_map/all_to_all | solution.py:630
  108.3 40.2 %copy-start.1 = (bf16[2,256,256]{2,1,0:T(8,128)(2,1)S(1)}, bf16[2,256,256]{2,1,0:T(8,128)(2,1)}, u32[]{:S(2)}) copy-start(bf16[2,256,256]{2,1,0:T(8,128)(2,1)} %constant.52.clone.w0_ref) | copy-start | bytes 786436
  108.3 40.2 %copy-start.2 = (bf16[2,256,256]{2,1,0:T(8,128)(2,1)S(1)}, bf16[2,256,256]{2,1,0:T(8,128)(2,1)}, u32[]{:S(2)}) copy-start(bf16[2,256,256]{2,1,0:T(8,128)(2,1)} %constant.51.clone.w_ref) | copy-start | bytes 786436
  189.7 8.1 %collective-permute-start.1 = (bf16[16,2176]{1,0:T(8,128)(2,1)S(1)}, bf16[16,2176]{1,0:T(8,128)(2,1)S(1)}, u32[]{:S(2)}, u32[]{:S(2)}) collective-permute-start(bf16[16,2176]{1,0:T(8,128)(2,1)S(1)} %get-tuple-element.5), channel_id=1, source_target_pairs={{8,0},{16,8},{24,16},{32,24},{40,32},{48,40},{56,48},{64,56},{72,6... | collective-permute-start | bytes 208904 | tf_op jit(solution)/shard_map/ppermute | solution.py:636
  194.6 4.4 %collective-permute-start = (bf16[16,2176]{1,0:T(8,128)(2,1)S(1)}, bf16[16,2176]{1,0:T(8,128)(2,1)S(1)}, u32[]{:S(2)}, u32[]{:S(2)}) collective-permute-start(bf16[16,2176]{1,0:T(8,128)(2,1)S(1)} %get-tuple-element.6), channel_id=1, source_target_pairs={{0,8},{8,16},{16,24},{24,32},{32,40},{40,48},{48,56},{56,64},{64,7... | collective-permute-start | bytes 208904 | tf_op jit(solution)/shard_map/ppermute | solution.py:635

commit v2 on v1

--- a/solution.py
+++ b/solution.py
@@ -230,7 +230,12 @@
     return high, low
 
 
-def forward_kernel(x_ref, ok_ref, tc_ref, ts_ref, w_ref, w0_ref, out_ref, stage, hi_ref, lo_ref):
+def forward_kernel(spot_ref, *refs):
+    blocks = refs[:8]
+    ok_ref, tc_ref, ts_ref, w_ref, w0_ref, out_ref, x_ref, stage, hi_ref, lo_ref = refs[8:]
+    for n in range(8):
+        x_ref[spot_ref[n]] = blocks[n][...]
+
     def tile_body(tile, carry):
         rows = pl.ds(pl.multiple_of(tile * 16, 16), 16)
         good = ok_ref[rows, :]
@@ -290,7 +295,10 @@
     lax.fori_loop(0, 9, wave_body, 0)
 
 
-def backward_kernel(in_ref, tc_ref, ts_ref, w_ref, w0_ref, out_ref, stage, mid_ref):
+def backward_kernel(spot_ref, in_ref, tc_ref, ts_ref, w_ref, w0_ref, *refs):
+    outs = refs[:8]
+    out_ref, stage, mid_ref = refs[8:]
+
     def joined(slot):
         return jnp.concatenate([in_ref[2 * slot], in_ref[2 * slot + 1]], axis=1)
 
@@ -355,6 +363,8 @@
         return carry
 
     lax.fori_loop(0, 5, tile_body, 0)
+    for n in range(8):
+        outs[n][...] = out_ref[spot_ref[n]]
 
 
 STEP = 8
@@ -459,84 +469,210 @@
     lax.fori_loop(0, 128, store_body, 0, unroll=4)
 
 
-def tensor_kernel(place_ref, x_ref, above_ref, below_ref, out_ref, wide, prod):
-    chan, part = place_ref[0], place_ref[1]
-    lane = lax.broadcasted_iota(jnp.int32, (16, 128), 1)
-
-    def spread(start, block):
-        block = block.astype(F32)
-        side = block[:, 2048:]
-        rows = pl.ds(start, 16)
-        wide[rows, 128:2176] = block[:, :2048]
-        wide[rows, :128] = side
-        wide[rows, 2176:] = side
-
-    spread(0, above_ref[...])
-    spread(656, below_ref[...])
-
-    def spread_body(step, carry):
-        start = pl.multiple_of(step * 16, 16)
-        spread(pl.multiple_of(start + 16, 16), x_ref[pl.ds(start, 16), :])
-        return carry
-
-    lax.fori_loop(0, 40, spread_body, 0)
-    time = lax.broadcasted_iota(jnp.int32, (8, 2304), 1) - 128
-    time_in = ((time >= 0) | (part > 0)) & ((time < 2048) | (part < 7))
-    sub = lax.broadcasted_iota(jnp.int32, (8, 2304), 0)
-
-    def down(a, b, count):
-        return jnp.where(
-            sub < 8 - count, pltpu.roll(a, 8 - count, 0), pltpu.roll(b, 8 - count, 0)
-        )
-
-    def prod_body(step, carry):
-        start = pl.multiple_of(step * 8 + 8, 8)
-        here = wide[pl.ds(start, 8), :]
-        prev = wide[pl.ds(pl.multiple_of(start - 8, 8), 8), :]
-        nxt = wide[pl.ds(pl.multiple_of(start + 8, 8), 8), :]
-        grad_chan = (down(here, nxt, 1) - down(prev, here, 7)) * 0.5
-        grad_time = (pltpu.roll(here, 2303, 1) - pltpu.roll(here, 1, 1)) * 0.5
-        row = sub + (start - 16)
-        inside = time_in & ((row >= 0) | (chan > 0)) & ((row < 640) | (chan < 15))
-        grad_time_in = jnp.where(inside, grad_time, 0.0)
-        prod[0, pl.ds(start, 8), :] = grad_chan * grad_time_in
-        prod[1, pl.ds(start, 8), :] = grad_time * grad_time_in
-        return carry
-
-    lax.fori_loop(0, 82, prod_body, 0)
-
-    def sum_body(step, carry):
-        start = pl.multiple_of(step * 8 + 8, 8)
+TILES = 18
+
+
+def spread(wide, start, block, count):
+    block = block.astype(F32)
+    rows = pl.ds(start, count)
+    for t in range(16):
+        wide[t + 1, rows, :] = block[:, t * 128 : (t + 1) * 128]
+    wide[0, rows, :] = block[:, 2048:]
+    wide[17, rows, :] = block[:, 2048:]
+
+
+def ahead(parts, count, lane):
+    turned = [pltpu.roll(v, (-count) % 128, 1) for v in parts]
+    out = []
+    for t in range(len(parts)):
+        if count > 0:
+            other = turned[t + 1] if t + 1 < len(parts) else turned[t]
+            out.append(jnp.where(lane < 128 - count, turned[t], other))
+        else:
+            other = turned[t - 1] if t > 0 else turned[t]
+            out.append(jnp.where(lane < -count, other, turned[t]))
+    return out
+
+
+def products(wide, start, first_keep, last_keep, row_keep, lane):
+    low = [wide[t, pl.ds(start, 8), :] for t in range(TILES)]
+    here = [wide[t, pl.ds(start + 1, 8), :] for t in range(TILES)]
+    high = [wide[t, pl.ds(start + 2, 8), :] for t in range(TILES)]
+    right = ahead(here, 1, lane)
+    left = ahead(here, -1, lane)
+    both = []
+    for t in range(TILES):
+        grad_time = right[t] - left[t]
+        masked = grad_time
+        if t == 0:
+            masked = jnp.where(first_keep, grad_time, 0.0)
+        if t == TILES - 1:
+            masked = jnp.where(last_keep, grad_time, 0.0)
+        if row_keep is not None:
+            masked = jnp.where(row_keep, masked, 0.0)
+        both.append(((high[t] - low[t]) * masked, grad_time * masked))
+    return both
+
+
+def quotient(cross, along, lane):
+    sums = []
+    for parts in (cross, along):
+        near, far = ahead(parts, 1, lane), ahead(parts, -1, lane)
+        three = [v + n + f for v, n, f in zip(parts, near, far)]
+        near, far = ahead(three, 3, lane), ahead(three, -3, lane)
+        sums.append([v + n + f for v, n, f in zip(three, near, far)][1:17])
+    scale = 1.0 / 324.0
+    out = []
+    for c, a in zip(*sums):
+        out.append((c * -scale) / (a * scale + 1e-05))
+    return jnp.concatenate(out, axis=1)
+
+
+def slide_tables():
+    row = np.arange(256)[:, None]
+    col = np.arange(128)[None, :]
+    change = (row == col + 125) * 1.0 - (row == col + 123) * 1.0
+    shift = (row == col + 124) * 1.0
+    nine = ((row >= col) & (row <= col + 8)) * 1.0
+    return np.concatenate([change, shift], axis=1), nine
+
+
+SLABS = 17
+BAND = 128
+
+
+def tensor_kernel(spot_ref, *refs):
+    blocks = refs[:8]
+    lanes_ref, nine_ref, out_ref, slope, level, prod, trio, hi_ref, lo_ref = refs[8:]
+    lane = lax.broadcasted_iota(jnp.int32, (8, 128), 1)
+    step = pl.program_id(0)
+    part = spot_ref[9]
+
+    @pl.when(step == 0)
+    def _():
+        def lanes(t, cells):
+            res = dot(cells, lanes_ref[...])
+            for n in range(8):
+                rows = pl.ds(pl.multiple_of(spot_ref[n] * ROWS + 16, 16), ROWS)
+                slope[t, rows, :] = res[n * ROWS : (n + 1) * ROWS, :128]
+                level[t, rows, :] = res[n * ROWS : (n + 1) * ROWS, 128:]
+
+        def row_body(t, carry):
+            cols = pl.ds(pl.multiple_of(t * 128 - 128, 128), 256)
+            lanes(t, jnp.concatenate([b[:, cols] for b in blocks], axis=0))
+            return carry
+
+        lax.fori_loop(1, 16, row_body, 0)
+        first = [jnp.concatenate([b[:, 2048:], b[:, :128]], axis=1) for b in blocks]
+        lanes(0, jnp.concatenate(first, axis=0))
+        last = [b[:, 1920:] for b in blocks]
+        lanes(16, jnp.concatenate(last, axis=0))
+
+    top = step * BAND
+
+    def prod_body(k, carry):
+        start = pl.multiple_of(k * 8, 8)
+        base = pl.multiple_of(top + k * 8, 8)
+        for t in range(SLABS):
+            grad_time = slope[t, pl.ds(base + 12, 8), :]
+            masked = grad_time
+            if t == 0:
+                masked = jnp.where((lane >= 4) | (part > 0), grad_time, 0.0)
+            if t == SLABS - 1:
+                masked = jnp.where((lane < 4) | (part < 7), grad_time, 0.0)
+            grad_chan = level[t, pl.ds(base + 13, 8), :] - level[t, pl.ds(base + 11, 8), :]
+            prod[0, t, pl.ds(start, 8), :] = grad_chan * masked
+            prod[1, t, pl.ds(start, 8), :] = grad_time * masked
+        return carry
+
+    lax.fori_loop(0, BAND // 8 + 2, prod_body, 0)
+
+    def trio_body(k, carry):
+        start = pl.multiple_of(k * 8, 8)
+        for n in range(2):
+            for t in range(SLABS):
+                trio[n, t, pl.ds(start, 8), :] = (
+                    prod[n, t, pl.ds(start, 8), :]
+                    + prod[n, t, pl.ds(start + 1, 8), :]
+                    + prod[n, t, pl.ds(start + 2, 8), :]
+                )
+        return carry
+
+    lax.fori_loop(0, BAND // 8 + 1, trio_body, 0)
+
+    def split_body(k, carry):
+        start = pl.multiple_of(k * 16, 16)
+        for n in range(2):
+            for t in range(SLABS):
+                total = (
+                    trio[n, t, pl.ds(start, 16), :]
+                    + trio[n, t, pl.ds(start + 3, 16), :]
+                    + trio[n, t, pl.ds(start + 6, 16), :]
+                )
+                for ref, value in zip((hi_ref, lo_ref), parted(total)):
+                    if t < SLABS - 1:
+                        ref[n, t, pl.ds(start, 16), :128] = value
+                    if t > 0:
+                        ref[n, t - 1, pl.ds(start, 16), 128:] = value
+        return carry
+
+    lax.fori_loop(0, BAND // 16, split_body, 0)
+    nine = nine_ref[...]
+    scale = 1.0 / 324.0
+
+    def sum_body(g, carry):
         sums = []
         for n in range(2):
-            a = prod[n, pl.ds(start, 8), :]
-            b = prod[n, pl.ds(pl.multiple_of(start + 8, 8), 8), :]
-            c = prod[n, pl.ds(pl.multiple_of(start + 16, 8), 8), :]
-            p = down(a, b, 4)
-            q = down(b, c, 4)
-            acc = p + q
-            for d in range(1, 8):
-                acc = acc + down(p, q, d)
-            s2 = acc + pltpu.roll(acc, 2303, 1)
-            s4 = s2 + pltpu.roll(s2, 2302, 1)
-            s8 = s4 + pltpu.roll(s4, 2300, 1)
-            s9 = s8 + pltpu.roll(acc, 2296, 1)
-            sums.append(pltpu.roll(s9, 4, 1)[:, 128:2176])
-        cross = sums[0] * (1.0 / 81.0)
-        along = sums[1] * (1.0 / 81.0)
-        out_ref[pl.ds(pl.multiple_of(step * 8, 8), 8), :] = -cross / (along + 1e-05)
-        return carry
-
-    lax.fori_loop(0, 80, sum_body, 0)
+            high = hi_ref[n, pl.ds(g * 4, 4)].reshape(4 * BAND, 256)
+            low = lo_ref[n, pl.ds(g * 4, 4)].reshape(4 * BAND, 256)
+            sums.append(dot(high, nine) + dot(low, nine))
+        res = (sums[0] * -scale) / (sums[1] * scale + 1e-05)
+        for t in range(4):
+            cols = pl.ds(pl.multiple_of(g * 512 + t * 128, 128), 128)
+            out_ref[:, cols] = res[t * BAND : (t + 1) * BAND]
+        return carry
+
+    lax.fori_loop(0, 4, sum_body, 0)
+
+
+def edge_kernel(spot_ref, old_ref, rows_ref, out_ref, wide, prod):
+    lane = lax.broadcasted_iota(jnp.int32, (8, 128), 1)
+    sub = lax.broadcasted_iota(jnp.int32, (8, 128), 0)
+    step = pl.program_id(0)
+    chan, part = spot_ref[8], spot_ref[9]
+    for k in range(2):
+        spread(wide, k * 16, rows_ref[0, pl.ds(k * 16, 16), :], 16)
+    open_low = (step == 0) & (chan == 0)
+    open_high = (step == 1) & (chan == 15)
+    skip = 8 - step * 8
+    for k in range(2):
+        row = sub + (k * 8 + skip + 4)
+        row_keep = ((row >= 16) | jnp.logical_not(open_low)) & (
+            (row < 16) | jnp.logical_not(open_high)
+        )
+        both = products(wide, k * 8 + skip + 3, part > 0, part < 7, row_keep, lane)
+        for t in range(TILES):
+            prod[0, t, pl.ds(k * 8, 8), :] = both[t][0]
+            prod[1, t, pl.ds(k * 8, 8), :] = both[t][1]
+    sums = []
+    for n in range(2):
+        parts = []
+        for t in range(TILES):
+            total = prod[n, t, pl.ds(0, 8), :]
+            for d in range(1, 9):
+                total = total + prod[n, t, pl.ds(d, 8), :]
+            parts.append(total)
+        sums.append(parts)
+    out_ref[...] = quotient(sums[0], sums[1], lane)
 
 
 def call(kernel, out, scratch, flops, *args, smem=0):
-    nbytes = sum(a.size * a.dtype.itemsize for a in args) + out.size * out.dtype.itemsize
+    nbytes = sum(a.size * a.dtype.itemsize for a in args) + 3 * 2**20
     return pl.pallas_call(
         kernel,
         out_shape=out,
         in_specs=[SMEM] * smem + [VMEM] * (len(args) - smem),
-        out_specs=VMEM,
+        out_specs=[VMEM] * len(out) if isinstance(out, list) else VMEM,
         scratch_shapes=scratch,
         compiler_params=pltpu.CompilerParams(vmem_limit_bytes=48 * 2**20),
         cost_estimate=pl.CostEstimate(flops=flops, bytes_accessed=nbytes, transcendentals=0),
@@ -551,25 +687,51 @@
     return jnp.asarray(table.astype(np.float32))
 
 
-def forward(series, good):
+def forward(spot, blocks, good):
     fwd, _, first, _, tc, ts = time_tables()
     scratch = [
+        pltpu.VMEM((8, ROWS, 2048), BF),
         pltpu.VMEM((16, 8, 16, 128), F32),
         pltpu.VMEM((64 * ROWS, 256), BF),
         pltpu.VMEM((64 * ROWS, 256), BF),
     ]
     out = jax.ShapeDtypeStruct((128, ROWS, 128), BF)
     return call(
-        forward_kernel, out, scratch, 4 * 10**9, series, good, single(tc), single(ts), pair(fwd), pair(first)
+        forward_kernel,
+        out,
+        scratch,
+        4 * 10**9,
+        spot,
+        *blocks,
+        good,
+        single(tc),
+        single(ts),
+        pair(fwd),
+        pair(first),
+        smem=1,
     )
 
 
-def backward(spectra):
+def backward(spot, spectra):
     _, bwd, _, last, tc, ts = time_tables()
-    scratch = [pltpu.VMEM((16, 8, 16, 128), F32), pltpu.VMEM((64 * ROWS, 256), F32)]
-    out = jax.ShapeDtypeStruct((8, ROWS, WIDE), BF)
+    scratch = [
+        pltpu.VMEM((8, ROWS, WIDE), BF),
+        pltpu.VMEM((16, 8, 16, 128), F32),
+        pltpu.VMEM((64 * ROWS, 256), F32),
+    ]
+    out = [jax.ShapeDtypeStruct((ROWS, WIDE), BF)] * 8
     return call(
-        backward_kernel, out, scratch, 4 * 10**9, spectra, single(tc), single(ts), pair(bwd), pair(last)
+        backward_kernel,
+        out,
+        scratch,
+        4 * 10**9,
+        spot,
+        spectra,
+        single(tc),
+        single(ts),
+        pair(bwd),
+        pair(last),
+        smem=1,
     )
 
 
@@ -599,10 +761,45 @@
     )
 
 
-def tensor(place, cells, above, below):
-    scratch = [pltpu.VMEM((672, 2304), F32), pltpu.VMEM((2, 672, 2304), F32)]
-    out = jax.ShapeDtypeStruct((640, 2048), F32)
-    return call(tensor_kernel, out, scratch, 10**9, place, cells, above, below, smem=1)
+def tensor(spot, blocks):
+    lanes, nine = slide_tables()
+    scratch = [
+        pltpu.VMEM((SLABS, 672, 128), F32),
+        pltpu.VMEM((SLABS, 672, 128), F32),
+        pltpu.VMEM((2, SLABS, BAND + 16, 128), F32),
+        pltpu.VMEM((2, SLABS, BAND + 16, 128), F32),
+        pltpu.VMEM((2, 16, BAND, 256), BF),
+        pltpu.VMEM((2, 16, BAND, 256), BF),
+    ]
+    return pl.pallas_call(
+        tensor_kernel,
+        grid=(640 // BAND,),
+        out_shape=jax.ShapeDtypeStruct((640, 2048), F32),
+        in_specs=[SMEM] + [VMEM] * 10,
+        out_specs=pl.BlockSpec((BAND, 2048), lambda g: (g, 0)),
+        scratch_shapes=scratch,
+        compiler_params=pltpu.CompilerParams(vmem_limit_bytes=48 * 2**20),
+        cost_estimate=pl.CostEstimate(flops=10**9, bytes_accessed=9 * 2**20, transcendentals=0),
+    )(spot, *blocks, jnp.asarray(lanes.astype(ml_dtypes.bfloat16)), jnp.asarray(nine.astype(ml_dtypes.bfloat16)))
+
+
+def edges(spot, whole, rows):
+    scratch = [pltpu.VMEM((TILES, 32, 128), F32), pltpu.VMEM((2, TILES, 16, 128), F32)]
+    return pl.pallas_call(
+        edge_kernel,
+        grid=(2,),
+        out_shape=jax.ShapeDtypeStruct((640, 2048), F32),
+        in_specs=[
+            SMEM,
+            pl.BlockSpec(memory_space=pl.ANY),
+            pl.BlockSpec((1, 32, WIDE), lambda g: (g, 0, 0)),
+        ],
+        out_specs=pl.BlockSpec((8, 2048), lambda g: (79 * g, 0)),
+        scratch_shapes=scratch,
+        input_output_aliases={1: 0},
+        compiler_params=pltpu.CompilerParams(vmem_limit_bytes=16 * 2**20),
+        cost_estimate=pl.CostEstimate(flops=10**7, bytes_accessed=2**19, transcendentals=0),
+    )(spot, whole, rows)
 
 
 def window_bounds(fan_bounds, block):
@@ -617,25 +814,50 @@
     return both[0], both[1]
 
 
+MOVES = [(0, 0), (1, 2), (0, 2), (1, 1), (1, 3), (0, 1), (0, 3), (1, 0)]
+
+
+def moved(part, move, sign):
+    return (part // 4 + move[0]) % 2 * 4 + (part % 4 + sign * move[1]) % 4
+
+
+def traded(blocks):
+    out = [blocks[0]]
+    for move, block in list(zip(MOVES, blocks))[1:]:
+        out.append(lax.ppermute(block, "tm", [(j, moved(j, move, 1)) for j in range(8)]))
+    return out
+
+
 def per_device(record, channel_ok, fan_bounds):
     chan, part = lax.axis_index("chan"), lax.axis_index("tm")
     block = chan * 8 + part
-    series = lax.all_to_all(record.reshape(8, ROWS, 2048), "tm", 0, 0, tiled=True)
+    targets = [moved(part, move, 1) for move in MOVES]
+    sources = [moved(part, move, -1) for move in MOVES]
+    to = jnp.stack(targets).astype(jnp.int32)
+    came = jnp.stack(sources + [chan, part]).astype(jnp.int32)
+    pieces = [lax.dynamic_slice(record, (t * ROWS, 0), (ROWS, 2048)) for t in targets]
+    series = traded(pieces)
     good = lax.dynamic_slice(channel_ok, (part * ROWS,), (ROWS,)).astype(F32)
     good = jnp.broadcast_to(good[:, None], (ROWS, 128))
-    spectra = forward(series, good)
+    spectra = forward(came, series, good)
     low, high = window_bounds(fan_bounds, block)
     corner = lax.broadcasted_iota(jnp.int32, (8, 128), 0) == 0
     packed = (corner & (block == 0)).astype(F32)
     pencil = lax.all_to_all(spectra, ("chan", "tm"), 0, 0, tiled=True)
     passed = channels(pencil, low, high, packed)
     back = lax.all_to_all(passed, ("chan", "tm"), 0, 0, tiled=True)
-    rows = backward(back)
-    cells = lax.all_to_all(rows, "tm", 0, 0, tiled=True).reshape(640, WIDE)
-    above = lax.ppermute(cells[624:], "chan", [(i, i + 1) for i in range(15)])
-    below = lax.ppermute(cells[:16], "chan", [(i + 1, i) for i in range(15)])
-    place = jnp.stack([chan, part]).astype(jnp.int32)
-    return tensor(place, cells, above, below)
+    cells = traded(backward(to, back))
+    top, bottom = cells[0][:16], cells[0][64:]
+    for source, cell in list(zip(sources, cells))[1:]:
+        top = jnp.where(source == 0, cell[:16], top)
+        bottom = jnp.where(source == 7, cell[64:], bottom)
+    above = lax.ppermute(bottom, "chan", [(i, i + 1) for i in range(15)])
+    below = lax.ppermute(top, "chan", [(i + 1, i) for i in range(15)])
+    whole = tensor(came, cells)
+    rows = jnp.stack(
+        [jnp.concatenate([above, top], axis=0), jnp.concatenate([bottom, below], axis=0)]
+    )
+    return edges(came, whole, rows)
 
 
 def solution(mesh):

time: 251 us -> 237 us (0.944)
  blocking collectives: 74.8 us -> 0 us
  waiting for transfers between devices: 65.2 us -> 116 us
  starting transfers between devices: 23.5 us -> 49.2 us
  Pallas kernels: 80.4 us -> 58.5 us
  local copies, waits for them, and re-layouts: 2.8 us -> 10 us
    all_to_all x2 -> x0, blocking collectives: 74.8 us -> none  [the longest x1 40.2 us: per_device(): back = lax.all_to_all(passed, ('chan', 'tm'), 0, 0, tiled=True)]
    pallas_call x4 -> x3, Pallas kernels: 80.4 us -> 32.6 us  [call(): pl.pallas_call(kernel, out_shape=out, in_specs=[SMEM] * smem + [VMEM] * (...]
    ppermute x2 -> x16, waiting for transfers between devices: 1.27 us -> 47.6 us  [the longest x14 47.6 us: traded(): lax.ppermute(block, 'tm', [(j, moved(j, move, 1)) for j in range(8)])]
    pallas_call x0 -> x2, Pallas kernels: none -> 25.9 us  [the longest x1 23.7 us: tensor(): pl.pallas_call(tensor_kernel, grid=(640 // BAND,), out_shape=jax.ShapeDty...]
    ppermute x2 -> x16, starting transfers between devices: 8.05 us -> 31 us  [the longest x14 23 us: traded(): lax.ppermute(block, 'tm', [(j, moved(j, move, 1)) for j in range(8)])]
    all_to_all x1, starting transfers between devices: 8.41 us -> 13.3 us  [per_device(): pencil = lax.all_to_all(spectra, ('chan', 'tm'), 0, 0, tiled=True)]
    all_to_all x1, waiting for transfers between devices: 31 us -> 35.7 us  [per_device(): back = lax.all_to_all(passed, ('chan', 'tm'), 0, 0, tiled=True)]
    unnamed x29 -> x37, local copies, waits for them, and re-layouts: 1.65 us -> 5.79 us
  transfers between devices with their start and end apart: 4 -> 18, of which waited for: 3 -> 10; matrix products, arithmetic and copies ran while one was open for 1% -> 1% of each run, Pallas kernels for 0% -> 10%
where the time goes in v2:
time: 237 us
  waiting for transfers between devices  116 us (49%)
  Pallas kernels  58.5 us (25%)
  starting transfers between devices  49.2 us (21%)
  local copies, waits for them, and re-layouts  10 us (4%)
    ppermute x14, waiting for transfers between devices, traded(): lax.ppermute(block, 'tm', [(j, moved(j, move, 1)) for j in range(8)])  47.6 us
    all_to_all x1, waiting for transfers between devices, per_device(): back = lax.all_to_all(passed, ('chan', 'tm'), 0, 0, tiled=True)  35.7 us
    all_to_all x1, waiting for transfers between devices, per_device(): pencil = lax.all_to_all(spectra, ('chan', 'tm'), 0, 0, tiled=True)  32.7 us
    pallas_call x3, Pallas kernels, call(): pl.pallas_call(kernel, out_shape=out, in_specs=[SMEM] * smem + [VMEM] * (...  32.6 us
    pallas_call x1, Pallas kernels, tensor(): pl.pallas_call(tensor_kernel, grid=(640 // BAND,), out_shape=jax.ShapeDty...  23.7 us
    ppermute x14, starting transfers between devices, traded(): lax.ppermute(block, 'tm', [(j, moved(j, move, 1)) for j in range(8)])  23 us
    all_to_all x1, starting transfers between devices, per_device(): pencil = lax.all_to_all(spectra, ('chan', 'tm'), 0, 0, tiled=True)  13.3 us
    ppermute x1, starting transfers between devices, per_device(): above = lax.ppermute(bottom, 'chan', [(i, i + 1) for i in range(15)])  6.1 us
  transfers between devices with their start and end apart: 18, of which 10 were waited for; matrix products, arithmetic and copies ran while one was open for 1% of the time, Pallas kernels for 10%

profile of v2, /device:TPU:1, one launch (start us, length us, event | category | flops | bytes accessed | tf_op | source)
XLA Modules:
  0.0 236.8 jit_solution(10069261615179064074)
XLA Ops:
  0.0 2.9 %constant_dynamic-slice_fusion.1 = (bf16[80,2048]{1,0:T(8,128)(2,1)S(1)}, bf16[80,2048]{1,0:T(8,128)(2,1)S(1)}, bf16[80,2048]{1,0:T(8,128)(2,1)}, bf16[80,2048]{...) fusion(bf16[640,2048]{1,0:T(8,128)(2,1)} %param.18, ...), kind=kLoop, calls=%fused_computation.20 | loop fusion | bytes 5242912 | tf_op jit(solution)/shard_map/dynamic_slice | solution.py:838
  2.9 2.1 collective-permute-start.6
  5.1 1.6 collective-permute-start.4
  6.7 2.0 collective-permute-start.3
  8.7 0.4 collective-permute-start.2
  9.1 3.3 %collective-permute-start.1 = (bf16[80,2048]{1,0:T(8,128)(2,1)}, bf16[80,2048]{1,0:T(8,128)(2,1)S(1)}, u32[]{:S(2)}, u32[]{:S(2)}) collective-permute-start(bf16[80,2048]{1,0:T(8,128)(2,1)} %get-tuple-element.25), channel_id=1, source_target_pairs={{0,2},{1,3},{2,0},{3,1},{4,6},{5,7},{6,4},{7,5},{8,10},{9,11},{10,... | collective-permute-start | bytes 983048 | tf_op jit(solution)/shard_map/ppermute | solution.py:827
  12.4 4.6 %collective-permute-start = (bf16[80,2048]{1,0:T(8,128)(2,1)}, bf16[80,2048]{1,0:T(8,128)(2,1)S(1)}, u32[]{:S(2)}, u32[]{:S(2)}) collective-permute-start(bf16[80,2048]{1,0:T(8,128)(2,1)} %get-tuple-element.26), channel_id=1, source_target_pairs={{0,6},{1,7},{2,4},{3,5},{4,2},{5,3},{6,0},{7,1},{8,14},{9,15},{10,... | collective-permute-start | bytes 983048 | tf_op jit(solution)/shard_map/ppermute | solution.py:827
  16.9 0.4 collective-permute-start.5
  17.4 0.1 stack.75.spot_ref
  17.5 0.8 dynamic-slice_convert_fusion
  18.2 2.5 %collective-permute-done.3.refs_4_ = bf16[80,2048]{1,0:T(8,128)(2,1)S(1)} collective-permute-done((bf16[80,2048]{1,0:T(8,128)(2,1)}, bf16[80,2048]{1,0:T(8,128)(2,1)S(1)}, u32[]{:S(2)}, u32[]{:S(2)}) %collective-permute-start.3) | collective-permute-done | bytes 327712 | tf_op jit(solution)/shard_map/ppermute | solution.py:827
  20.8 10.2 %collective-permute-done.2.refs_3_ = bf16[80,2048]{1,0:T(8,128)(2,1)S(1)} collective-permute-done((bf16[80,2048]{1,0:T(8,128)(2,1)}, bf16[80,2048]{1,0:T(8,128)(2,1)S(1)}, u32[]{:S(2)}, u32[]{:S(2)}) %collective-permute-start.2) | collective-permute-done | bytes 327712 | tf_op jit(solution)/shard_map/ppermute | solution.py:827
  30.9 7.0 %collective-permute-done.refs_1_ = bf16[80,2048]{1,0:T(8,128)(2,1)S(1)} collective-permute-done((bf16[80,2048]{1,0:T(8,128)(2,1)}, bf16[80,2048]{1,0:T(8,128)(2,1)S(1)}, u32[]{:S(2)}, u32[]{:S(2)}) %collective-permute-start) | collective-permute-done | bytes 327712 | tf_op jit(solution)/shard_map/ppermute | solution.py:827
  38.0 1.8 collective-permute-done.5.refs_6_
  39.8 0.1 broadcast_in_dim.24.refs_8_
  39.9 8.8 %shard_map.172 = bf16[128,80,128]{2,1,0:T(8,128)(2,1)S(1)} custom-call(s32[10]{0:T(128)S(1)} %stack.75.spot_ref, bf16[80,2048]{1,0:T(8,128)(2,1)S(1)} %get-tuple-element.27.refs_0_, bf16[80,2048]{1,0:T(8,128)(2,1)S(1)} %collective-permute-done.refs_1_, bf16[80,2048]{1,0:T(8,128)(2,1)S(1)} %collective-permute-done.1.refs_2_, ...), custom_call_target="tpu_custom_call" | custom-call | flops 4000000000 | bytes 6397992 | tf_op jit(solution)/shard_map/pallas_call | solution.py:671
  48.7 1.5 copy-done
  50.2 13.3 %all-to-all-start = ((bf16[128,80,128]{2,1,0:T(8,128)(2,1)}), bf16[128,80,128]{2,1,0:T(8,128)(2,1)S(1)}, u32[]{:S(2)}, u32[]{:S(2)}) async-start(bf16[128,80,128]{2,1,0:T(8,128)(2,1)} %copy-done), calls=%async_computation | async-start | bytes 5242880 | tf_op jit(solution)/shard_map/all_to_all | solution.py:846
  63.6 0.6 dynamic_slice.42
  66.0 0.1 constant_dynamic-slice_fusion
  66.1 0.1 copy.21
  66.2 0.1 slice_reduce_fusion
  66.3 0.1 broadcast_in_dim.26
  66.4 0.1 fusion.14
  66.5 32.7 %all-to-all-done.in_ref = bf16[128,80,128]{2,1,0:T(8,128)(2,1)S(1)} async-done(((bf16[128,80,128]{2,1,0:T(8,128)(2,1)}), bf16[128,80,128]{2,1,0:T(8,128)(2,1)S(1)}, u32[]{:S(2)}, u32[]{:S(2)}) %all-to-all-start) | async-done | bytes 2621472 | tf_op jit(solution)/shard_map/all_to_all | solution.py:846
  99.3 0.1 broadcast_in_dim.30.high_ref
  99.4 0.1 broadcast_in_dim.28.low_ref
  99.5 15.5 %shard_map.173 = bf16[128,80,128]{2,1,0:T(8,128)(2,1)S(1)} custom-call(bf16[128,80,128]{2,1,0:T(8,128)(2,1)S(1)} %all-to-all-done.in_ref, s32[72,128]{1,0:T(8,128)S(1)} %broadcast_in_dim.28.low_ref, s32[72,128]{1,0:T(8,128)S(1)} %broadcast_in_dim.30.high_ref, f32[8,128]{1,0:T(8,128)S(1)} %iota.7.first_ref, f32[80,128]{1,0:T(8,128)S(1)} %copy-done.11, ...), custom_call_target="tpu_custom_call" | custom-call | flops 8000000000 | bytes 6451200 | tf_op jit(solution)/shard_map/pallas_call | solution.py:671
  115.0 1.5 copy-done.1
  116.5 4.9 %all-to-all-start.1 = ((bf16[128,80,128]{2,1,0:T(8,128)(2,1)}), bf16[128,80,128]{2,1,0:T(8,128)(2,1)S(1)}, u32[]{:S(2)}, u32[]{:S(2)}) async-start(bf16[128,80,128]{2,1,0:T(8,128)(2,1)} %copy-done.1), calls=%async_computation.1 | async-start | bytes 5242880 | tf_op jit(solution)/shard_map/all_to_all | solution.py:848
  121.4 0.1 stack.82.spot_ref
  121.5 35.7 %all-to-all-done.1.in_ref = bf16[128,80,128]{2,1,0:T(8,128)(2,1)S(1)} async-done(((bf16[128,80,128]{2,1,0:T(8,128)(2,1)}), bf16[128,80,128]{2,1,0:T(8,128)(2,1)S(1)}, u32[]{:S(2)}, u32[]{:S(2)}) %all-to-all-start.1) | async-done | bytes 2621472 | tf_op jit(solution)/shard_map/all_to_all | solution.py:848
  157.2 0.9 copy-done.4
  158.2 0.9 copy-done.5
  159.1 0.8 copy-done.14
  159.9 8.2 %shard_map.174 = (bf16[80,2176]{1,0:T(8,128)(2,1)S(1)}, bf16[80,2176]{1,0:T(8,128)(2,1)S(1)}, bf16[80,2176]{1,0:T(8,128)(2,1)S(1)}, bf16[80,2176]{1,0:T(8,128)(2...) custom-call(s32[8]{0:T(128)S(1)} %stack.82.spot_ref, ...), custom_call_target="tpu_custom_call" | custom-call | flops 4000000000 | bytes 6357024 | tf_op jit(solution)/shard_map/pallas_call | solution.py:671
  168.1 2.9 %collective-permute-start.8 = (bf16[80,2176]{1,0:T(8,128)(2,1)S(1)}, bf16[80,2176]{1,0:T(8,128)(2,1)S(1)}, u32[]{:S(2)}, u32[]{:S(2)}) collective-permute-start(bf16[80,2176]{1,0:T(8,128)(2,1)S(1)} %get-tuple-element.15), channel_id=1, source_target_pairs={{0,2},{1,3},{2,0},{3,1},{4,6},{5,7},{6,4},{7,5},{8,10},{9,11},{10,... | collective-permute-start | bytes 1044488 | tf_op jit(solution)/shard_map/ppermute | solution.py:827
  171.0 1.6 collective-permute-start.9
  172.7 2.0 collective-permute-start.10
  174.6 4.2 %collective-permute-done.7.refs_1_ = bf16[80,2176]{1,0:T(8,128)(2,1)S(1)} collective-permute-done((bf16[80,2176]{1,0:T(8,128)(2,1)S(1)}, bf16[80,2176]{1,0:T(8,128)(2,1)S(1)}, u32[]{:S(2)}, u32[]{:S(2)}) %collective-permute-start.7) | collective-permute-done | bytes 348192 | tf_op jit(solution)/shard_map/ppermute | solution.py:827
  178.9 14.9 %collective-permute-done.8.refs_2_ = bf16[80,2176]{1,0:T(8,128)(2,1)S(1)} collective-permute-done((bf16[80,2176]{1,0:T(8,128)(2,1)S(1)}, bf16[80,2176]{1,0:T(8,128)(2,1)S(1)}, u32[]{:S(2)}, u32[]{:S(2)}) %collective-permute-start.8) | collective-permute-done | bytes 348192 | tf_op jit(solution)/shard_map/ppermute | solution.py:827
  193.7 2.1 collective-permute-start.13
  195.8 6.3 %collective-permute-done.11.refs_5_ = bf16[80,2176]{1,0:T(8,128)(2,1)S(1)} collective-permute-done((bf16[80,2176]{1,0:T(8,128)(2,1)}, bf16[80,2176]{1,0:T(8,128)(2,1)S(1)}, u32[]{:S(2)}, u32[]{:S(2)}) %collective-permute-start.11) | collective-permute-done | bytes 348192 | tf_op jit(solution)/shard_map/ppermute | solution.py:827
  202.1 0.6 collective-permute-done.13.refs_7_
  202.7 6.1 %collective-permute-start.14 = (bf16[16,2176]{1,0:T(8,128)(2,1)S(1)}, bf16[16,2176]{1,0:T(8,128)(2,1)S(1)}, u32[]{:S(2)}, u32[]{:S(2)}) collective-permute-start(bf16[16,2176]{1,0:T(8,128)(2,1)S(1)} %fusion.11), channel_id=1, source_target_pairs={{0,8},{8,16},{16,24},{24,32},{32,40},{40,48},{48,56},{56,64},{64,7... | collective-permute-start | bytes 208904 | tf_op jit(solution)/shard_map/ppermute | solution.py:854
  208.9 1.9 collective-permute-start.15
  210.9 23.7 %shard_map.175.old_ref = f32[640,2048]{1,0:T(8,128)} custom-call(s32[10]{0:T(128)S(1)} %stack.75.spot_ref, bf16[80,2176]{1,0:T(8,128)(2,1)S(1)} %get-tuple-element.13.refs_0_, bf16[80,2176]{1,0:T(8,128)(2,1)S(1)} %collective-permute-done.7.refs_1_, bf16[80,2176]{1,0:T(8,128)(2,1)S(1)} %collective-permute-done.8.refs_2_, ...), custom_call_target="tpu_custom_call" | custom-call | flops 1000000000 | bytes 9437184 | tf_op jit(solution)/shard_map/pallas_call | solution.py:774
  234.6 2.2 shard_map.176
  (49 shorter events, 0.3 us)
Async XLA Ops:
  0.0 39.9 %copy-start.8 = (bf16[2,256,256]{2,1,0:T(8,128)(2,1)S(1)}, bf16[2,256,256]{2,1,0:T(8,128)(2,1)}, u32[]{:S(2)}) copy-start(bf16[2,256,256]{2,1,0:T(8,128)(2,1)} %constant.229.clone.refs_12_) | copy-start | bytes 786436
  0.0 39.9 %copy-start.9 = (bf16[2,256,256]{2,1,0:T(8,128)(2,1)S(1)}, bf16[2,256,256]{2,1,0:T(8,128)(2,1)}, u32[]{:S(2)}) copy-start(bf16[2,256,256]{2,1,0:T(8,128)(2,1)} %constant.228.clone.refs_11_) | copy-start | bytes 786436
  0.0 39.9 %copy-start.12 = (f32[64,128]{1,0:T(8,128)S(1)}, f32[64,128]{1,0:T(8,128)}, u32[]{:S(2)}) copy-start(f32[64,128]{1,0:T(8,128)} %constant.227.clone.refs_10_.ts_ref) | copy-start | bytes 98308
  0.0 39.9 %copy-start.13 = (f32[64,128]{1,0:T(8,128)S(1)}, f32[64,128]{1,0:T(8,128)}, u32[]{:S(2)}) copy-start(f32[64,128]{1,0:T(8,128)} %constant.226.clone.refs_9_.tc_ref) | copy-start | bytes 98308
  2.9 9.4 %collective-permute-start.6 = (bf16[80,2048]{1,0:T(8,128)(2,1)S(1)}, bf16[80,2048]{1,0:T(8,128)(2,1)S(1)}, u32[]{:S(2)}, u32[]{:S(2)}) collective-permute-start(bf16[80,2048]{1,0:T(8,128)(2,1)S(1)} %get-tuple-element.21), channel_id=1, source_target_pairs={{0,4},{1,5},{2,6},{3,7},{4,0},{5,1},{6,2},{7,3},{8,12},{9,13},{10,... | collective-permute-start | bytes 983048 | tf_op jit(solution)/shard_map/ppermute | solution.py:827
  5.1 11.9 %collective-permute-start.4 = (bf16[80,2048]{1,0:T(8,128)(2,1)S(1)}, bf16[80,2048]{1,0:T(8,128)(2,1)S(1)}, u32[]{:S(2)}, u32[]{:S(2)}) collective-permute-start(bf16[80,2048]{1,0:T(8,128)(2,1)S(1)} %get-tuple-element.22), channel_id=1, source_target_pairs={{0,1},{1,2},{2,3},{3,0},{4,5},{5,6},{6,7},{7,4},{8,9},{9,10},{10,1... | collective-permute-start | bytes 983048 | tf_op jit(solution)/shard_map/ppermute | solution.py:827
  6.7 14.1 %collective-permute-start.3 = (bf16[80,2048]{1,0:T(8,128)(2,1)}, bf16[80,2048]{1,0:T(8,128)(2,1)S(1)}, u32[]{:S(2)}, u32[]{:S(2)}) collective-permute-start(bf16[80,2048]{1,0:T(8,128)(2,1)} %get-tuple-element.23), channel_id=1, source_target_pairs={{0,7},{1,4},{2,5},{3,6},{4,3},{5,0},{6,1},{7,2},{8,15},{9,12},{10,... | collective-permute-start | bytes 983048 | tf_op jit(solution)/shard_map/ppermute | solution.py:827
  8.7 22.2 %collective-permute-start.2 = (bf16[80,2048]{1,0:T(8,128)(2,1)}, bf16[80,2048]{1,0:T(8,128)(2,1)S(1)}, u32[]{:S(2)}, u32[]{:S(2)}) collective-permute-start(bf16[80,2048]{1,0:T(8,128)(2,1)} %get-tuple-element.24), channel_id=1, source_target_pairs={{0,5},{1,6},{2,7},{3,4},{4,1},{5,2},{6,3},{7,0},{8,13},{9,14},{10,... | collective-permute-start | bytes 983048 | tf_op jit(solution)/shard_map/ppermute | solution.py:827
  9.1 21.9 %collective-permute-start.1 = (bf16[80,2048]{1,0:T(8,128)(2,1)}, bf16[80,2048]{1,0:T(8,128)(2,1)S(1)}, u32[]{:S(2)}, u32[]{:S(2)}) collective-permute-start(bf16[80,2048]{1,0:T(8,128)(2,1)} %get-tuple-element.25), channel_id=1, source_target_pairs={{0,2},{1,3},{2,0},{3,1},{4,6},{5,7},{6,4},{7,5},{8,10},{9,11},{10,... | collective-permute-start | bytes 983048 | tf_op jit(solution)/shard_map/ppermute | solution.py:827
  12.4 25.6 %collective-permute-start = (bf16[80,2048]{1,0:T(8,128)(2,1)}, bf16[80,2048]{1,0:T(8,128)(2,1)S(1)}, u32[]{:S(2)}, u32[]{:S(2)}) collective-permute-start(bf16[80,2048]{1,0:T(8,128)(2,1)} %get-tuple-element.26), channel_id=1, source_target_pairs={{0,6},{1,7},{2,4},{3,5},{4,2},{5,3},{6,0},{7,1},{8,14},{9,15},{10,... | collective-permute-start | bytes 983048 | tf_op jit(solution)/shard_map/ppermute | solution.py:827
  16.9 22.8 %collective-permute-start.5 = (bf16[80,2048]{1,0:T(8,128)(2,1)}, bf16[80,2048]{1,0:T(8,128)(2,1)S(1)}, u32[]{:S(2)}, u32[]{:S(2)}) collective-permute-start(bf16[80,2048]{1,0:T(8,128)(2,1)} %get-tuple-element.28), channel_id=1, source_target_pairs={{0,3},{1,0},{2,1},{3,2},{4,7},{5,4},{6,5},{7,6},{8,11},{9,8},{10,9... | collective-permute-start | bytes 983048 | tf_op jit(solution)/shard_map/ppermute | solution.py:827
  48.7 1.5 copy-start
  50.2 13.3 %copy-start.16 = (s32[128]{0:T(128)S(1)}, s32[128]{0:T(128)}, u32[]{:S(2)}) copy-start(s32[128]{0:T(128)} %constant.230.clone) | copy-start | bytes 1540
  50.2 15.2 %copy-start.15 = (s32[2,8193]{1,0:T(2,128)S(1)}, s32[2,8193]{1,0:T(2,128)}, u32[]{:S(2)}) copy-start(s32[2,8193]{1,0:T(2,128)} %param.20) | copy-start | bytes 196636
  50.2 49.2 %copy-start.6 = (bf16[2,256,256]{2,1,0:T(8,128)(2,1)S(1)}, bf16[2,256,256]{2,1,0:T(8,128)(2,1)}, u32[]{:S(2)}) copy-start(bf16[2,256,256]{2,1,0:T(8,128)(2,1)} %constant.234.clone.v_ref) | copy-start | bytes 786436
  50.2 49.2 %copy-start.7 = (bf16[2,256,256]{2,1,0:T(8,128)(2,1)S(1)}, bf16[2,256,256]{2,1,0:T(8,128)(2,1)}, u32[]{:S(2)}) copy-start(bf16[2,256,256]{2,1,0:T(8,128)(2,1)} %constant.233.clone.w_ref) | copy-start | bytes 786436
  50.2 49.2 %copy-start.10 = (f32[80,128]{1,0:T(8,128)S(1)}, f32[80,128]{1,0:T(8,128)}, u32[]{:S(2)}) copy-start(f32[80,128]{1,0:T(8,128)} %constant.232.clone.ts_ref) | copy-start | bytes 122884
  50.2 49.2 %copy-start.11 = (f32[80,128]{1,0:T(8,128)S(1)}, f32[80,128]{1,0:T(8,128)}, u32[]{:S(2)}) copy-start(f32[80,128]{1,0:T(8,128)} %constant.231.clone.tc_ref) | copy-start | bytes 122884
  50.2 49.0 %all-to-all-start = ((bf16[128,80,128]{2,1,0:T(8,128)(2,1)}), bf16[128,80,128]{2,1,0:T(8,128)(2,1)S(1)}, u32[]{:S(2)}, u32[]{:S(2)}) async-start(bf16[128,80,128]{2,1,0:T(8,128)(2,1)} %copy-done), calls=%async_computation | async-start | bytes 5242880 | tf_op jit(solution)/shard_map/all_to_all | solution.py:846
  115.0 1.5 copy-start.1
  116.5 40.7 %all-to-all-start.1 = ((bf16[128,80,128]{2,1,0:T(8,128)(2,1)}), bf16[128,80,128]{2,1,0:T(8,128)(2,1)S(1)}, u32[]{:S(2)}, u32[]{:S(2)}) async-start(bf16[128,80,128]{2,1,0:T(8,128)(2,1)} %copy-done.1), calls=%async_computation.1 | async-start | bytes 5242880 | tf_op jit(solution)/shard_map/all_to_all | solution.py:848
  121.5 89.4 %copy-start.2 = (bf16[256,256]{1,0:T(8,128)(2,1)S(1)}, bf16[256,256]{1,0:T(8,128)(2,1)}, u32[]{:S(2)}) copy-start(bf16[256,256]{1,0:T(8,128)(2,1)} %constant.237.clone.refs_8_) | copy-start | bytes 393220
  121.5 89.4 %copy-start.3 = (bf16[256,128]{1,0:T(8,128)(2,1)S(1)}, bf16[256,128]{1,0:T(8,128)(2,1)}, u32[]{:S(2)}) copy-start(bf16[256,128]{1,0:T(8,128)(2,1)} %constant.238.clone.refs_9_) | copy-start | bytes 196612
  157.2 1.0 copy-start.4
  158.2 0.9 copy-start.5
  159.1 0.8 copy-start.14
  168.1 10.7 %collective-permute-start.7 = (bf16[80,2176]{1,0:T(8,128)(2,1)S(1)}, bf16[80,2176]{1,0:T(8,128)(2,1)S(1)}, u32[]{:S(2)}, u32[]{:S(2)}) collective-permute-start(bf16[80,2176]{1,0:T(8,128)(2,1)S(1)} %get-tuple-element.14), channel_id=1, source_target_pairs={{0,6},{1,7},{2,4},{3,5},{4,2},{5,3},{6,0},{7,1},{8,14},{9,15},{10,... | collective-permute-start | bytes 1044488 | tf_op jit(solution)/shard_map/ppermute | solution.py:827
  168.1 25.6 %collective-permute-start.8 = (bf16[80,2176]{1,0:T(8,128)(2,1)S(1)}, bf16[80,2176]{1,0:T(8,128)(2,1)S(1)}, u32[]{:S(2)}, u32[]{:S(2)}) collective-permute-start(bf16[80,2176]{1,0:T(8,128)(2,1)S(1)} %get-tuple-element.15), channel_id=1, source_target_pairs={{0,2},{1,3},{2,0},{3,1},{4,6},{5,7},{6,4},{7,5},{8,10},{9,11},{10,... | collective-permute-start | bytes 1044488 | tf_op jit(solution)/shard_map/ppermute | solution.py:827
  171.0 24.8 %collective-permute-start.9 = (bf16[80,2176]{1,0:T(8,128)(2,1)}, bf16[80,2176]{1,0:T(8,128)(2,1)S(1)}, u32[]{:S(2)}, u32[]{:S(2)}) collective-permute-start(bf16[80,2176]{1,0:T(8,128)(2,1)} %get-tuple-element.16), channel_id=1, source_target_pairs={{0,5},{1,6},{2,7},{3,4},{4,1},{5,2},{6,3},{7,0},{8,13},{9,14},{10,... | collective-permute-start | bytes 1044488 | tf_op jit(solution)/shard_map/ppermute | solution.py:827
  172.7 23.1 %collective-permute-start.10 = (bf16[80,2176]{1,0:T(8,128)(2,1)}, bf16[80,2176]{1,0:T(8,128)(2,1)S(1)}, u32[]{:S(2)}, u32[]{:S(2)}) collective-permute-start(bf16[80,2176]{1,0:T(8,128)(2,1)} %get-tuple-element.17), channel_id=1, source_target_pairs={{0,7},{1,4},{2,5},{3,6},{4,3},{5,0},{6,1},{7,2},{8,15},{9,12},{10,... | collective-permute-start | bytes 1044488 | tf_op jit(solution)/shard_map/ppermute | solution.py:827
  174.6 27.4 %collective-permute-start.11 = (bf16[80,2176]{1,0:T(8,128)(2,1)}, bf16[80,2176]{1,0:T(8,128)(2,1)S(1)}, u32[]{:S(2)}, u32[]{:S(2)}) collective-permute-start(bf16[80,2176]{1,0:T(8,128)(2,1)} %get-tuple-element.18), channel_id=1, source_target_pairs={{0,1},{1,2},{2,3},{3,0},{4,5},{5,6},{6,7},{7,4},{8,9},{9,10},{10,1... | collective-permute-start | bytes 1044488 | tf_op jit(solution)/shard_map/ppermute | solution.py:827
  178.9 23.2 %collective-permute-start.12 = (bf16[80,2176]{1,0:T(8,128)(2,1)}, bf16[80,2176]{1,0:T(8,128)(2,1)S(1)}, u32[]{:S(2)}, u32[]{:S(2)}) collective-permute-start(bf16[80,2176]{1,0:T(8,128)(2,1)} %get-tuple-element.19), channel_id=1, source_target_pairs={{0,3},{1,0},{2,1},{3,2},{4,7},{5,4},{6,5},{7,6},{8,11},{9,8},{10,9... | collective-permute-start | bytes 1044488 | tf_op jit(solution)/shard_map/ppermute | solution.py:827
  193.7 9.0 %collective-permute-start.13 = (bf16[80,2176]{1,0:T(8,128)(2,1)S(1)}, bf16[80,2176]{1,0:T(8,128)(2,1)S(1)}, u32[]{:S(2)}, u32[]{:S(2)}) collective-permute-start(bf16[80,2176]{1,0:T(8,128)(2,1)S(1)} %get-tuple-element.20), channel_id=1, source_target_pairs={{0,4},{1,5},{2,6},{3,7},{4,0},{5,1},{6,2},{7,3},{8,12},{9,13},{10,... | collective-permute-start | bytes 1044488 | tf_op jit(solution)/shard_map/ppermute | solution.py:827
  202.7 31.8 %collective-permute-start.14 = (bf16[16,2176]{1,0:T(8,128)(2,1)S(1)}, bf16[16,2176]{1,0:T(8,128)(2,1)S(1)}, u32[]{:S(2)}, u32[]{:S(2)}) collective-permute-start(bf16[16,2176]{1,0:T(8,128)(2,1)S(1)} %fusion.11), channel_id=1, source_target_pairs={{0,8},{8,16},{16,24},{24,32},{32,40},{40,48},{48,56},{56,64},{64,7... | collective-permute-start | bytes 208904 | tf_op jit(solution)/shard_map/ppermute | solution.py:854
  208.9 25.6 %collective-permute-start.15 = (bf16[16,2176]{1,0:T(8,128)(2,1)S(1)}, bf16[16,2176]{1,0:T(8,128)(2,1)S(1)}, u32[]{:S(2)}, u32[]{:S(2)}) collective-permute-start(bf16[16,2176]{1,0:T(8,128)(2,1)S(1)} %fusion.5), channel_id=1, source_target_pairs={{8,0},{16,8},{24,16},{32,24},{40,32},{48,40},{56,48},{64,56},{72,6... | collective-permute-start | bytes 208904 | tf_op jit(solution)/shard_map/ppermute | solution.py:855

commit v3 on v2

--- a/solution.py
+++ b/solution.py
@@ -16,11 +16,13 @@
 R = 4
 ROWS = 80
 HALF = 64
-WIDE = 2176
+NEAR = 1280
+FAR = 896
 BF = jnp.bfloat16
 F32 = jnp.float32
 VMEM = pl.BlockSpec(memory_space=pltpu.VMEM)
 SMEM = pl.BlockSpec(memory_space=pltpu.SMEM)
+ANY = pl.BlockSpec(memory_space=pl.ANY)
 
 WAVES = [0] + [8 * n for n in range(1, 8)] + [4 + 8 * n for n in range(8)]
 WAVES += [q + 8 * n for q in (1, 2, 3) for n in range(16)]
@@ -230,12 +232,10 @@
     return high, low
 
 
-def forward_kernel(spot_ref, *refs):
-    blocks = refs[:8]
-    ok_ref, tc_ref, ts_ref, w_ref, w0_ref, out_ref, x_ref, stage, hi_ref, lo_ref = refs[8:]
-    for n in range(8):
-        x_ref[spot_ref[n]] = blocks[n][...]
-
+def forward_kernel(
+    x_ref, ok_ref, low_ref, high_ref, packed_ref, tc_ref, ts_ref, w_ref, w0_ref, out_ref,
+    stage, hi_ref, lo_ref
+):
     def tile_body(tile, carry):
         rows = pl.ds(pl.multiple_of(tile * 16, 16), 16)
         good = ok_ref[rows, :]
@@ -295,10 +295,7 @@
     lax.fori_loop(0, 9, wave_body, 0)
 
 
-def backward_kernel(spot_ref, in_ref, tc_ref, ts_ref, w_ref, w0_ref, *refs):
-    outs = refs[:8]
-    out_ref, stage, mid_ref = refs[8:]
-
+def backward_kernel(in_ref, tc_ref, ts_ref, w_ref, w0_ref, near_ref, far_ref, stage, mid_ref):
     def joined(slot):
         return jnp.concatenate([in_ref[2 * slot], in_ref[2 * slot + 1]], axis=1)
 
@@ -350,28 +347,30 @@
         for a in range(16):
             ys = series(a)
             for s in range(8):
-                out_ref[s, rows, a * 128 : (a + 1) * 128] = ys[s]
+                if a < 9:
+                    near_ref[s, rows, a * 128 + 128 : a * 128 + 256] = ys[s]
+                else:
+                    far_ref[s, rows, (a - 9) * 128 : (a - 8) * 128] = ys[s]
             if a in (0, 15):
                 ends[a] = ys
         blank = jnp.zeros((16, 128), BF)
         for s in range(8):
             after = ends[0][s + 1] if s < 7 else blank
             before = ends[15][s - 1] if s > 0 else blank
-            out_ref[s, rows, 2048:] = jnp.where(
+            near_ref[s, rows, :128] = jnp.where(
                 lane < 64, after.astype(F32), before.astype(F32)
             ).astype(BF)
         return carry
 
     lax.fori_loop(0, 5, tile_body, 0)
-    for n in range(8):
-        outs[n][...] = out_ref[spot_ref[n]]
 
 
 STEP = 8
 
 
 def channel_kernel(
-    in_ref, low_ref, high_ref, first_ref, tc_ref, ts_ref, w_ref, v_ref, out_ref, flat, u_re, u_im, a_re, a_im
+    in_ref, low_ref, high_ref, first_ref, tc_ref, ts_ref, w_ref, v_ref, out_ref,
+    flat, u_re, u_im, a_re, a_im
 ):
     def load_body(p, carry):
         flat[pl.ds(pl.multiple_of(p * ROWS, 8), ROWS), :] = in_ref[p].astype(F32)
@@ -475,10 +474,9 @@
 def spread(wide, start, block, count):
     block = block.astype(F32)
     rows = pl.ds(start, count)
-    for t in range(16):
-        wide[t + 1, rows, :] = block[:, t * 128 : (t + 1) * 128]
-    wide[0, rows, :] = block[:, 2048:]
-    wide[17, rows, :] = block[:, 2048:]
+    for t in range(17):
+        wide[t, rows, :] = block[:, t * 128 : (t + 1) * 128]
+    wide[17, rows, :] = block[:, :128]
 
 
 def ahead(parts, count, lane):
@@ -534,51 +532,63 @@
     change = (row == col + 125) * 1.0 - (row == col + 123) * 1.0
     shift = (row == col + 124) * 1.0
     nine = ((row >= col) & (row <= col + 8)) * 1.0
-    return np.concatenate([change, shift], axis=1), nine
-
-
-SLABS = 17
+    nine = np.concatenate([nine[:128], nine[128:]], axis=1)
+    return np.concatenate([change, shift], axis=1), np.concatenate([nine, nine], axis=0)
+
+
 BAND = 128
-
-
-def tensor_kernel(spot_ref, *refs):
-    blocks = refs[:8]
-    lanes_ref, nine_ref, out_ref, slope, level, prod, trio, hi_ref, lo_ref = refs[8:]
+PER = 9
+
+
+def tensor_kernel(half, place_ref, *refs):
+    if half == 0:
+        near_ref, lanes_ref, nine_ref, out_ref, slope, level, prod, trio, both_ref = refs
+    else:
+        near_ref, far_ref, lanes_ref, nine_ref, _, out_ref = refs[:6]
+        slope, level, prod, trio, both_ref = refs[6:]
     lane = lax.broadcasted_iota(jnp.int32, (8, 128), 1)
     step = pl.program_id(0)
-    part = spot_ref[9]
+    part = place_ref[1]
+
+    def lanes(t, cells):
+        res = dot(cells, lanes_ref[...])
+        slope[t, 16:656, :] = res[:, :128]
+        level[t, 16:656, :] = res[:, 128:]
+
+    def cut(ref, t):
+        return ref[:, pl.ds(pl.multiple_of(t * 128, 128), 256)]
 
     @pl.when(step == 0)
     def _():
-        def lanes(t, cells):
-            res = dot(cells, lanes_ref[...])
-            for n in range(8):
-                rows = pl.ds(pl.multiple_of(spot_ref[n] * ROWS + 16, 16), ROWS)
-                slope[t, rows, :] = res[n * ROWS : (n + 1) * ROWS, :128]
-                level[t, rows, :] = res[n * ROWS : (n + 1) * ROWS, 128:]
-
-        def row_body(t, carry):
-            cols = pl.ds(pl.multiple_of(t * 128 - 128, 128), 256)
-            lanes(t, jnp.concatenate([b[:, cols] for b in blocks], axis=0))
-            return carry
-
-        lax.fori_loop(1, 16, row_body, 0)
-        first = [jnp.concatenate([b[:, 2048:], b[:, :128]], axis=1) for b in blocks]
-        lanes(0, jnp.concatenate(first, axis=0))
-        last = [b[:, 1920:] for b in blocks]
-        lanes(16, jnp.concatenate(last, axis=0))
+        if half == 0:
+
+            def lanes_body(t, carry):
+                lanes(t, cut(near_ref, t))
+                return carry
+
+            lax.fori_loop(0, PER, lanes_body, 0)
+        else:
+
+            def lanes_body(t, carry):
+                lanes(t + 2, cut(far_ref, t))
+                return carry
+
+            lanes(0, near_ref[:, 1024:])
+            lanes(1, jnp.concatenate([near_ref[:, 1152:], far_ref[:, :128]], axis=1))
+            lax.fori_loop(0, PER - 3, lanes_body, 0)
+            lanes(8, jnp.concatenate([far_ref[:, 768:], near_ref[:, :128]], axis=1))
 
     top = step * BAND
 
     def prod_body(k, carry):
         start = pl.multiple_of(k * 8, 8)
         base = pl.multiple_of(top + k * 8, 8)
-        for t in range(SLABS):
+        for t in range(PER):
             grad_time = slope[t, pl.ds(base + 12, 8), :]
             masked = grad_time
-            if t == 0:
+            if half == 0 and t == 0:
                 masked = jnp.where((lane >= 4) | (part > 0), grad_time, 0.0)
-            if t == SLABS - 1:
+            if half == 1 and t == PER - 1:
                 masked = jnp.where((lane < 4) | (part < 7), grad_time, 0.0)
             grad_chan = level[t, pl.ds(base + 13, 8), :] - level[t, pl.ds(base + 11, 8), :]
             prod[0, t, pl.ds(start, 8), :] = grad_chan * masked
@@ -590,7 +600,7 @@
     def trio_body(k, carry):
         start = pl.multiple_of(k * 8, 8)
         for n in range(2):
-            for t in range(SLABS):
+            for t in range(PER):
                 trio[n, t, pl.ds(start, 8), :] = (
                     prod[n, t, pl.ds(start, 8), :]
                     + prod[n, t, pl.ds(start + 1, 8), :]
@@ -603,17 +613,15 @@
     def split_body(k, carry):
         start = pl.multiple_of(k * 16, 16)
         for n in range(2):
-            for t in range(SLABS):
+            for t in range(PER):
                 total = (
                     trio[n, t, pl.ds(start, 16), :]
                     + trio[n, t, pl.ds(start + 3, 16), :]
                     + trio[n, t, pl.ds(start + 6, 16), :]
                 )
-                for ref, value in zip((hi_ref, lo_ref), parted(total)):
-                    if t < SLABS - 1:
-                        ref[n, t, pl.ds(start, 16), :128] = value
-                    if t > 0:
-                        ref[n, t - 1, pl.ds(start, 16), 128:] = value
+                high, low = parted(total)
+                both_ref[n, t, pl.ds(start, 16), :128] = high
+                both_ref[n, t, pl.ds(start, 16), 128:] = low
         return carry
 
     lax.fori_loop(0, BAND // 16, split_body, 0)
@@ -623,25 +631,25 @@
     def sum_body(g, carry):
         sums = []
         for n in range(2):
-            high = hi_ref[n, pl.ds(g * 4, 4)].reshape(4 * BAND, 256)
-            low = lo_ref[n, pl.ds(g * 4, 4)].reshape(4 * BAND, 256)
-            sums.append(dot(high, nine) + dot(low, nine))
+            res = dot(both_ref[n, pl.ds(g * 4, 5)].reshape(5 * BAND, 256), nine)
+            sums.append(res[: 4 * BAND, :128] + res[BAND:, 128:])
         res = (sums[0] * -scale) / (sums[1] * scale + 1e-05)
         for t in range(4):
             cols = pl.ds(pl.multiple_of(g * 512 + t * 128, 128), 128)
             out_ref[:, cols] = res[t * BAND : (t + 1) * BAND]
         return carry
 
-    lax.fori_loop(0, 4, sum_body, 0)
-
-
-def edge_kernel(spot_ref, old_ref, rows_ref, out_ref, wide, prod):
+    lax.fori_loop(0, 2, sum_body, 0)
+
+
+def edge_kernel(place_ref, old_ref, rows_ref, out_ref, wide, prod):
     lane = lax.broadcasted_iota(jnp.int32, (8, 128), 1)
     sub = lax.broadcasted_iota(jnp.int32, (8, 128), 0)
     step = pl.program_id(0)
-    chan, part = spot_ref[8], spot_ref[9]
+    chan, part = place_ref[0], place_ref[1]
     for k in range(2):
-        spread(wide, k * 16, rows_ref[0, pl.ds(k * 16, 16), :], 16)
+        rows = pl.ds(k * 16, 16)
+        spread(wide, k * 16, rows_ref[0, rows, :], 16)
     open_low = (step == 0) & (chan == 0)
     open_high = (step == 1) & (chan == 15)
     skip = 8 - step * 8
@@ -666,13 +674,13 @@
     out_ref[...] = quotient(sums[0], sums[1], lane)
 
 
-def call(kernel, out, scratch, flops, *args, smem=0):
+def call(kernel, out, specs, scratch, flops, *args):
     nbytes = sum(a.size * a.dtype.itemsize for a in args) + 3 * 2**20
     return pl.pallas_call(
         kernel,
         out_shape=out,
-        in_specs=[SMEM] * smem + [VMEM] * (len(args) - smem),
-        out_specs=[VMEM] * len(out) if isinstance(out, list) else VMEM,
+        in_specs=[VMEM] * len(args),
+        out_specs=specs,
         scratch_shapes=scratch,
         compiler_params=pltpu.CompilerParams(vmem_limit_bytes=48 * 2**20),
         cost_estimate=pl.CostEstimate(flops=flops, bytes_accessed=nbytes, transcendentals=0),
@@ -687,52 +695,24 @@
     return jnp.asarray(table.astype(np.float32))
 
 
-def forward(spot, blocks, good):
+def forward(series, good, low, high, packed):
     fwd, _, first, _, tc, ts = time_tables()
     scratch = [
-        pltpu.VMEM((8, ROWS, 2048), BF),
         pltpu.VMEM((16, 8, 16, 128), F32),
         pltpu.VMEM((64 * ROWS, 256), BF),
         pltpu.VMEM((64 * ROWS, 256), BF),
     ]
     out = jax.ShapeDtypeStruct((128, ROWS, 128), BF)
-    return call(
-        forward_kernel,
-        out,
-        scratch,
-        4 * 10**9,
-        spot,
-        *blocks,
-        good,
-        single(tc),
-        single(ts),
-        pair(fwd),
-        pair(first),
-        smem=1,
-    )
-
-
-def backward(spot, spectra):
+    tables = single(tc), single(ts), pair(fwd), pair(first)
+    return call(forward_kernel, out, VMEM, scratch, 4 * 10**9, series, good, low, high, packed, *tables)
+
+
+def backward(spectra):
     _, bwd, _, last, tc, ts = time_tables()
-    scratch = [
-        pltpu.VMEM((8, ROWS, WIDE), BF),
-        pltpu.VMEM((16, 8, 16, 128), F32),
-        pltpu.VMEM((64 * ROWS, 256), F32),
-    ]
-    out = [jax.ShapeDtypeStruct((ROWS, WIDE), BF)] * 8
-    return call(
-        backward_kernel,
-        out,
-        scratch,
-        4 * 10**9,
-        spot,
-        spectra,
-        single(tc),
-        single(ts),
-        pair(bwd),
-        pair(last),
-        smem=1,
-    )
+    scratch = [pltpu.VMEM((16, 8, 16, 128), F32), pltpu.VMEM((64 * ROWS, 256), F32)]
+    out = [jax.ShapeDtypeStruct((8, ROWS, n), BF) for n in (NEAR, FAR)]
+    tables = single(tc), single(ts), pair(bwd), pair(last)
+    return call(backward_kernel, out, [VMEM, VMEM], scratch, 4 * 10**9, spectra, *tables)
 
 
 def channels(pencil, low, high, packed):
@@ -745,45 +725,39 @@
         pltpu.VMEM((ROWS, 8, 128), F32),
     ]
     out = jax.ShapeDtypeStruct((128, ROWS, 128), BF)
-    return call(
-        channel_kernel,
-        out,
-        scratch,
-        8 * 10**9,
-        pencil,
-        low,
-        high,
-        packed,
-        single(tc),
-        single(ts),
-        pair(fwd),
-        pair(bwd),
-    )
-
-
-def tensor(spot, blocks):
-    lanes, nine = slide_tables()
+    tables = single(tc), single(ts), pair(fwd), pair(bwd)
+    return call(channel_kernel, out, VMEM, scratch, 8 * 10**9, pencil, low, high, packed, *tables)
+
+
+def tensor(half, place, near, far=None, whole=None):
+    lanes, nine = (jnp.asarray(t.astype(ml_dtypes.bfloat16)) for t in slide_tables())
     scratch = [
-        pltpu.VMEM((SLABS, 672, 128), F32),
-        pltpu.VMEM((SLABS, 672, 128), F32),
-        pltpu.VMEM((2, SLABS, BAND + 16, 128), F32),
-        pltpu.VMEM((2, SLABS, BAND + 16, 128), F32),
-        pltpu.VMEM((2, 16, BAND, 256), BF),
-        pltpu.VMEM((2, 16, BAND, 256), BF),
+        pltpu.VMEM((PER, 672, 128), F32),
+        pltpu.VMEM((PER, 672, 128), F32),
+        pltpu.VMEM((2, PER, BAND + 16, 128), F32),
+        pltpu.VMEM((2, PER, BAND + 16, 128), F32),
+        pltpu.VMEM((2, PER, BAND, 256), BF),
     ]
+    if half == 0:
+        args, specs, alias = (place, near, lanes, nine), [SMEM] + [VMEM] * 3, {}
+    else:
+        args = (place, near, far, lanes, nine, whole)
+        specs = [SMEM] + [VMEM] * 4 + [pl.BlockSpec(memory_space=pl.ANY)]
+        alias = {5: 0}
     return pl.pallas_call(
-        tensor_kernel,
+        functools.partial(tensor_kernel, half),
         grid=(640 // BAND,),
         out_shape=jax.ShapeDtypeStruct((640, 2048), F32),
-        in_specs=[SMEM] + [VMEM] * 10,
-        out_specs=pl.BlockSpec((BAND, 2048), lambda g: (g, 0)),
+        in_specs=specs,
+        out_specs=pl.BlockSpec((BAND, 1024), lambda g: (g, half)),
         scratch_shapes=scratch,
-        compiler_params=pltpu.CompilerParams(vmem_limit_bytes=48 * 2**20),
+        input_output_aliases=alias,
+        compiler_params=pltpu.CompilerParams(vmem_limit_bytes=40 * 2**20),
         cost_estimate=pl.CostEstimate(flops=10**9, bytes_accessed=9 * 2**20, transcendentals=0),
-    )(spot, *blocks, jnp.asarray(lanes.astype(ml_dtypes.bfloat16)), jnp.asarray(nine.astype(ml_dtypes.bfloat16)))
-
-
-def edges(spot, whole, rows):
+    )(*args)
+
+
+def edges(place, whole, rows):
     scratch = [pltpu.VMEM((TILES, 32, 128), F32), pltpu.VMEM((2, TILES, 16, 128), F32)]
     return pl.pallas_call(
         edge_kernel,
@@ -792,14 +766,14 @@
         in_specs=[
             SMEM,
             pl.BlockSpec(memory_space=pl.ANY),
-            pl.BlockSpec((1, 32, WIDE), lambda g: (g, 0, 0)),
+            pl.BlockSpec((1, 32, NEAR + FAR), lambda g: (g, 0, 0)),
         ],
         out_specs=pl.BlockSpec((8, 2048), lambda g: (79 * g, 0)),
         scratch_shapes=scratch,
         input_output_aliases={1: 0},
         compiler_params=pltpu.CompilerParams(vmem_limit_bytes=16 * 2**20),
         cost_estimate=pl.CostEstimate(flops=10**7, bytes_accessed=2**19, transcendentals=0),
-    )(spot, whole, rows)
+    )(place, whole, rows)
 
 
 def window_bounds(fan_bounds, block):
@@ -814,50 +788,52 @@
     return both[0], both[1]
 
 
-MOVES = [(0, 0), (1, 2), (0, 2), (1, 1), (1, 3), (0, 1), (0, 3), (1, 0)]
-
-
-def moved(part, move, sign):
-    return (part // 4 + move[0]) % 2 * 4 + (part % 4 + sign * move[1]) % 4
-
-
-def traded(blocks):
-    out = [blocks[0]]
-    for move, block in list(zip(MOVES, blocks))[1:]:
-        out.append(lax.ppermute(block, "tm", [(j, moved(j, move, 1)) for j in range(8)]))
-    return out
+def after_kernel(value_ref, sign_ref, out_ref):
+    pass
+
+
+def after(value, sign):
+    return pl.pallas_call(
+        after_kernel,
+        out_shape=jax.ShapeDtypeStruct(value.shape, value.dtype),
+        in_specs=[ANY, ANY],
+        out_specs=ANY,
+        input_output_aliases={0: 0},
+        cost_estimate=pl.CostEstimate(flops=0, bytes_accessed=0, transcendentals=0),
+    )(value, sign)
+
+
+def trimmed(near, far):
+    top = jnp.concatenate([near[:16], far[:16]], axis=1)
+    bottom = jnp.concatenate([near[624:], far[624:]], axis=1)
+    above = lax.ppermute(bottom, "chan", [(i, i + 1) for i in range(15)])
+    below = lax.ppermute(top, "chan", [(i + 1, i) for i in range(15)])
+    return jnp.stack(
+        [jnp.concatenate([above, top], axis=0), jnp.concatenate([bottom, below], axis=0)]
+    )
 
 
 def per_device(record, channel_ok, fan_bounds):
     chan, part = lax.axis_index("chan"), lax.axis_index("tm")
     block = chan * 8 + part
-    targets = [moved(part, move, 1) for move in MOVES]
-    sources = [moved(part, move, -1) for move in MOVES]
-    to = jnp.stack(targets).astype(jnp.int32)
-    came = jnp.stack(sources + [chan, part]).astype(jnp.int32)
-    pieces = [lax.dynamic_slice(record, (t * ROWS, 0), (ROWS, 2048)) for t in targets]
-    series = traded(pieces)
+    place = jnp.stack([chan, part]).astype(jnp.int32)
+    series = lax.all_to_all(record.reshape(8, ROWS, 2048), "tm", 0, 0, tiled=True)
     good = lax.dynamic_slice(channel_ok, (part * ROWS,), (ROWS,)).astype(F32)
     good = jnp.broadcast_to(good[:, None], (ROWS, 128))
-    spectra = forward(came, series, good)
     low, high = window_bounds(fan_bounds, block)
     corner = lax.broadcasted_iota(jnp.int32, (8, 128), 0) == 0
     packed = (corner & (block == 0)).astype(F32)
+    spectra = forward(series, good, low, high, packed)
     pencil = lax.all_to_all(spectra, ("chan", "tm"), 0, 0, tiled=True)
     passed = channels(pencil, low, high, packed)
     back = lax.all_to_all(passed, ("chan", "tm"), 0, 0, tiled=True)
-    cells = traded(backward(to, back))
-    top, bottom = cells[0][:16], cells[0][64:]
-    for source, cell in list(zip(sources, cells))[1:]:
-        top = jnp.where(source == 0, cell[:16], top)
-        bottom = jnp.where(source == 7, cell[64:], bottom)
-    above = lax.ppermute(bottom, "chan", [(i, i + 1) for i in range(15)])
-    below = lax.ppermute(top, "chan", [(i + 1, i) for i in range(15)])
-    whole = tensor(came, cells)
-    rows = jnp.stack(
-        [jnp.concatenate([above, top], axis=0), jnp.concatenate([bottom, below], axis=0)]
-    )
-    return edges(came, whole, rows)
+    near, far = backward(back)
+    near = lax.all_to_all(near, "tm", 0, 0, tiled=True).reshape(640, NEAR)
+    whole = tensor(0, place, near)
+    far = lax.all_to_all(after(far, near), "tm", 0, 0, tiled=True).reshape(640, FAR)
+    rows = trimmed(near, far)
+    whole = tensor(1, place, near, far, whole)
+    return edges(place, whole, rows)
 
 
 def solution(mesh):

time: 237 us -> 217 us (0.916)
  blocking collectives: 0 us -> 108 us
  waiting for transfers between devices: 116 us -> 28 us
  starting transfers between devices: 49.2 us -> 19.9 us
  local copies, waits for them, and re-layouts: 10 us -> 1.41 us
  Pallas kernels: 58.5 us -> 56 us
    all_to_all x0 -> x3, blocking collectives: none -> 108 us  [the longest x1 43.9 us: per_device(): pencil = lax.all_to_all(spectra, ('chan', 'tm'), 0, 0, tiled=True)]
    ppermute x16 -> x2, waiting for transfers between devices: 47.6 us -> 0.01 us  [the longest x1 0.01 us: trimmed(): below = lax.ppermute(top, 'chan', [(i + 1, i) for i in range(15)])]
    all_to_all x2, waiting for transfers between devices: 68.5 us -> 28 us  [the longest x1 28 us: per_device(): lax.all_to_all(record.reshape(8, ROWS, 2048), 'tm', 0, 0, tiled=True)]
    ppermute x16 -> x2, starting transfers between devices: 31 us -> 9.21 us  [the longest x1 6.57 us: trimmed(): below = lax.ppermute(top, 'chan', [(i + 1, i) for i in range(15)])]
    all_to_all x2, starting transfers between devices: 18.1 us -> 10.7 us  [the longest x1 7.02 us: per_device(): lax.all_to_all(record.reshape(8, ROWS, 2048), 'tm', 0, 0, tiled=True)]
    unnamed x37 -> x35, local copies, waits for them, and re-layouts: 5.79 us -> 0.2 us
    dynamic_slice x1 -> x0, local copies, waits for them, and re-layouts: 2.9 us -> none  [per_device(): lax.dynamic_slice(record, (t * ROWS, 0), (ROWS, 2048))]
    pallas_call x4 -> x6, Pallas kernels: 56.3 us -> 53.8 us  [the longest x3 30.1 us: call(): pl.pallas_call(kernel, out_shape=out, in_specs=[VMEM] * len(args), out_sp...]
  transfers between devices with their start and end apart: 18 -> 4, of which waited for: 10 -> 1; matrix products, arithmetic and copies ran while one was open for 1% -> 1% of each run, Pallas kernels for 10% -> 11%
where the time goes in v3:
time: 217 us; the launch traced here: 216 us
  blocking collectives  108 us (50%)
  Pallas kernels  56 us (26%)
  waiting for transfers between devices  28 us (13%)
  starting transfers between devices  19.9 us (9%)
    all_to_all x1, blocking collectives, per_device(): pencil = lax.all_to_all(spectra, ('chan', 'tm'), 0, 0, tiled=True)  43.9 us
    all_to_all x1, blocking collectives, per_device(): back = lax.all_to_all(passed, ('chan', 'tm'), 0, 0, tiled=True)  40.2 us
    pallas_call x3, Pallas kernels, call(): pl.pallas_call(kernel, out_shape=out, in_specs=[VMEM] * len(args), out_sp...  30.1 us
    all_to_all x1, waiting for transfers between devices, per_device(): lax.all_to_all(record.reshape(8, ROWS, 2048), 'tm', 0, 0, tiled=True)  28 us
    pallas_call x2, Pallas kernels, tensor(): pl.pallas_call(functools.partial(tensor_kernel, half), grid=(640 // BAND,...  23.7 us
    all_to_all x1, blocking collectives, per_device(): near = lax.all_to_all(near, 'tm', 0, 0, tiled=True).reshape(640, NEAR)  23.5 us
    all_to_all x1, starting transfers between devices, per_device(): lax.all_to_all(record.reshape(8, ROWS, 2048), 'tm', 0, 0, tiled=True)  7.02 us
    ppermute x1, starting transfers between devices, trimmed(): below = lax.ppermute(top, 'chan', [(i + 1, i) for i in range(15)])  6.57 us
  transfers between devices with their start and end apart: 4, of which 1 were waited for; matrix products, arithmetic and copies ran while one was open for 1% of the time, Pallas kernels for 11%

profile of v3, /device:TPU:1, one launch (start us, length us, event | category | flops | bytes accessed | tf_op | source)
XLA Modules:
  0.0 216.0 jit_solution(6898969194472470512)
XLA Ops:
  0.0 0.0 copy-start.9
  0.0 0.0 copy-start.12
  0.0 0.0 copy-start.13
  0.0 7.0 %all-to-all-start = ((bf16[8,80,2048]{2,1,0:T(8,128)(2,1)}), bf16[8,80,2048]{2,1,0:T(8,128)(2,1)S(1)}, u32[]{:S(2)}, u32[]{:S(2)}) async-start(bf16[8,80,2048]{2,1,0:T(8,128)(2,1)} %bitcast.25), calls=%async_computation | async-start | bytes 5242880 | tf_op jit(solution)/shard_map/all_to_all | solution.py:820
  7.1 0.0 copy-done.15
  7.1 0.7 dynamic_slice.10
  9.0 0.0 copy-done.14
  9.6 0.1 constant_dynamic-slice_fusion
  9.7 0.1 copy.25
  9.8 0.8 dynamic-slice_convert_fusion
  10.6 0.1 slice_reduce_fusion
  10.7 0.1 broadcast_in_dim.26
  10.8 0.1 fusion.2
  10.9 28.0 %all-to-all-done.x_ref = bf16[8,80,2048]{2,1,0:T(8,128)(2,1)S(1)} async-done(((bf16[8,80,2048]{2,1,0:T(8,128)(2,1)}), bf16[8,80,2048]{2,1,0:T(8,128)(2,1)S(1)}, u32[]{:S(2)}, u32[]{:S(2)}) %all-to-all-start) | async-done | bytes 2621472 | tf_op jit(solution)/shard_map/all_to_all | solution.py:820
  38.8 0.1 broadcast_in_dim.24.ok_ref
  38.9 0.1 broadcast_in_dim.28.low_ref
  39.0 0.1 broadcast_in_dim.30.high_ref
  39.0 0.1 iota.7.packed_ref.first_ref
  39.1 0.0 copy-done.9
  39.1 0.0 copy-done.13
  39.1 8.1 %shard_map.190 = bf16[128,80,128]{2,1,0:T(8,128)(2,1)S(1)} custom-call(bf16[8,80,2048]{2,1,0:T(8,128)(2,1)S(1)} %all-to-all-done.x_ref, f32[80,128]{1,0:T(8,128)S(1)} %broadcast_in_dim.24.ok_ref, s32[72,128]{1,0:T(8,128)S(1)} %broadcast_in_dim.28.low_ref, s32[72,128]{1,0:T(8,128)S(1)} %broadcast_in_dim.30.high_ref, f32[8,128]{1,0:T(8,128)S(1)} %iota.7.packed_ref.first_ref, ...), custom_call_target="tpu_custom_call" | custom-call | flops 4000000000 | bytes 6475776 | tf_op jit(solution)/shard_map/pallas_call | solution.py:679
  47.2 0.0 copy-start.6
  47.3 0.0 copy-start.7
  47.3 0.0 copy-start.10
  47.3 0.0 copy-start.11
  47.3 43.9 %all_to_all.25.in_ref = bf16[128,80,128]{2,1,0:T(8,128)(2,1)S(1)} all-to-all(bf16[128,80,128]{2,1,0:T(8,128)(2,1)S(1)} %shard_map.190), channel_id=1, replica_groups=mesh['chan'=16,'tm'=8] {'chan','tm'}, dimensions={0} | all-to-all | bytes 5242880 | tf_op jit(solution)/shard_map/all_to_all | solution.py:827
  91.2 0.0 copy-done.10
  91.2 0.0 copy-done.11
  91.2 15.5 %shard_map.191 = bf16[128,80,128]{2,1,0:T(8,128)(2,1)S(1)} custom-call(bf16[128,80,128]{2,1,0:T(8,128)(2,1)S(1)} %all_to_all.25.in_ref, s32[72,128]{1,0:T(8,128)S(1)} %broadcast_in_dim.28.low_ref, s32[72,128]{1,0:T(8,128)S(1)} %broadcast_in_dim.30.high_ref, f32[8,128]{1,0:T(8,128)S(1)} %iota.7.packed_ref.first_ref, f32[80,128]{1,0:T(8,128)S(1)} %copy-done.10, ...), custom_call_target="tpu_custom_call" | custom-call | flops 8000000000 | bytes 6451200 | tf_op jit(solution)/shard_map/pallas_call | solution.py:679
  106.8 0.0 copy-start.4
  106.8 0.0 copy-start.5
  106.8 40.2 %all_to_all.26.in_ref = bf16[128,80,128]{2,1,0:T(8,128)(2,1)S(1)} all-to-all(bf16[128,80,128]{2,1,0:T(8,128)(2,1)S(1)} %shard_map.191), channel_id=1, replica_groups=mesh['chan'=16,'tm'=8] {'chan','tm'}, dimensions={0} | all-to-all | bytes 5242880 | tf_op jit(solution)/shard_map/all_to_all | solution.py:829
  146.9 0.0 copy-done.4
  146.9 6.5 %shard_map.192 = (bf16[8,80,1280]{2,1,0:T(8,128)(2,1)S(1)}, bf16[8,80,896]{2,1,0:T(8,128)(2,1)S(1)}) custom-call(bf16[128,80,128]{2,1,0:T(8,128)(2,1)S(1)} %all_to_all.26.in_ref, f32[64,128]{1,0:T(8,128)S(1)} %copy-done.12, f32[64,128]{1,0:T(8,128)S(1)} %copy-done.13, bf16[2,256,256]{2,1,0:T(8,128)(2,1)S(1)} %copy-done.4, bf16[2,256,256]{2,1,0:T(8,128)(2,1)S(1)} %copy-done.5), custom_call_target="tpu_custom_call" | custom-call | flops 4000000000 | bytes 6356992 | tf_op jit(solution)/shard_map/pallas_call | solution.py:679
  153.4 0.0 copy-start.1
  153.4 23.5 %all_to_all.27 = bf16[8,80,1280]{2,1,0:T(8,128)(2,1)} all-to-all(bf16[8,80,1280]{2,1,0:T(8,128)(2,1)S(1)} %get-tuple-element.7), channel_id=1, replica_groups=mesh['chan'=16,'tm'=8] {'tm'}, dimensions={0} | all-to-all | bytes 3276800 | tf_op jit(solution)/shard_map/all_to_all | solution.py:831
  176.9 0.0 copy-done.1
  176.9 3.7 %all-to-all-start.4 = ((bf16[8,80,896]{2,1,0:T(8,128)(2,1)}), bf16[8,80,896]{2,1,0:T(8,128)(2,1)S(1)}, u32[]{:S(2)}, u32[]{:S(2)}) async-start(bf16[8,80,896]{2,1,0:T(8,128)(2,1)} %shard_map.193), calls=%async_computation.4 | async-start | bytes 2293760 | tf_op jit(solution)/shard_map/all_to_all | solution.py:833
  180.6 0.1 pad_add_fusion.1.place_ref
  180.7 0.0 copy-done
  180.7 11.9 %shard_map.194.refs_4_ = f32[640,2048]{1,0:T(8,128)} custom-call(s32[2]{0:T(128)S(1)} %pad_add_fusion.1.place_ref, bf16[640,1280]{1,0:T(8,128)(2,1)S(1)} %bitcast.20, bf16[256,256]{1,0:T(8,128)(2,1)S(1)} %copy-done.2, bf16[256,256]{1,0:T(8,128)(2,1)S(1)} %copy-done.3), custom_call_target="tpu_custom_call" | custom-call | flops 1000000000 | bytes 9437184 | tf_op jit(solution)/shard_map/pallas_call | solution.py:747
  192.7 0.0 all-to-all-done.4
  192.7 6.6 %collective-permute-start.1 = (bf16[16,2176]{1,0:T(8,128)(2,1)S(1)}, bf16[16,2176]{1,0:T(8,128)(2,1)S(1)}, u32[]{:S(2)}, u32[]{:S(2)}) collective-permute-start(bf16[16,2176]{1,0:T(8,128)(2,1)S(1)} %pad_maximum_fusion.2), channel_id=1, source_target_pairs={{8,0},{16,8},{24,16},{32,24},{40,32},{48,40},{56,48},{64,56},{72,6... | collective-permute-start | bytes 208904 | tf_op jit(solution)/shard_map/ppermute | solution.py:810
  199.3 2.6 %collective-permute-start = (bf16[16,2176]{1,0:T(8,128)(2,1)S(1)}, bf16[16,2176]{1,0:T(8,128)(2,1)S(1)}, u32[]{:S(2)}, u32[]{:S(2)}) collective-permute-start(bf16[16,2176]{1,0:T(8,128)(2,1)S(1)} %pad_maximum_fusion.1), channel_id=1, source_target_pairs={{0,8},{8,16},{16,24},{24,32},{32,40},{40,48},{48,56},{56,64},{64,7... | collective-permute-start | bytes 208904 | tf_op jit(solution)/shard_map/ppermute | solution.py:809
  202.0 11.8 %shard_map.195.old_ref = f32[640,2048]{1,0:T(8,128)} custom-call(s32[2]{0:T(128)S(1)} %pad_add_fusion.1.place_ref, bf16[640,1280]{1,0:T(8,128)(2,1)S(1)} %bitcast.22, bf16[640,896]{1,0:T(8,128)(2,1)S(1)} %bitcast.24, bf16[256,256]{1,0:T(8,128)(2,1)S(1)} %copy-done.2, bf16[256,256]{1,0:T(8,128)(2,1)S(1)} %copy-done.3, ...), custom_call_target="tpu_custom_call", output_to_operand_aliasing={{}: (5, {})} | custom-call | flops 1000000000 | bytes 9437184 | tf_op jit(solution)/shard_map/pallas_call | solution.py:747
  213.7 0.0 collective-permute-done.1
  213.7 0.0 collective-permute-done
  213.8 2.2 %shard_map.196 = f32[640,2048]{1,0:T(8,128)} custom-call(s32[2]{0:T(128)S(1)} %pad_add_fusion.1.place_ref, f32[640,2048]{1,0:T(8,128)} %shard_map.195.old_ref, bf16[2,32,2176]{2,1,0:T(8,128)(2,1)S(1)} %pad_maximum_fusion.rows_ref), custom_call_target="tpu_custom_call", output_to_operand_aliasing={{}: (1, {})} | custom-call | flops 10000000 | bytes 524288 | tf_op jit(solution)/shard_map/pallas_call | solution.py:762
  (24 shorter events, 0.1 us)
Async XLA Ops:
  0.0 7.1 %copy-start.15 = (s32[128]{0:T(128)S(1)}, s32[128]{0:T(128)}, u32[]{:S(2)}) copy-start(s32[128]{0:T(128)} %constant.46.clone) | copy-start | bytes 1540
  0.0 9.0 %copy-start.14 = (s32[2,8193]{1,0:T(2,128)S(1)}, s32[2,8193]{1,0:T(2,128)}, u32[]{:S(2)}) copy-start(s32[2,8193]{1,0:T(2,128)} %param.22) | copy-start | bytes 196636
  0.0 39.1 %copy-start.8 = (bf16[2,256,256]{2,1,0:T(8,128)(2,1)S(1)}, bf16[2,256,256]{2,1,0:T(8,128)(2,1)}, u32[]{:S(2)}) copy-start(bf16[2,256,256]{2,1,0:T(8,128)(2,1)} %constant.49.clone.w_ref) | copy-start | bytes 786436
  0.0 39.1 %copy-start.9 = (bf16[2,256,256]{2,1,0:T(8,128)(2,1)S(1)}, bf16[2,256,256]{2,1,0:T(8,128)(2,1)}, u32[]{:S(2)}) copy-start(bf16[2,256,256]{2,1,0:T(8,128)(2,1)} %constant.50.clone.w0_ref) | copy-start | bytes 786436
  0.0 39.1 %copy-start.12 = (f32[64,128]{1,0:T(8,128)S(1)}, f32[64,128]{1,0:T(8,128)}, u32[]{:S(2)}) copy-start(f32[64,128]{1,0:T(8,128)} %constant.47.clone.tc_ref) | copy-start | bytes 98308
  0.0 39.1 %copy-start.13 = (f32[64,128]{1,0:T(8,128)S(1)}, f32[64,128]{1,0:T(8,128)}, u32[]{:S(2)}) copy-start(f32[64,128]{1,0:T(8,128)} %constant.48.clone.ts_ref) | copy-start | bytes 98308
  0.0 38.8 %all-to-all-start = ((bf16[8,80,2048]{2,1,0:T(8,128)(2,1)}), bf16[8,80,2048]{2,1,0:T(8,128)(2,1)S(1)}, u32[]{:S(2)}, u32[]{:S(2)}) async-start(bf16[8,80,2048]{2,1,0:T(8,128)(2,1)} %bitcast.25), calls=%async_computation | async-start | bytes 5242880 | tf_op jit(solution)/shard_map/all_to_all | solution.py:820
  47.2 44.0 %copy-start.6 = (bf16[2,256,256]{2,1,0:T(8,128)(2,1)S(1)}, bf16[2,256,256]{2,1,0:T(8,128)(2,1)}, u32[]{:S(2)}) copy-start(bf16[2,256,256]{2,1,0:T(8,128)(2,1)} %constant.53.clone.w_ref) | copy-start | bytes 786436
  47.3 44.0 %copy-start.7 = (bf16[2,256,256]{2,1,0:T(8,128)(2,1)S(1)}, bf16[2,256,256]{2,1,0:T(8,128)(2,1)}, u32[]{:S(2)}) copy-start(bf16[2,256,256]{2,1,0:T(8,128)(2,1)} %constant.54.clone.v_ref) | copy-start | bytes 786436
  47.3 43.9 %copy-start.10 = (f32[80,128]{1,0:T(8,128)S(1)}, f32[80,128]{1,0:T(8,128)}, u32[]{:S(2)}) copy-start(f32[80,128]{1,0:T(8,128)} %constant.51.clone.tc_ref) | copy-start | bytes 122884
  47.3 43.9 %copy-start.11 = (f32[80,128]{1,0:T(8,128)S(1)}, f32[80,128]{1,0:T(8,128)}, u32[]{:S(2)}) copy-start(f32[80,128]{1,0:T(8,128)} %constant.52.clone.ts_ref) | copy-start | bytes 122884
  106.8 40.2 %copy-start.4 = (bf16[2,256,256]{2,1,0:T(8,128)(2,1)S(1)}, bf16[2,256,256]{2,1,0:T(8,128)(2,1)}, u32[]{:S(2)}) copy-start(bf16[2,256,256]{2,1,0:T(8,128)(2,1)} %constant.55.clone.w_ref) | copy-start | bytes 786436
  106.8 40.2 %copy-start.5 = (bf16[2,256,256]{2,1,0:T(8,128)(2,1)S(1)}, bf16[2,256,256]{2,1,0:T(8,128)(2,1)}, u32[]{:S(2)}) copy-start(bf16[2,256,256]{2,1,0:T(8,128)(2,1)} %constant.56.clone.w0_ref) | copy-start | bytes 786436
  153.4 23.5 %copy-start.1 = (bf16[8,80,896]{2,1,0:T(8,128)(2,1)}, bf16[8,80,896]{2,1,0:T(8,128)(2,1)S(1)}, u32[]{:S(2)}) copy-start(bf16[8,80,896]{2,1,0:T(8,128)(2,1)S(1)} %get-tuple-element.8.value_ref) | copy-start | bytes 3440644
  176.9 3.8 %copy-start = (bf16[8,80,1280]{2,1,0:T(8,128)(2,1)S(1)}, bf16[8,80,1280]{2,1,0:T(8,128)(2,1)}, u32[]{:S(2)}) copy-start(bf16[8,80,1280]{2,1,0:T(8,128)(2,1)} %all_to_all.27) | copy-start | bytes 4915204
  176.9 3.8 %copy-start.2 = (bf16[256,256]{1,0:T(8,128)(2,1)S(1)}, bf16[256,256]{1,0:T(8,128)(2,1)}, u32[]{:S(2)}) copy-start(bf16[256,256]{1,0:T(8,128)(2,1)} %constant.57.clone.refs_1_.refs_2_) | copy-start | bytes 393220
  176.9 3.8 %copy-start.3 = (bf16[256,256]{1,0:T(8,128)(2,1)S(1)}, bf16[256,256]{1,0:T(8,128)(2,1)}, u32[]{:S(2)}) copy-start(bf16[256,256]{1,0:T(8,128)(2,1)} %constant.58.clone.refs_2_.refs_3_) | copy-start | bytes 393220
  176.9 15.8 %all-to-all-start.4 = ((bf16[8,80,896]{2,1,0:T(8,128)(2,1)}), bf16[8,80,896]{2,1,0:T(8,128)(2,1)S(1)}, u32[]{:S(2)}, u32[]{:S(2)}) async-start(bf16[8,80,896]{2,1,0:T(8,128)(2,1)} %shard_map.193), calls=%async_computation.4 | async-start | bytes 2293760 | tf_op jit(solution)/shard_map/all_to_all | solution.py:833
  192.7 21.0 %collective-permute-start.1 = (bf16[16,2176]{1,0:T(8,128)(2,1)S(1)}, bf16[16,2176]{1,0:T(8,128)(2,1)S(1)}, u32[]{:S(2)}, u32[]{:S(2)}) collective-permute-start(bf16[16,2176]{1,0:T(8,128)(2,1)S(1)} %pad_maximum_fusion.2), channel_id=1, source_target_pairs={{8,0},{16,8},{24,16},{32,24},{40,32},{48,40},{56,48},{64,56},{72,6... | collective-permute-start | bytes 208904 | tf_op jit(solution)/shard_map/ppermute | solution.py:810
  199.3 14.4 %collective-permute-start = (bf16[16,2176]{1,0:T(8,128)(2,1)S(1)}, bf16[16,2176]{1,0:T(8,128)(2,1)S(1)}, u32[]{:S(2)}, u32[]{:S(2)}) collective-permute-start(bf16[16,2176]{1,0:T(8,128)(2,1)S(1)} %pad_maximum_fusion.1), channel_id=1, source_target_pairs={{0,8},{8,16},{16,24},{24,32},{32,40},{40,48},{48,56},{56,64},{64,7... | collective-permute-start | bytes 208904 | tf_op jit(solution)/shard_map/ppermute | solution.py:809

commit v4 on v3

--- a/solution.py
+++ b/solution.py
@@ -15,7 +15,7 @@
 TF = 128
 R = 4
 ROWS = 80
-HALF = 64
+GROUP = 63
 NEAR = 1280
 FAR = 896
 BF = jnp.bfloat16
@@ -275,7 +275,7 @@
                 twist(16 * q + n, ys[n])
         return carry
 
-    lax.fori_loop(0, 5, tile_body, 0)
+    lax.fori_loop(0, 5, tile_body, 0, unroll=5)
 
     def mixed(rows, w):
         high, low = hi_ref[rows, :], lo_ref[rows, :]
@@ -286,13 +286,13 @@
     out_ref[1] = first[:, 128:]
 
     def wave_body(step, carry):
-        res = mixed(pl.ds(pl.multiple_of(ROWS + step * 7 * ROWS, 16), 7 * ROWS), w_ref).astype(BF)
-        for n in range(7):
-            out_ref[2 + 14 * step + 2 * n] = res[n * ROWS : (n + 1) * ROWS, :128]
-            out_ref[3 + 14 * step + 2 * n] = res[n * ROWS : (n + 1) * ROWS, 128:]
-        return carry
-
-    lax.fori_loop(0, 9, wave_body, 0)
+        res = mixed(pl.ds(pl.multiple_of(ROWS + step * GROUP * ROWS, 16), GROUP * ROWS), w_ref).astype(BF)
+        for n in range(GROUP):
+            out_ref[2 + 2 * GROUP * step + 2 * n] = res[n * ROWS : (n + 1) * ROWS, :128]
+            out_ref[3 + 2 * GROUP * step + 2 * n] = res[n * ROWS : (n + 1) * ROWS, 128:]
+        return carry
+
+    lax.fori_loop(0, 63 // GROUP, wave_body, 0)
 
 
 def backward_kernel(in_ref, tc_ref, ts_ref, w_ref, w0_ref, near_ref, far_ref, stage, mid_ref):
@@ -303,13 +303,13 @@
     mid_ref[pl.ds(0, ROWS), :] = dot(first, w0_ref[0]) + dot(first, w0_ref[1])
 
     def wave_body(step, carry):
-        data = jnp.concatenate([joined(1 + step * 7 + n) for n in range(7)], axis=0)
-        mid_ref[pl.ds(pl.multiple_of(ROWS + step * 7 * ROWS, 16), 7 * ROWS), :] = dot(
+        data = jnp.concatenate([joined(1 + step * GROUP + n) for n in range(GROUP)], axis=0)
+        mid_ref[pl.ds(pl.multiple_of(ROWS + step * GROUP * ROWS, 16), GROUP * ROWS), :] = dot(
             data, w_ref[0]
         ) + dot(data, w_ref[1])
         return carry
 
-    lax.fori_loop(0, 9, wave_body, 0)
+    lax.fori_loop(0, 63 // GROUP, wave_body, 0)
     lane = lax.broadcasted_iota(jnp.int32, (16, 128), 1)
 
     def tile_body(tile, carry):
@@ -362,10 +362,10 @@
             ).astype(BF)
         return carry
 
-    lax.fori_loop(0, 5, tile_body, 0)
-
-
-STEP = 8
+    lax.fori_loop(0, 5, tile_body, 0, unroll=5)
+
+
+STEP = 40
 
 
 def channel_kernel(
@@ -376,7 +376,7 @@
         flat[pl.ds(pl.multiple_of(p * ROWS, 8), ROWS), :] = in_ref[p].astype(F32)
         return carry
 
-    lax.fori_loop(0, 128, load_body, 0, unroll=4)
+    lax.fori_loop(0, 128, load_body, 0, unroll=16)
     packed = first_ref[...]
     blank = jnp.zeros((8, 128), F32)
 
@@ -465,7 +465,7 @@
         out_ref[p] = flat[pl.ds(pl.multiple_of(p * ROWS, 8), ROWS), :].astype(BF)
         return carry
 
-    lax.fori_loop(0, 128, store_body, 0, unroll=4)
+    lax.fori_loop(0, 128, store_body, 0, unroll=16)
 
 
 TILES = 18
@@ -566,7 +566,7 @@
                 lanes(t, cut(near_ref, t))
                 return carry
 
-            lax.fori_loop(0, PER, lanes_body, 0)
+            lax.fori_loop(0, PER, lanes_body, 0, unroll=PER)
         else:
 
             def lanes_body(t, carry):
@@ -575,7 +575,7 @@
 
             lanes(0, near_ref[:, 1024:])
             lanes(1, jnp.concatenate([near_ref[:, 1152:], far_ref[:, :128]], axis=1))
-            lax.fori_loop(0, PER - 3, lanes_body, 0)
+            lax.fori_loop(0, PER - 3, lanes_body, 0, unroll=PER - 3)
             lanes(8, jnp.concatenate([far_ref[:, 768:], near_ref[:, :128]], axis=1))
 
     top = step * BAND
@@ -595,7 +595,7 @@
             prod[1, t, pl.ds(start, 8), :] = grad_time * masked
         return carry
 
-    lax.fori_loop(0, BAND // 8 + 2, prod_body, 0)
+    lax.fori_loop(0, BAND // 8 + 2, prod_body, 0, unroll=BAND // 8 + 2)
 
     def trio_body(k, carry):
         start = pl.multiple_of(k * 8, 8)
@@ -608,7 +608,7 @@
                 )
         return carry
 
-    lax.fori_loop(0, BAND // 8 + 1, trio_body, 0)
+    lax.fori_loop(0, BAND // 8 + 1, trio_body, 0, unroll=BAND // 8 + 1)
 
     def split_body(k, carry):
         start = pl.multiple_of(k * 16, 16)
@@ -624,7 +624,7 @@
                 both_ref[n, t, pl.ds(start, 16), 128:] = low
         return carry
 
-    lax.fori_loop(0, BAND // 16, split_body, 0)
+    lax.fori_loop(0, BAND // 16, split_body, 0, unroll=BAND // 16)
     nine = nine_ref[...]
     scale = 1.0 / 324.0
 
@@ -639,7 +639,7 @@
             out_ref[:, cols] = res[t * BAND : (t + 1) * BAND]
         return carry
 
-    lax.fori_loop(0, 2, sum_body, 0)
+    lax.fori_loop(0, 2, sum_body, 0, unroll=2)
 
 
 def edge_kernel(place_ref, old_ref, rows_ref, out_ref, wide, prod):

time: 217 us -> 203 us (0.935)
  Pallas kernels: 56 us -> 36.1 us
  waiting for transfers between devices: 28 us -> 33.7 us
    pallas_call x2, Pallas kernels: 23.7 us -> 12.5 us  [tensor(): pl.pallas_call(functools.partial(tensor_kernel, half), grid=(640 // BAND,...]
    pallas_call x3, Pallas kernels: 30.1 us -> 21.4 us  [call(): pl.pallas_call(kernel, out_shape=out, in_specs=[VMEM] * len(args), out_sp...]
    all_to_all x1, waiting for transfers between devices: 0.01 us -> 5.67 us  [per_device(): lax.all_to_all(after(far, near), 'tm', 0, 0, tiled=True).reshape(640, FAR)]
  transfers between devices with their start and end apart: 4 -> 4, of which waited for: 1 -> 2; matrix products, arithmetic and copies ran while one was open for 1% -> 1% of each run, Pallas kernels for 11% -> 6%
where the time goes in v4:
time: 203 us; the launch traced here: 202 us
  blocking collectives  108 us (53%)
  Pallas kernels  36.1 us (18%)
  waiting for transfers between devices  33.7 us (17%)
  starting transfers between devices  20 us (10%)
  between operations  2.13 us (1%)
    all_to_all x1, blocking collectives, per_device(): pencil = lax.all_to_all(spectra, ('chan', 'tm'), 0, 0, tiled=True)  43.9 us
    all_to_all x1, blocking collectives, per_device(): back = lax.all_to_all(passed, ('chan', 'tm'), 0, 0, tiled=True)  40.2 us
    all_to_all x1, waiting for transfers between devices, per_device(): lax.all_to_all(record.reshape(8, ROWS, 2048), 'tm', 0, 0, tiled=True)  28 us
    all_to_all x1, blocking collectives, per_device(): near = lax.all_to_all(near, 'tm', 0, 0, tiled=True).reshape(640, NEAR)  23.5 us
    pallas_call x3, Pallas kernels, call(): pl.pallas_call(kernel, out_shape=out, in_specs=[VMEM] * len(args), out_sp...  21.4 us
    pallas_call x2, Pallas kernels, tensor(): pl.pallas_call(functools.partial(tensor_kernel, half), grid=(640 // BAND,...  12.5 us
    all_to_all x1, starting transfers between devices, per_device(): lax.all_to_all(record.reshape(8, ROWS, 2048), 'tm', 0, 0, tiled=True)  7.02 us
    ppermute x1, starting transfers between devices, trimmed(): below = lax.ppermute(top, 'chan', [(i + 1, i) for i in range(15)])  6.64 us
  transfers between devices with their start and end apart: 4, of which 2 were waited for; matrix products, arithmetic and copies ran while one was open for 1% of the time, Pallas kernels for 6%

profile of v4, /device:TPU:1, one launch (start us, length us, event | category | flops | bytes accessed | tf_op | source)
XLA Modules:
  0.0 201.9 jit_solution(16842129648789891001)
XLA Ops:
  0.0 0.0 copy-start.9
  0.0 0.0 copy-start.12
  0.0 0.0 copy-start.13
  0.0 7.0 %all-to-all-start = ((bf16[8,80,2048]{2,1,0:T(8,128)(2,1)}), bf16[8,80,2048]{2,1,0:T(8,128)(2,1)S(1)}, u32[]{:S(2)}, u32[]{:S(2)}) async-start(bf16[8,80,2048]{2,1,0:T(8,128)(2,1)} %bitcast.25), calls=%async_computation | async-start | bytes 5242880 | tf_op jit(solution)/shard_map/all_to_all | solution.py:820
  7.1 0.0 copy-done.15
  7.1 0.7 dynamic_slice.10
  9.0 0.0 copy-done.14
  9.6 0.1 constant_dynamic-slice_fusion
  9.7 0.1 copy.25
  9.8 0.8 dynamic-slice_convert_fusion
  10.6 0.1 slice_reduce_fusion
  10.7 0.1 broadcast_in_dim.26
  10.8 0.1 fusion.2
  10.9 28.0 %all-to-all-done.x_ref = bf16[8,80,2048]{2,1,0:T(8,128)(2,1)S(1)} async-done(((bf16[8,80,2048]{2,1,0:T(8,128)(2,1)}), bf16[8,80,2048]{2,1,0:T(8,128)(2,1)S(1)}, u32[]{:S(2)}, u32[]{:S(2)}) %all-to-all-start) | async-done | bytes 2621472 | tf_op jit(solution)/shard_map/all_to_all | solution.py:820
  38.8 0.1 broadcast_in_dim.24.ok_ref
  38.9 0.1 broadcast_in_dim.28.low_ref
  39.0 0.1 broadcast_in_dim.30.high_ref
  39.0 0.1 iota.7.packed_ref.first_ref
  39.1 0.0 copy-done.8
  39.1 0.0 copy-done.9
  39.1 0.0 copy-done.12
  39.1 0.0 copy-done.13
  39.1 6.0 %shard_map.190 = bf16[128,80,128]{2,1,0:T(8,128)(2,1)S(1)} custom-call(bf16[8,80,2048]{2,1,0:T(8,128)(2,1)S(1)} %all-to-all-done.x_ref, f32[80,128]{1,0:T(8,128)S(1)} %broadcast_in_dim.24.ok_ref, s32[72,128]{1,0:T(8,128)S(1)} %broadcast_in_dim.28.low_ref, s32[72,128]{1,0:T(8,128)S(1)} %broadcast_in_dim.30.high_ref, f32[8,128]{1,0:T(8,128)S(1)} %iota.7.packed_ref.first_ref, ...), custom_call_target="tpu_custom_call" | custom-call | flops 4000000000 | bytes 6475776 | tf_op jit(solution)/shard_map/pallas_call | solution.py:679
  45.1 0.0 copy-start.6
  45.1 0.0 copy-start.7
  45.2 0.0 copy-start.10
  45.2 0.0 copy-start.11
  45.2 43.9 %all_to_all.25.in_ref = bf16[128,80,128]{2,1,0:T(8,128)(2,1)S(1)} all-to-all(bf16[128,80,128]{2,1,0:T(8,128)(2,1)S(1)} %shard_map.190), channel_id=1, replica_groups=mesh['chan'=16,'tm'=8] {'chan','tm'}, dimensions={0} | all-to-all | bytes 5242880 | tf_op jit(solution)/shard_map/all_to_all | solution.py:827
  89.1 0.0 copy-done.6
  89.1 0.0 copy-done.7
  89.1 0.0 copy-done.10
  89.1 0.0 copy-done.11
  89.1 11.6 %shard_map.191 = bf16[128,80,128]{2,1,0:T(8,128)(2,1)S(1)} custom-call(bf16[128,80,128]{2,1,0:T(8,128)(2,1)S(1)} %all_to_all.25.in_ref, s32[72,128]{1,0:T(8,128)S(1)} %broadcast_in_dim.28.low_ref, s32[72,128]{1,0:T(8,128)S(1)} %broadcast_in_dim.30.high_ref, f32[8,128]{1,0:T(8,128)S(1)} %iota.7.packed_ref.first_ref, f32[80,128]{1,0:T(8,128)S(1)} %copy-done.10, ...), custom_call_target="tpu_custom_call" | custom-call | flops 8000000000 | bytes 6451200 | tf_op jit(solution)/shard_map/pallas_call | solution.py:679
  100.7 0.0 copy-start.4
  100.8 0.0 copy-start.5
  100.8 40.2 %all_to_all.26.in_ref = bf16[128,80,128]{2,1,0:T(8,128)(2,1)S(1)} all-to-all(bf16[128,80,128]{2,1,0:T(8,128)(2,1)S(1)} %shard_map.191), channel_id=1, replica_groups=mesh['chan'=16,'tm'=8] {'chan','tm'}, dimensions={0} | all-to-all | bytes 5242880 | tf_op jit(solution)/shard_map/all_to_all | solution.py:829
  140.9 3.8 %shard_map.192 = (bf16[8,80,1280]{2,1,0:T(8,128)(2,1)S(1)}, bf16[8,80,896]{2,1,0:T(8,128)(2,1)S(1)}) custom-call(bf16[128,80,128]{2,1,0:T(8,128)(2,1)S(1)} %all_to_all.26.in_ref, f32[64,128]{1,0:T(8,128)S(1)} %copy-done.12, f32[64,128]{1,0:T(8,128)S(1)} %copy-done.13, bf16[2,256,256]{2,1,0:T(8,128)(2,1)S(1)} %copy-done.4, bf16[2,256,256]{2,1,0:T(8,128)(2,1)S(1)} %copy-done.5), custom_call_target="tpu_custom_call" | custom-call | flops 4000000000 | bytes 6356992 | tf_op jit(solution)/shard_map/pallas_call | solution.py:679
  144.8 23.5 %all_to_all.27 = bf16[8,80,1280]{2,1,0:T(8,128)(2,1)} all-to-all(bf16[8,80,1280]{2,1,0:T(8,128)(2,1)S(1)} %get-tuple-element.7), channel_id=1, replica_groups=mesh['chan'=16,'tm'=8] {'tm'}, dimensions={0} | all-to-all | bytes 3276800 | tf_op jit(solution)/shard_map/all_to_all | solution.py:831
  168.3 3.7 %all-to-all-start.4 = ((bf16[8,80,896]{2,1,0:T(8,128)(2,1)}), bf16[8,80,896]{2,1,0:T(8,128)(2,1)S(1)}, u32[]{:S(2)}, u32[]{:S(2)}) async-start(bf16[8,80,896]{2,1,0:T(8,128)(2,1)} %shard_map.193), calls=%async_computation.4 | async-start | bytes 2293760 | tf_op jit(solution)/shard_map/all_to_all | solution.py:833
  172.0 0.1 pad_add_fusion.1.place_ref
  172.1 6.2 %shard_map.194.refs_4_ = f32[640,2048]{1,0:T(8,128)} custom-call(s32[2]{0:T(128)S(1)} %pad_add_fusion.1.place_ref, bf16[640,1280]{1,0:T(8,128)(2,1)S(1)} %bitcast.20, bf16[256,256]{1,0:T(8,128)(2,1)S(1)} %copy-done.2, bf16[256,256]{1,0:T(8,128)(2,1)S(1)} %copy-done.3), custom_call_target="tpu_custom_call" | custom-call | flops 1000000000 | bytes 9437184 | tf_op jit(solution)/shard_map/pallas_call | solution.py:747
  178.3 5.7 %all-to-all-done.4 = bf16[8,80,896]{2,1,0:T(8,128)(2,1)S(1)} async-done(((bf16[8,80,896]{2,1,0:T(8,128)(2,1)}), bf16[8,80,896]{2,1,0:T(8,128)(2,1)S(1)}, u32[]{:S(2)}, u32[]{:S(2)}) %all-to-all-start.4) | async-done | bytes 1146912 | tf_op jit(solution)/shard_map/all_to_all | solution.py:833
  184.0 6.6 %collective-permute-start.1 = (bf16[16,2176]{1,0:T(8,128)(2,1)S(1)}, bf16[16,2176]{1,0:T(8,128)(2,1)S(1)}, u32[]{:S(2)}, u32[]{:S(2)}) collective-permute-start(bf16[16,2176]{1,0:T(8,128)(2,1)S(1)} %pad_maximum_fusion.2), channel_id=1, source_target_pairs={{8,0},{16,8},{24,16},{32,24},{40,32},{48,40},{56,48},{64,56},{72,6... | collective-permute-start | bytes 208904 | tf_op jit(solution)/shard_map/ppermute | solution.py:810
  190.7 2.6 %collective-permute-start = (bf16[16,2176]{1,0:T(8,128)(2,1)S(1)}, bf16[16,2176]{1,0:T(8,128)(2,1)S(1)}, u32[]{:S(2)}, u32[]{:S(2)}) collective-permute-start(bf16[16,2176]{1,0:T(8,128)(2,1)S(1)} %pad_maximum_fusion.1), channel_id=1, source_target_pairs={{0,8},{8,16},{16,24},{24,32},{32,40},{40,48},{48,56},{56,64},{64,7... | collective-permute-start | bytes 208904 | tf_op jit(solution)/shard_map/ppermute | solution.py:809
  193.3 6.3 %shard_map.195.old_ref = f32[640,2048]{1,0:T(8,128)} custom-call(s32[2]{0:T(128)S(1)} %pad_add_fusion.1.place_ref, bf16[640,1280]{1,0:T(8,128)(2,1)S(1)} %bitcast.22, bf16[640,896]{1,0:T(8,128)(2,1)S(1)} %bitcast.24, bf16[256,256]{1,0:T(8,128)(2,1)S(1)} %copy-done.2, bf16[256,256]{1,0:T(8,128)(2,1)S(1)} %copy-done.3, ...), custom_call_target="tpu_custom_call", output_to_operand_aliasing={{}: (5, {})} | custom-call | flops 1000000000 | bytes 9437184 | tf_op jit(solution)/shard_map/pallas_call | solution.py:747
  199.6 0.0 collective-permute-done.1
  199.6 0.0 collective-permute-done
  199.7 2.2 %shard_map.196 = f32[640,2048]{1,0:T(8,128)} custom-call(s32[2]{0:T(128)S(1)} %pad_add_fusion.1.place_ref, f32[640,2048]{1,0:T(8,128)} %shard_map.195.old_ref, bf16[2,32,2176]{2,1,0:T(8,128)(2,1)S(1)} %pad_maximum_fusion.rows_ref), custom_call_target="tpu_custom_call", output_to_operand_aliasing={{}: (1, {})} | custom-call | flops 10000000 | bytes 524288 | tf_op jit(solution)/shard_map/pallas_call | solution.py:762
  (24 shorter events, 0.1 us)
Async XLA Ops:
  0.0 7.1 %copy-start.15 = (s32[128]{0:T(128)S(1)}, s32[128]{0:T(128)}, u32[]{:S(2)}) copy-start(s32[128]{0:T(128)} %constant.46.clone) | copy-start | bytes 1540
  0.0 9.0 %copy-start.14 = (s32[2,8193]{1,0:T(2,128)S(1)}, s32[2,8193]{1,0:T(2,128)}, u32[]{:S(2)}) copy-start(s32[2,8193]{1,0:T(2,128)} %param.22) | copy-start | bytes 196636
  0.0 39.1 %copy-start.8 = (bf16[2,256,256]{2,1,0:T(8,128)(2,1)S(1)}, bf16[2,256,256]{2,1,0:T(8,128)(2,1)}, u32[]{:S(2)}) copy-start(bf16[2,256,256]{2,1,0:T(8,128)(2,1)} %constant.49.clone.w_ref) | copy-start | bytes 786436
  0.0 39.1 %copy-start.9 = (bf16[2,256,256]{2,1,0:T(8,128)(2,1)S(1)}, bf16[2,256,256]{2,1,0:T(8,128)(2,1)}, u32[]{:S(2)}) copy-start(bf16[2,256,256]{2,1,0:T(8,128)(2,1)} %constant.50.clone.w0_ref) | copy-start | bytes 786436
  0.0 39.1 %copy-start.12 = (f32[64,128]{1,0:T(8,128)S(1)}, f32[64,128]{1,0:T(8,128)}, u32[]{:S(2)}) copy-start(f32[64,128]{1,0:T(8,128)} %constant.47.clone.tc_ref) | copy-start | bytes 98308
  0.0 39.1 %copy-start.13 = (f32[64,128]{1,0:T(8,128)S(1)}, f32[64,128]{1,0:T(8,128)}, u32[]{:S(2)}) copy-start(f32[64,128]{1,0:T(8,128)} %constant.48.clone.ts_ref) | copy-start | bytes 98308
  0.0 38.8 %all-to-all-start = ((bf16[8,80,2048]{2,1,0:T(8,128)(2,1)}), bf16[8,80,2048]{2,1,0:T(8,128)(2,1)S(1)}, u32[]{:S(2)}, u32[]{:S(2)}) async-start(bf16[8,80,2048]{2,1,0:T(8,128)(2,1)} %bitcast.25), calls=%async_computation | async-start | bytes 5242880 | tf_op jit(solution)/shard_map/all_to_all | solution.py:820
  45.1 44.0 %copy-start.6 = (bf16[2,256,256]{2,1,0:T(8,128)(2,1)S(1)}, bf16[2,256,256]{2,1,0:T(8,128)(2,1)}, u32[]{:S(2)}) copy-start(bf16[2,256,256]{2,1,0:T(8,128)(2,1)} %constant.53.clone.w_ref) | copy-start | bytes 786436
  45.1 44.0 %copy-start.7 = (bf16[2,256,256]{2,1,0:T(8,128)(2,1)S(1)}, bf16[2,256,256]{2,1,0:T(8,128)(2,1)}, u32[]{:S(2)}) copy-start(bf16[2,256,256]{2,1,0:T(8,128)(2,1)} %constant.54.clone.v_ref) | copy-start | bytes 786436
  45.2 43.9 %copy-start.10 = (f32[80,128]{1,0:T(8,128)S(1)}, f32[80,128]{1,0:T(8,128)}, u32[]{:S(2)}) copy-start(f32[80,128]{1,0:T(8,128)} %constant.51.clone.tc_ref) | copy-start | bytes 122884
  45.2 43.9 %copy-start.11 = (f32[80,128]{1,0:T(8,128)S(1)}, f32[80,128]{1,0:T(8,128)}, u32[]{:S(2)}) copy-start(f32[80,128]{1,0:T(8,128)} %constant.52.clone.ts_ref) | copy-start | bytes 122884
  100.7 40.2 %copy-start.4 = (bf16[2,256,256]{2,1,0:T(8,128)(2,1)S(1)}, bf16[2,256,256]{2,1,0:T(8,128)(2,1)}, u32[]{:S(2)}) copy-start(bf16[2,256,256]{2,1,0:T(8,128)(2,1)} %constant.55.clone.w_ref) | copy-start | bytes 786436
  100.8 40.2 %copy-start.5 = (bf16[2,256,256]{2,1,0:T(8,128)(2,1)S(1)}, bf16[2,256,256]{2,1,0:T(8,128)(2,1)}, u32[]{:S(2)}) copy-start(bf16[2,256,256]{2,1,0:T(8,128)(2,1)} %constant.56.clone.w0_ref) | copy-start | bytes 786436
  144.8 23.5 %copy-start.1 = (bf16[8,80,896]{2,1,0:T(8,128)(2,1)}, bf16[8,80,896]{2,1,0:T(8,128)(2,1)S(1)}, u32[]{:S(2)}) copy-start(bf16[8,80,896]{2,1,0:T(8,128)(2,1)S(1)} %get-tuple-element.8.value_ref) | copy-start | bytes 3440644
  168.3 3.8 %copy-start = (bf16[8,80,1280]{2,1,0:T(8,128)(2,1)S(1)}, bf16[8,80,1280]{2,1,0:T(8,128)(2,1)}, u32[]{:S(2)}) copy-start(bf16[8,80,1280]{2,1,0:T(8,128)(2,1)} %all_to_all.27) | copy-start | bytes 4915204
  168.3 3.8 %copy-start.2 = (bf16[256,256]{1,0:T(8,128)(2,1)S(1)}, bf16[256,256]{1,0:T(8,128)(2,1)}, u32[]{:S(2)}) copy-start(bf16[256,256]{1,0:T(8,128)(2,1)} %constant.57.clone.refs_1_.refs_2_) | copy-start | bytes 393220
  168.3 3.8 %copy-start.3 = (bf16[256,256]{1,0:T(8,128)(2,1)S(1)}, bf16[256,256]{1,0:T(8,128)(2,1)}, u32[]{:S(2)}) copy-start(bf16[256,256]{1,0:T(8,128)(2,1)} %constant.58.clone.refs_2_.refs_3_) | copy-start | bytes 393220
  168.3 15.7 %all-to-all-start.4 = ((bf16[8,80,896]{2,1,0:T(8,128)(2,1)}), bf16[8,80,896]{2,1,0:T(8,128)(2,1)S(1)}, u32[]{:S(2)}, u32[]{:S(2)}) async-start(bf16[8,80,896]{2,1,0:T(8,128)(2,1)} %shard_map.193), calls=%async_computation.4 | async-start | bytes 2293760 | tf_op jit(solution)/shard_map/all_to_all | solution.py:833
  184.0 15.6 %collective-permute-start.1 = (bf16[16,2176]{1,0:T(8,128)(2,1)S(1)}, bf16[16,2176]{1,0:T(8,128)(2,1)S(1)}, u32[]{:S(2)}, u32[]{:S(2)}) collective-permute-start(bf16[16,2176]{1,0:T(8,128)(2,1)S(1)} %pad_maximum_fusion.2), channel_id=1, source_target_pairs={{8,0},{16,8},{24,16},{32,24},{40,32},{48,40},{56,48},{64,56},{72,6... | collective-permute-start | bytes 208904 | tf_op jit(solution)/shard_map/ppermute | solution.py:810
  190.7 8.9 %collective-permute-start = (bf16[16,2176]{1,0:T(8,128)(2,1)S(1)}, bf16[16,2176]{1,0:T(8,128)(2,1)S(1)}, u32[]{:S(2)}, u32[]{:S(2)}) collective-permute-start(bf16[16,2176]{1,0:T(8,128)(2,1)S(1)} %pad_maximum_fusion.1), channel_id=1, source_target_pairs={{0,8},{8,16},{16,24},{24,32},{32,40},{40,48},{48,56},{56,64},{64,7... | collective-permute-start | bytes 208904 | tf_op jit(solution)/shard_map/ppermute | solution.py:809

commit v5 on v4

--- a/solution.py
+++ b/solution.py
@@ -12,11 +12,13 @@
 
 NC = 10240
 NT = 16384
+ROWS = 80
 TF = 128
 R = 4
-ROWS = 80
 GROUP = 63
-NEAR = 1280
+SIDE = 9 * ROWS
+OUTER = SIDE + 16
+NEAR = OUTER + 7 * 16
 FAR = 896
 BF = jnp.bfloat16
 F32 = jnp.float32
@@ -233,7 +235,7 @@
 
 
 def forward_kernel(
-    x_ref, ok_ref, low_ref, high_ref, packed_ref, tc_ref, ts_ref, w_ref, w0_ref, out_ref,
+    place_ref, x_ref, ok_ref, low_ref, high_ref, packed_ref, tc_ref, ts_ref, w_ref, w0_ref, out_ref,
     stage, hi_ref, lo_ref
 ):
     def tile_body(tile, carry):
@@ -295,7 +297,9 @@
     lax.fori_loop(0, 63 // GROUP, wave_body, 0)
 
 
-def backward_kernel(in_ref, tc_ref, ts_ref, w_ref, w0_ref, near_ref, far_ref, stage, mid_ref):
+def backward_kernel(
+    place_ref, in_ref, tc_ref, ts_ref, w_ref, w0_ref, near_ref, far_ref, stage, mid_ref
+):
     def joined(slot):
         return jnp.concatenate([in_ref[2 * slot], in_ref[2 * slot + 1]], axis=1)
 
@@ -312,9 +316,11 @@
     lax.fori_loop(0, 63 // GROUP, wave_body, 0)
     lane = lax.broadcasted_iota(jnp.int32, (16, 128), 1)
 
-    def tile_body(tile, carry):
+    sides = [jnp.zeros((16, 128), F32) for _ in range(8)]
+    for tile in range(5):
+
         def get(slot):
-            base = pl.ds(pl.multiple_of(slot * ROWS + tile * 16, 16), 16)
+            base = pl.ds(slot * ROWS + tile * 16, 16)
             return mid_ref[base, :128], mid_ref[base, 128:]
 
         def twisted(slot):
@@ -336,7 +342,7 @@
                 re, im = spun(ys[a], a * q, 128, 1.0)
                 stage[a, 2 * q] = re
                 stage[a, 2 * q + 1] = im
-        rows = pl.ds(pl.multiple_of(tile * 16, 16), 16)
+        rows = pl.ds(tile * 16, 16)
 
         def series(a):
             parts = [(stage[a, 0], None)]
@@ -348,7 +354,7 @@
             ys = series(a)
             for s in range(8):
                 if a < 9:
-                    near_ref[s, rows, a * 128 + 128 : a * 128 + 256] = ys[s]
+                    near_ref[s, pl.ds(a * ROWS + tile * 16, 16), :] = ys[s]
                 else:
                     far_ref[s, rows, (a - 9) * 128 : (a - 8) * 128] = ys[s]
             if a in (0, 15):
@@ -357,12 +363,16 @@
         for s in range(8):
             after = ends[0][s + 1] if s < 7 else blank
             before = ends[15][s - 1] if s > 0 else blank
-            near_ref[s, rows, :128] = jnp.where(
-                lane < 64, after.astype(F32), before.astype(F32)
-            ).astype(BF)
-        return carry
-
-    lax.fori_loop(0, 5, tile_body, 0, unroll=5)
+            both = jnp.where(lane < 64, after.astype(F32), before.astype(F32))
+            here = ((lane - 16 * tile + 5) & 127) < 10
+            sides[s] = jnp.where(here, pltpu.roll(both, 16 * tile, 1), sides[s])
+    base = pl.multiple_of(jnp.where(place_ref[1] == 7, 64, 0), 16)
+    for s in range(8):
+        near_ref[s, pl.ds(SIDE, 16), :] = sides[s].astype(BF)
+        for n in range(7):
+            near_ref[s, pl.ds(OUTER + 16 * n, 16), :] = far_ref[
+                s, pl.ds(base, 16), n * 128 : (n + 1) * 128
+            ]
 
 
 STEP = 40
@@ -468,64 +478,6 @@
     lax.fori_loop(0, 128, store_body, 0, unroll=16)
 
 
-TILES = 18
-
-
-def spread(wide, start, block, count):
-    block = block.astype(F32)
-    rows = pl.ds(start, count)
-    for t in range(17):
-        wide[t, rows, :] = block[:, t * 128 : (t + 1) * 128]
-    wide[17, rows, :] = block[:, :128]
-
-
-def ahead(parts, count, lane):
-    turned = [pltpu.roll(v, (-count) % 128, 1) for v in parts]
-    out = []
-    for t in range(len(parts)):
-        if count > 0:
-            other = turned[t + 1] if t + 1 < len(parts) else turned[t]
-            out.append(jnp.where(lane < 128 - count, turned[t], other))
-        else:
-            other = turned[t - 1] if t > 0 else turned[t]
-            out.append(jnp.where(lane < -count, other, turned[t]))
-    return out
-
-
-def products(wide, start, first_keep, last_keep, row_keep, lane):
-    low = [wide[t, pl.ds(start, 8), :] for t in range(TILES)]
-    here = [wide[t, pl.ds(start + 1, 8), :] for t in range(TILES)]
-    high = [wide[t, pl.ds(start + 2, 8), :] for t in range(TILES)]
-    right = ahead(here, 1, lane)
-    left = ahead(here, -1, lane)
-    both = []
-    for t in range(TILES):
-        grad_time = right[t] - left[t]
-        masked = grad_time
-        if t == 0:
-            masked = jnp.where(first_keep, grad_time, 0.0)
-        if t == TILES - 1:
-            masked = jnp.where(last_keep, grad_time, 0.0)
-        if row_keep is not None:
-            masked = jnp.where(row_keep, masked, 0.0)
-        both.append(((high[t] - low[t]) * masked, grad_time * masked))
-    return both
-
-
-def quotient(cross, along, lane):
-    sums = []
-    for parts in (cross, along):
-        near, far = ahead(parts, 1, lane), ahead(parts, -1, lane)
-        three = [v + n + f for v, n, f in zip(parts, near, far)]
-        near, far = ahead(three, 3, lane), ahead(three, -3, lane)
-        sums.append([v + n + f for v, n, f in zip(three, near, far)][1:17])
-    scale = 1.0 / 324.0
-    out = []
-    for c, a in zip(*sums):
-        out.append((c * -scale) / (a * scale + 1e-05))
-    return jnp.concatenate(out, axis=1)
-
-
 def slide_tables():
     row = np.arange(256)[:, None]
     col = np.arange(128)[None, :]
@@ -542,144 +494,97 @@
 
 def tensor_kernel(half, place_ref, *refs):
     if half == 0:
-        near_ref, lanes_ref, nine_ref, out_ref, slope, level, prod, trio, both_ref = refs
+        near_ref, above_ref, below_ref, lanes_ref, nine_ref, out_ref = refs[:6]
+        slope, level, prod, trio, both_ref = refs[6:]
     else:
-        near_ref, far_ref, lanes_ref, nine_ref, _, out_ref = refs[:6]
-        slope, level, prod, trio, both_ref = refs[6:]
+        near_ref, above_ref, below_ref, far_ref, lanes_ref, nine_ref, _, out_ref = refs[:8]
+        slope, level, prod, trio, both_ref = refs[8:]
     lane = lax.broadcasted_iota(jnp.int32, (8, 128), 1)
+    sub = lax.broadcasted_iota(jnp.int32, (8, 128), 0)
     step = pl.program_id(0)
-    part = place_ref[1]
-
-    def lanes(t, cells):
-        res = dot(cells, lanes_ref[...])
-        slope[t, 16:656, :] = res[:, :128]
-        level[t, 16:656, :] = res[:, 128:]
-
-    def cut(ref, t):
-        return ref[:, pl.ds(pl.multiple_of(t * 128, 128), 256)]
+    chan, part = place_ref[0], place_ref[1]
+
+    def column(t):
+        if t in (-1, 16):
+            parts = [pltpu.roll(above_ref[pl.ds(144, 16), :].astype(F32), 64, 1).astype(BF)]
+            for j in range(8):
+                side = near_ref[j, pl.ds(SIDE, 16), :].astype(F32)
+                parts.append(side.astype(BF))
+                for n in range(1, 5):
+                    parts.append(pltpu.roll(side, 128 - 16 * n, 1).astype(BF))
+            return jnp.concatenate(parts + [below_ref[pl.ds(144, 16), :]], axis=0)
+        rows = pl.ds(16 * t if t < 9 else 160 + 16 * (t - 9), 16)
+        if t < 9:
+            inner = [near_ref[j, pl.ds(t * ROWS, ROWS), :] for j in range(8)]
+        else:
+            inner = [far_ref[:, (t - 9) * 128 : (t - 8) * 128]]
+        return jnp.concatenate([above_ref[rows, :]] + inner + [below_ref[rows, :]], axis=0)
 
     @pl.when(step == 0)
     def _():
-        if half == 0:
-
-            def lanes_body(t, carry):
-                lanes(t, cut(near_ref, t))
-                return carry
-
-            lax.fori_loop(0, PER, lanes_body, 0, unroll=PER)
-        else:
-
-            def lanes_body(t, carry):
-                lanes(t + 2, cut(far_ref, t))
-                return carry
-
-            lanes(0, near_ref[:, 1024:])
-            lanes(1, jnp.concatenate([near_ref[:, 1152:], far_ref[:, :128]], axis=1))
-            lax.fori_loop(0, PER - 3, lanes_body, 0, unroll=PER - 3)
-            lanes(8, jnp.concatenate([far_ref[:, 768:], near_ref[:, :128]], axis=1))
-
-    top = step * BAND
-
-    def prod_body(k, carry):
-        start = pl.multiple_of(k * 8, 8)
+        left = column(8 * half - 1)
+        for t in range(PER):
+            right = column(8 * half + t)
+            res = dot(jnp.concatenate([left, right], axis=1), lanes_ref[...])
+            slope[t] = res[:, :128]
+            level[t] = res[:, 128:]
+            left = right
+
+    top = pl.multiple_of(step * BAND, BAND)
+    for k in range(BAND // 8 + 2):
         base = pl.multiple_of(top + k * 8, 8)
         for t in range(PER):
             grad_time = slope[t, pl.ds(base + 12, 8), :]
             masked = grad_time
             if half == 0 and t == 0:
-                masked = jnp.where((lane >= 4) | (part > 0), grad_time, 0.0)
+                masked = jnp.where((lane >= 4) | (part > 0), masked, 0.0)
             if half == 1 and t == PER - 1:
-                masked = jnp.where((lane < 4) | (part < 7), grad_time, 0.0)
+                masked = jnp.where((lane < 4) | (part < 7), masked, 0.0)
+            if k == 0:
+                masked = jnp.where((sub >= 4) | (chan > 0) | (step > 0), masked, 0.0)
+            if k == BAND // 8:
+                masked = jnp.where((sub < 4) | (chan < 15) | (step < 640 // BAND - 1), masked, 0.0)
             grad_chan = level[t, pl.ds(base + 13, 8), :] - level[t, pl.ds(base + 11, 8), :]
-            prod[0, t, pl.ds(start, 8), :] = grad_chan * masked
-            prod[1, t, pl.ds(start, 8), :] = grad_time * masked
-        return carry
-
-    lax.fori_loop(0, BAND // 8 + 2, prod_body, 0, unroll=BAND // 8 + 2)
-
-    def trio_body(k, carry):
-        start = pl.multiple_of(k * 8, 8)
+            prod[0, t, pl.ds(k * 8, 8), :] = grad_chan * masked
+            prod[1, t, pl.ds(k * 8, 8), :] = grad_time * masked
+    for k in range(BAND // 8 + 1):
         for n in range(2):
             for t in range(PER):
-                trio[n, t, pl.ds(start, 8), :] = (
-                    prod[n, t, pl.ds(start, 8), :]
-                    + prod[n, t, pl.ds(start + 1, 8), :]
-                    + prod[n, t, pl.ds(start + 2, 8), :]
+                trio[n, t, pl.ds(k * 8, 8), :] = (
+                    prod[n, t, pl.ds(k * 8, 8), :]
+                    + prod[n, t, pl.ds(k * 8 + 1, 8), :]
+                    + prod[n, t, pl.ds(k * 8 + 2, 8), :]
                 )
-        return carry
-
-    lax.fori_loop(0, BAND // 8 + 1, trio_body, 0, unroll=BAND // 8 + 1)
-
-    def split_body(k, carry):
-        start = pl.multiple_of(k * 16, 16)
+    for k in range(BAND // 16):
         for n in range(2):
             for t in range(PER):
                 total = (
-                    trio[n, t, pl.ds(start, 16), :]
-                    + trio[n, t, pl.ds(start + 3, 16), :]
-                    + trio[n, t, pl.ds(start + 6, 16), :]
+                    trio[n, t, pl.ds(k * 16, 16), :]
+                    + trio[n, t, pl.ds(k * 16 + 3, 16), :]
+                    + trio[n, t, pl.ds(k * 16 + 6, 16), :]
                 )
                 high, low = parted(total)
-                both_ref[n, t, pl.ds(start, 16), :128] = high
-                both_ref[n, t, pl.ds(start, 16), 128:] = low
-        return carry
-
-    lax.fori_loop(0, BAND // 16, split_body, 0, unroll=BAND // 16)
+                both_ref[n, t, pl.ds(k * 16, 16), :128] = high
+                both_ref[n, t, pl.ds(k * 16, 16), 128:] = low
     nine = nine_ref[...]
     scale = 1.0 / 324.0
-
-    def sum_body(g, carry):
+    for g in range(2):
         sums = []
         for n in range(2):
             res = dot(both_ref[n, pl.ds(g * 4, 5)].reshape(5 * BAND, 256), nine)
             sums.append(res[: 4 * BAND, :128] + res[BAND:, 128:])
         res = (sums[0] * -scale) / (sums[1] * scale + 1e-05)
         for t in range(4):
-            cols = pl.ds(pl.multiple_of(g * 512 + t * 128, 128), 128)
+            cols = slice(g * 512 + t * 128, g * 512 + t * 128 + 128)
             out_ref[:, cols] = res[t * BAND : (t + 1) * BAND]
-        return carry
-
-    lax.fori_loop(0, 2, sum_body, 0, unroll=2)
-
-
-def edge_kernel(place_ref, old_ref, rows_ref, out_ref, wide, prod):
-    lane = lax.broadcasted_iota(jnp.int32, (8, 128), 1)
-    sub = lax.broadcasted_iota(jnp.int32, (8, 128), 0)
-    step = pl.program_id(0)
-    chan, part = place_ref[0], place_ref[1]
-    for k in range(2):
-        rows = pl.ds(k * 16, 16)
-        spread(wide, k * 16, rows_ref[0, rows, :], 16)
-    open_low = (step == 0) & (chan == 0)
-    open_high = (step == 1) & (chan == 15)
-    skip = 8 - step * 8
-    for k in range(2):
-        row = sub + (k * 8 + skip + 4)
-        row_keep = ((row >= 16) | jnp.logical_not(open_low)) & (
-            (row < 16) | jnp.logical_not(open_high)
-        )
-        both = products(wide, k * 8 + skip + 3, part > 0, part < 7, row_keep, lane)
-        for t in range(TILES):
-            prod[0, t, pl.ds(k * 8, 8), :] = both[t][0]
-            prod[1, t, pl.ds(k * 8, 8), :] = both[t][1]
-    sums = []
-    for n in range(2):
-        parts = []
-        for t in range(TILES):
-            total = prod[n, t, pl.ds(0, 8), :]
-            for d in range(1, 9):
-                total = total + prod[n, t, pl.ds(d, 8), :]
-            parts.append(total)
-        sums.append(parts)
-    out_ref[...] = quotient(sums[0], sums[1], lane)
-
-
-def call(kernel, out, specs, scratch, flops, *args):
+
+
+def call(kernel, out, specs, scratch, flops, *args, smem=0):
     nbytes = sum(a.size * a.dtype.itemsize for a in args) + 3 * 2**20
     return pl.pallas_call(
         kernel,
         out_shape=out,
-        in_specs=[VMEM] * len(args),
+        in_specs=[SMEM] * smem + [VMEM] * (len(args) - smem),
         out_specs=specs,
         scratch_shapes=scratch,
         compiler_params=pltpu.CompilerParams(vmem_limit_bytes=48 * 2**20),
@@ -695,7 +600,7 @@
     return jnp.asarray(table.astype(np.float32))
 
 
-def forward(series, good, low, high, packed):
+def forward(place, series, good, low, high, packed):
     fwd, _, first, _, tc, ts = time_tables()
     scratch = [
         pltpu.VMEM((16, 8, 16, 128), F32),
@@ -704,15 +609,31 @@
     ]
     out = jax.ShapeDtypeStruct((128, ROWS, 128), BF)
     tables = single(tc), single(ts), pair(fwd), pair(first)
-    return call(forward_kernel, out, VMEM, scratch, 4 * 10**9, series, good, low, high, packed, *tables)
-
-
-def backward(spectra):
+    return call(
+        forward_kernel,
+        out,
+        VMEM,
+        scratch,
+        4 * 10**9,
+        place,
+        series,
+        good,
+        low,
+        high,
+        packed,
+        *tables,
+        smem=1,
+    )
+
+
+def backward(place, spectra):
     _, bwd, _, last, tc, ts = time_tables()
     scratch = [pltpu.VMEM((16, 8, 16, 128), F32), pltpu.VMEM((64 * ROWS, 256), F32)]
-    out = [jax.ShapeDtypeStruct((8, ROWS, n), BF) for n in (NEAR, FAR)]
+    out = [jax.ShapeDtypeStruct(s, BF) for s in ((8, NEAR, 128), (8, ROWS, FAR))]
     tables = single(tc), single(ts), pair(bwd), pair(last)
-    return call(backward_kernel, out, [VMEM, VMEM], scratch, 4 * 10**9, spectra, *tables)
+    return call(
+        backward_kernel, out, [VMEM, VMEM], scratch, 4 * 10**9, place, spectra, *tables, smem=1
+    )
 
 
 def channels(pencil, low, high, packed):
@@ -729,7 +650,7 @@
     return call(channel_kernel, out, VMEM, scratch, 8 * 10**9, pencil, low, high, packed, *tables)
 
 
-def tensor(half, place, near, far=None, whole=None):
+def tensor(half, place, near, above, below, far=None, whole=None):
     lanes, nine = (jnp.asarray(t.astype(ml_dtypes.bfloat16)) for t in slide_tables())
     scratch = [
         pltpu.VMEM((PER, 672, 128), F32),
@@ -739,11 +660,11 @@
         pltpu.VMEM((2, PER, BAND, 256), BF),
     ]
     if half == 0:
-        args, specs, alias = (place, near, lanes, nine), [SMEM] + [VMEM] * 3, {}
+        args = (place, near, above, below, lanes, nine)
+        specs, alias = [SMEM] + [VMEM] * 5, {}
     else:
-        args = (place, near, far, lanes, nine, whole)
-        specs = [SMEM] + [VMEM] * 4 + [pl.BlockSpec(memory_space=pl.ANY)]
-        alias = {5: 0}
+        args = (place, near, above, below, far, lanes, nine, whole)
+        specs, alias = [SMEM] + [VMEM] * 6 + [ANY], {7: 0}
     return pl.pallas_call(
         functools.partial(tensor_kernel, half),
         grid=(640 // BAND,),
@@ -757,25 +678,6 @@
     )(*args)
 
 
-def edges(place, whole, rows):
-    scratch = [pltpu.VMEM((TILES, 32, 128), F32), pltpu.VMEM((2, TILES, 16, 128), F32)]
-    return pl.pallas_call(
-        edge_kernel,
-        grid=(2,),
-        out_shape=jax.ShapeDtypeStruct((640, 2048), F32),
-        in_specs=[
-            SMEM,
-            pl.BlockSpec(memory_space=pl.ANY),
-            pl.BlockSpec((1, 32, NEAR + FAR), lambda g: (g, 0, 0)),
-        ],
-        out_specs=pl.BlockSpec((8, 2048), lambda g: (79 * g, 0)),
-        scratch_shapes=scratch,
-        input_output_aliases={1: 0},
-        compiler_params=pltpu.CompilerParams(vmem_limit_bytes=16 * 2**20),
-        cost_estimate=pl.CostEstimate(flops=10**7, bytes_accessed=2**19, transcendentals=0),
-    )(place, whole, rows)
-
-
 def window_bounds(fan_bounds, block):
     column = []
     for slot, k in enumerate(WAVES):
@@ -803,14 +705,11 @@
     )(value, sign)
 
 
-def trimmed(near, far):
-    top = jnp.concatenate([near[:16], far[:16]], axis=1)
-    bottom = jnp.concatenate([near[624:], far[624:]], axis=1)
-    above = lax.ppermute(bottom, "chan", [(i, i + 1) for i in range(15)])
-    below = lax.ppermute(top, "chan", [(i + 1, i) for i in range(15)])
-    return jnp.stack(
-        [jnp.concatenate([above, top], axis=0), jnp.concatenate([bottom, below], axis=0)]
-    )
+def outer_kernel(near_ref, top_ref, bottom_ref):
+    for ref, source, first in ((top_ref, 0, 0), (bottom_ref, 7, 64)):
+        for t in range(9):
+            ref[pl.ds(16 * t, 16), :] = near_ref[source, pl.ds(t * ROWS + first, 16), :]
+        ref[pl.ds(144, 128), :] = near_ref[source, pl.ds(SIDE, 128), :]
 
 
 def per_device(record, channel_ok, fan_bounds):
@@ -823,17 +722,20 @@
     low, high = window_bounds(fan_bounds, block)
     corner = lax.broadcasted_iota(jnp.int32, (8, 128), 0) == 0
     packed = (corner & (block == 0)).astype(F32)
-    spectra = forward(series, good, low, high, packed)
+    spectra = forward(place, series, good, low, high, packed)
     pencil = lax.all_to_all(spectra, ("chan", "tm"), 0, 0, tiled=True)
     passed = channels(pencil, low, high, packed)
     back = lax.all_to_all(passed, ("chan", "tm"), 0, 0, tiled=True)
-    near, far = backward(back)
-    near = lax.all_to_all(near, "tm", 0, 0, tiled=True).reshape(640, NEAR)
-    whole = tensor(0, place, near)
+    near, far = backward(place, back)
+    near = lax.all_to_all(near, "tm", 0, 0, tiled=True)
+    down = [(i, i + 1) for i in range(15)]
+    outer = jax.ShapeDtypeStruct((272, 128), BF)
+    top, bottom = call(outer_kernel, [outer, outer], [VMEM, VMEM], [], 10**6, near)
+    above = lax.ppermute(bottom, "chan", down)
+    below = lax.ppermute(top, "chan", [(b, a) for a, b in down])
+    whole = tensor(0, place, near, above, below)
     far = lax.all_to_all(after(far, near), "tm", 0, 0, tiled=True).reshape(640, FAR)
-    rows = trimmed(near, far)
-    whole = tensor(1, place, near, far, whole)
-    return edges(place, whole, rows)
+    return tensor(1, place, near, above, below, far, whole)
 
 
 def solution(mesh):

time: 203 us -> 202 us (level)
  waiting for transfers between devices: 33.7 us -> 36.1 us
    ppermute x2, waiting for transfers between devices: 0.01 us -> 8.17 us  [the longest x1 4.31 us: per_device(): below = lax.ppermute(top, 'chan', [(b, a) for a, b in down])]
    all_to_all x1, waiting for transfers between devices: 5.67 us -> 0.01 us  [per_device(): lax.all_to_all(after(far, near), 'tm', 0, 0, tiled=True).reshape(640, FAR)]
  transfers between devices with their start and end apart: 4 -> 4, of which waited for: 2 -> 3; matrix products, arithmetic and copies ran while one was open for 1% -> 1% of each run, Pallas kernels for 6% -> 3%
where the time goes in v5:
time: 202 us
  blocking collectives  108 us (53%)
  waiting for transfers between devices  36.1 us (18%)
  Pallas kernels  35.1 us (17%)
  starting transfers between devices  18.2 us (9%)
  between operations  2.11 us (1%)
    all_to_all x1, blocking collectives, per_device(): pencil = lax.all_to_all(spectra, ('chan', 'tm'), 0, 0, tiled=True)  43.9 us
    all_to_all x1, blocking collectives, per_device(): back = lax.all_to_all(passed, ('chan', 'tm'), 0, 0, tiled=True)  40.2 us
    all_to_all x1, waiting for transfers between devices, per_device(): lax.all_to_all(record.reshape(8, ROWS, 2048), 'tm', 0, 0, tiled=True)  27.9 us
    all_to_all x1, blocking collectives, per_device(): near = lax.all_to_all(near, 'tm', 0, 0, tiled=True)  24.1 us
    pallas_call x4, Pallas kernels, call(): pl.pallas_call(kernel, out_shape=out, in_specs=[SMEM] * smem + [VMEM] * (...  22.6 us
    pallas_call x2, Pallas kernels, tensor(): pl.pallas_call(functools.partial(tensor_kernel, half), grid=(640 // BAND,...  12.5 us
    all_to_all x1, starting transfers between devices, per_device(): lax.all_to_all(record.reshape(8, ROWS, 2048), 'tm', 0, 0, tiled=True)  7.02 us
    ppermute x1, starting transfers between devices, per_device(): above = lax.ppermute(bottom, 'chan', down)  5.53 us
  transfers between devices with their start and end apart: 4, of which 3 were waited for; matrix products, arithmetic and copies ran while one was open for 1% of the time, Pallas kernels for 3%

profile of v5, /device:TPU:1, one launch (start us, length us, event | category | flops | bytes accessed | tf_op | source)
XLA Modules:
  0.0 202.0 jit_solution(17476350565999509195)
XLA Ops:
  0.0 0.0 copy-start.9
  0.0 0.0 copy-start.12
  0.0 0.0 copy-start.13
  0.0 7.0 %all-to-all-start = ((bf16[8,80,2048]{2,1,0:T(8,128)(2,1)}), bf16[8,80,2048]{2,1,0:T(8,128)(2,1)S(1)}, u32[]{:S(2)}, u32[]{:S(2)}) async-start(bf16[8,80,2048]{2,1,0:T(8,128)(2,1)} %bitcast.15), calls=%async_computation | async-start | bytes 5242880 | tf_op jit(solution)/shard_map/all_to_all | solution.py:719
  7.1 0.0 copy-done.15
  7.1 0.7 dynamic_slice.10
  9.0 0.0 copy-done.14
  9.6 0.1 constant_dynamic-slice_fusion
  9.7 0.1 copy.24
  9.8 0.1 pad_add_fusion.1.place_ref
  9.9 0.8 dynamic-slice_convert_fusion
  10.7 0.1 slice_reduce_fusion
  10.8 0.1 broadcast_in_dim.26
  10.8 0.1 fusion.2
  10.9 27.9 %all-to-all-done.x_ref = bf16[8,80,2048]{2,1,0:T(8,128)(2,1)S(1)} async-done(((bf16[8,80,2048]{2,1,0:T(8,128)(2,1)}), bf16[8,80,2048]{2,1,0:T(8,128)(2,1)S(1)}, u32[]{:S(2)}, u32[]{:S(2)}) %all-to-all-start) | async-done | bytes 2621472 | tf_op jit(solution)/shard_map/all_to_all | solution.py:719
  38.8 0.1 iota.7.packed_ref.first_ref
  38.9 0.1 broadcast_in_dim.24.ok_ref
  39.0 0.1 broadcast_in_dim.30.high_ref
  39.0 0.1 broadcast_in_dim.28.low_ref
  39.1 0.0 copy-done.8
  39.1 0.0 copy-done.9
  39.1 0.0 copy-done.12
  39.1 0.0 copy-done.13
  39.2 6.5 %shard_map.190 = bf16[128,80,128]{2,1,0:T(8,128)(2,1)S(1)} custom-call(s32[2]{0:T(128)S(1)} %pad_add_fusion.1.place_ref, bf16[8,80,2048]{2,1,0:T(8,128)(2,1)S(1)} %all-to-all-done.x_ref, f32[80,128]{1,0:T(8,128)S(1)} %broadcast_in_dim.24.ok_ref, s32[72,128]{1,0:T(8,128)S(1)} %broadcast_in_dim.28.low_ref, s32[72,128]{1,0:T(8,128)S(1)} %broadcast_in_dim.30.high_ref, ...), custom_call_target="tpu_custom_call" | custom-call | flops 4000000000 | bytes 6475784 | tf_op jit(solution)/shard_map/pallas_call | solution.py:584
  45.7 0.0 copy-start.6
  45.7 0.0 copy-start.7
  45.7 0.0 copy-start.10
  45.7 0.0 copy-start.11
  45.7 43.9 %all_to_all.25.in_ref = bf16[128,80,128]{2,1,0:T(8,128)(2,1)S(1)} all-to-all(bf16[128,80,128]{2,1,0:T(8,128)(2,1)S(1)} %shard_map.190), channel_id=1, replica_groups=mesh['chan'=16,'tm'=8] {'chan','tm'}, dimensions={0} | all-to-all | bytes 5242880 | tf_op jit(solution)/shard_map/all_to_all | solution.py:726
  89.6 0.0 copy-done.6
  89.6 0.0 copy-done.7
  89.7 0.0 copy-done.10
  89.7 11.6 %shard_map.191 = bf16[128,80,128]{2,1,0:T(8,128)(2,1)S(1)} custom-call(bf16[128,80,128]{2,1,0:T(8,128)(2,1)S(1)} %all_to_all.25.in_ref, s32[72,128]{1,0:T(8,128)S(1)} %broadcast_in_dim.28.low_ref, s32[72,128]{1,0:T(8,128)S(1)} %broadcast_in_dim.30.high_ref, f32[8,128]{1,0:T(8,128)S(1)} %iota.7.packed_ref.first_ref, f32[80,128]{1,0:T(8,128)S(1)} %copy-done.11, ...), custom_call_target="tpu_custom_call" | custom-call | flops 8000000000 | bytes 6451200 | tf_op jit(solution)/shard_map/pallas_call | solution.py:584
  101.3 0.0 copy-start.4
  101.3 0.0 copy-start.5
  101.3 40.2 %all_to_all.26.in_ref = bf16[128,80,128]{2,1,0:T(8,128)(2,1)S(1)} all-to-all(bf16[128,80,128]{2,1,0:T(8,128)(2,1)S(1)} %shard_map.191), channel_id=1, replica_groups=mesh['chan'=16,'tm'=8] {'chan','tm'}, dimensions={0} | all-to-all | bytes 5242880 | tf_op jit(solution)/shard_map/all_to_all | solution.py:728
  141.5 0.0 copy-done.5
  141.5 4.4 %shard_map.192 = (bf16[8,848,128]{2,1,0:T(8,128)(2,1)S(1)}, bf16[8,80,896]{2,1,0:T(8,128)(2,1)S(1)}) custom-call(s32[2]{0:T(128)S(1)} %pad_add_fusion.1.place_ref, bf16[128,80,128]{2,1,0:T(8,128)(2,1)S(1)} %all_to_all.26.in_ref, f32[64,128]{1,0:T(8,128)S(1)} %copy-done.13, f32[64,128]{1,0:T(8,128)S(1)} %copy-done.12, bf16[2,256,256]{2,1,0:T(8,128)(2,1)S(1)} %copy-done.5, ...), custom_call_target="tpu_custom_call" | custom-call | flops 4000000000 | bytes 6357000 | tf_op jit(solution)/shard_map/pallas_call | solution.py:584
  145.9 24.1 %all_to_all.27.near_ref.sign_ref.refs_0_ = bf16[8,848,128]{2,1,0:T(8,128)(2,1)} all-to-all(bf16[8,848,128]{2,1,0:T(8,128)(2,1)S(1)} %get-tuple-element.9), channel_id=1, replica_groups=mesh['chan'=16,'tm'=8] {'tm'}, dimensions={0} | all-to-all | bytes 3473408 | tf_op jit(solution)/shard_map/all_to_all | solution.py:730
  170.1 0.0 copy-start.3
  170.1 3.7 %all-to-all-start.4 = ((bf16[8,80,896]{2,1,0:T(8,128)(2,1)}), bf16[8,80,896]{2,1,0:T(8,128)(2,1)S(1)}, u32[]{:S(2)}, u32[]{:S(2)}) async-start(bf16[8,80,896]{2,1,0:T(8,128)(2,1)} %shard_map.194), calls=%async_computation.4 | async-start | bytes 2293760 | tf_op jit(solution)/shard_map/all_to_all | solution.py:737
  173.8 5.5 %collective-permute-start = (bf16[272,128]{1,0:T(8,128)(2,1)S(1)}, bf16[272,128]{1,0:T(8,128)(2,1)S(1)}, u32[]{:S(2)}, u32[]{:S(2)}) collective-permute-start(bf16[272,128]{1,0:T(8,128)(2,1)S(1)} %get-tuple-element.10), channel_id=1, source_target_pairs={{0,8},{8,16},{16,24},{24,32},{32,40},{40,48},{48,56},{56,64},{64,7... | collective-permute-start | bytes 208904 | tf_op jit(solution)/shard_map/ppermute | solution.py:734
  179.4 1.9 collective-permute-start.1
  181.3 3.9 %collective-permute-done.refs_1_ = bf16[272,128]{1,0:T(8,128)(2,1)S(1)} collective-permute-done((bf16[272,128]{1,0:T(8,128)(2,1)S(1)}, bf16[272,128]{1,0:T(8,128)(2,1)S(1)}, u32[]{:S(2)}, u32[]{:S(2)}) %collective-permute-start) | collective-permute-done | bytes 69664 | tf_op jit(solution)/shard_map/ppermute | solution.py:734
  185.2 4.3 %collective-permute-done.1.refs_2_ = bf16[272,128]{1,0:T(8,128)(2,1)S(1)} collective-permute-done((bf16[272,128]{1,0:T(8,128)(2,1)S(1)}, bf16[272,128]{1,0:T(8,128)(2,1)S(1)}, u32[]{:S(2)}, u32[]{:S(2)}) %collective-permute-start.1) | collective-permute-done | bytes 69664 | tf_op jit(solution)/shard_map/ppermute | solution.py:735
  189.5 6.3 %shard_map.195.refs_6_ = f32[640,2048]{1,0:T(8,128)} custom-call(s32[2]{0:T(128)S(1)} %pad_add_fusion.1.place_ref, bf16[8,848,128]{2,1,0:T(8,128)(2,1)S(1)} %copy-done, bf16[272,128]{1,0:T(8,128)(2,1)S(1)} %collective-permute-done.refs_1_, bf16[272,128]{1,0:T(8,128)(2,1)S(1)} %collective-permute-done.1.refs_2_, bf16[256,256]{1,0:T(8,128)(2,1)S(1)} %copy-done.3, ...), custom_call_target="tpu_custom_call" | custom-call | flops 1000000000 | bytes 9437184 | tf_op jit(solution)/shard_map/pallas_call | solution.py:668
  195.8 0.0 all-to-all-done.4
  195.8 6.2 %shard_map.196 = f32[640,2048]{1,0:T(8,128)} custom-call(s32[2]{0:T(128)S(1)} %pad_add_fusion.1.place_ref, bf16[8,848,128]{2,1,0:T(8,128)(2,1)S(1)} %copy-done, bf16[272,128]{1,0:T(8,128)(2,1)S(1)} %collective-permute-done.refs_1_, bf16[272,128]{1,0:T(8,128)(2,1)S(1)} %collective-permute-done.1.refs_2_, ...), custom_call_target="tpu_custom_call", output_to_operand_aliasing={{}: (7, {})} | custom-call | flops 1000000000 | bytes 9437184 | tf_op jit(solution)/shard_map/pallas_call | solution.py:668
  (17 shorter events, 0.1 us)
Async XLA Ops:
  0.0 7.1 %copy-start.15 = (s32[128]{0:T(128)S(1)}, s32[128]{0:T(128)}, u32[]{:S(2)}) copy-start(s32[128]{0:T(128)} %constant.46.clone) | copy-start | bytes 1540
  0.0 9.0 %copy-start.14 = (s32[2,8193]{1,0:T(2,128)S(1)}, s32[2,8193]{1,0:T(2,128)}, u32[]{:S(2)}) copy-start(s32[2,8193]{1,0:T(2,128)} %param.22) | copy-start | bytes 196636
  0.0 39.1 %copy-start.8 = (bf16[2,256,256]{2,1,0:T(8,128)(2,1)S(1)}, bf16[2,256,256]{2,1,0:T(8,128)(2,1)}, u32[]{:S(2)}) copy-start(bf16[2,256,256]{2,1,0:T(8,128)(2,1)} %constant.50.clone.w0_ref) | copy-start | bytes 786436
  0.0 39.1 %copy-start.9 = (bf16[2,256,256]{2,1,0:T(8,128)(2,1)S(1)}, bf16[2,256,256]{2,1,0:T(8,128)(2,1)}, u32[]{:S(2)}) copy-start(bf16[2,256,256]{2,1,0:T(8,128)(2,1)} %constant.49.clone.w_ref) | copy-start | bytes 786436
  0.0 39.1 %copy-start.12 = (f32[64,128]{1,0:T(8,128)S(1)}, f32[64,128]{1,0:T(8,128)}, u32[]{:S(2)}) copy-start(f32[64,128]{1,0:T(8,128)} %constant.48.clone.ts_ref) | copy-start | bytes 98308
  0.0 39.1 %copy-start.13 = (f32[64,128]{1,0:T(8,128)S(1)}, f32[64,128]{1,0:T(8,128)}, u32[]{:S(2)}) copy-start(f32[64,128]{1,0:T(8,128)} %constant.47.clone.tc_ref) | copy-start | bytes 98308
  0.0 38.8 %all-to-all-start = ((bf16[8,80,2048]{2,1,0:T(8,128)(2,1)}), bf16[8,80,2048]{2,1,0:T(8,128)(2,1)S(1)}, u32[]{:S(2)}, u32[]{:S(2)}) async-start(bf16[8,80,2048]{2,1,0:T(8,128)(2,1)} %bitcast.15), calls=%async_computation | async-start | bytes 5242880 | tf_op jit(solution)/shard_map/all_to_all | solution.py:719
  45.7 44.0 %copy-start.6 = (bf16[2,256,256]{2,1,0:T(8,128)(2,1)S(1)}, bf16[2,256,256]{2,1,0:T(8,128)(2,1)}, u32[]{:S(2)}) copy-start(bf16[2,256,256]{2,1,0:T(8,128)(2,1)} %constant.54.clone.v_ref) | copy-start | bytes 786436
  45.7 44.0 %copy-start.7 = (bf16[2,256,256]{2,1,0:T(8,128)(2,1)S(1)}, bf16[2,256,256]{2,1,0:T(8,128)(2,1)}, u32[]{:S(2)}) copy-start(bf16[2,256,256]{2,1,0:T(8,128)(2,1)} %constant.53.clone.w_ref) | copy-start | bytes 786436
  45.7 43.9 %copy-start.10 = (f32[80,128]{1,0:T(8,128)S(1)}, f32[80,128]{1,0:T(8,128)}, u32[]{:S(2)}) copy-start(f32[80,128]{1,0:T(8,128)} %constant.52.clone.ts_ref) | copy-start | bytes 122884
  45.7 43.9 %copy-start.11 = (f32[80,128]{1,0:T(8,128)S(1)}, f32[80,128]{1,0:T(8,128)}, u32[]{:S(2)}) copy-start(f32[80,128]{1,0:T(8,128)} %constant.51.clone.tc_ref) | copy-start | bytes 122884
  101.3 40.2 %copy-start.4 = (bf16[2,256,256]{2,1,0:T(8,128)(2,1)S(1)}, bf16[2,256,256]{2,1,0:T(8,128)(2,1)}, u32[]{:S(2)}) copy-start(bf16[2,256,256]{2,1,0:T(8,128)(2,1)} %constant.56.clone.w0_ref) | copy-start | bytes 786436
  101.3 40.2 %copy-start.5 = (bf16[2,256,256]{2,1,0:T(8,128)(2,1)S(1)}, bf16[2,256,256]{2,1,0:T(8,128)(2,1)}, u32[]{:S(2)}) copy-start(bf16[2,256,256]{2,1,0:T(8,128)(2,1)} %constant.55.clone.w_ref) | copy-start | bytes 786436
  145.9 24.1 %copy-start.1 = (bf16[8,80,896]{2,1,0:T(8,128)(2,1)}, bf16[8,80,896]{2,1,0:T(8,128)(2,1)S(1)}, u32[]{:S(2)}) copy-start(bf16[8,80,896]{2,1,0:T(8,128)(2,1)S(1)} %get-tuple-element.12.value_ref) | copy-start | bytes 3440644
  170.1 3.7 %copy-start = (bf16[8,848,128]{2,1,0:T(8,128)(2,1)S(1)}, bf16[8,848,128]{2,1,0:T(8,128)(2,1)}, u32[]{:S(2)}) copy-start(bf16[8,848,128]{2,1,0:T(8,128)(2,1)} %all_to_all.27.near_ref.sign_ref.refs_0_) | copy-start | bytes 5210116
  170.1 19.4 %copy-start.2 = (bf16[256,256]{1,0:T(8,128)(2,1)S(1)}, bf16[256,256]{1,0:T(8,128)(2,1)}, u32[]{:S(2)}) copy-start(bf16[256,256]{1,0:T(8,128)(2,1)} %constant.58.clone.refs_4_.refs_5_) | copy-start | bytes 393220
  170.1 19.4 %copy-start.3 = (bf16[256,256]{1,0:T(8,128)(2,1)S(1)}, bf16[256,256]{1,0:T(8,128)(2,1)}, u32[]{:S(2)}) copy-start(bf16[256,256]{1,0:T(8,128)(2,1)} %constant.57.clone.refs_3_.refs_4_) | copy-start | bytes 393220
  170.1 25.7 %all-to-all-start.4 = ((bf16[8,80,896]{2,1,0:T(8,128)(2,1)}), bf16[8,80,896]{2,1,0:T(8,128)(2,1)S(1)}, u32[]{:S(2)}, u32[]{:S(2)}) async-start(bf16[8,80,896]{2,1,0:T(8,128)(2,1)} %shard_map.194), calls=%async_computation.4 | async-start | bytes 2293760 | tf_op jit(solution)/shard_map/all_to_all | solution.py:737
  173.8 11.3 %collective-permute-start = (bf16[272,128]{1,0:T(8,128)(2,1)S(1)}, bf16[272,128]{1,0:T(8,128)(2,1)S(1)}, u32[]{:S(2)}, u32[]{:S(2)}) collective-permute-start(bf16[272,128]{1,0:T(8,128)(2,1)S(1)} %get-tuple-element.10), channel_id=1, source_target_pairs={{0,8},{8,16},{16,24},{24,32},{32,40},{40,48},{48,56},{56,64},{64,7... | collective-permute-start | bytes 208904 | tf_op jit(solution)/shard_map/ppermute | solution.py:734
  179.4 10.1 %collective-permute-start.1 = (bf16[272,128]{1,0:T(8,128)(2,1)S(1)}, bf16[272,128]{1,0:T(8,128)(2,1)S(1)}, u32[]{:S(2)}, u32[]{:S(2)}) collective-permute-start(bf16[272,128]{1,0:T(8,128)(2,1)S(1)} %get-tuple-element.11), channel_id=1, source_target_pairs={{8,0},{16,8},{24,16},{32,24},{40,32},{48,40},{56,48},{64,56},{72,6... | collective-permute-start | bytes 208904 | tf_op jit(solution)/shard_map/ppermute | solution.py:735

commit v6 on v5

--- a/solution.py
+++ b/solution.py
@@ -180,7 +180,7 @@
         else:
             both = cadd(ys[k], mirror)
             gap = spun(csub(ys[k], mirror), k, count, 1.0)
-            if k == 0:
+            if half == 1 and k == 0:
                 both = (both[0], None)
                 gap = (gap[0], None)
             evens.append(both)
@@ -494,8 +494,8 @@
 
 def tensor_kernel(half, place_ref, *refs):
     if half == 0:
-        near_ref, above_ref, below_ref, lanes_ref, nine_ref, out_ref = refs[:6]
-        slope, level, prod, trio, both_ref = refs[6:]
+        near_ref, lanes_ref, nine_ref, out_ref = refs[:4]
+        slope, level, prod, trio, both_ref = refs[4:]
     else:
         near_ref, above_ref, below_ref, far_ref, lanes_ref, nine_ref, _, out_ref = refs[:8]
         slope, level, prod, trio, both_ref = refs[8:]
@@ -506,19 +506,24 @@
 
     def column(t):
         if t in (-1, 16):
-            parts = [pltpu.roll(above_ref[pl.ds(144, 16), :].astype(F32), 64, 1).astype(BF)]
+            parts = []
             for j in range(8):
                 side = near_ref[j, pl.ds(SIDE, 16), :].astype(F32)
                 parts.append(side.astype(BF))
                 for n in range(1, 5):
                     parts.append(pltpu.roll(side, 128 - 16 * n, 1).astype(BF))
-            return jnp.concatenate(parts + [below_ref[pl.ds(144, 16), :]], axis=0)
+            if half == 1:
+                first = pltpu.roll(above_ref[pl.ds(144, 16), :].astype(F32), 64, 1).astype(BF)
+                parts = [first] + parts + [below_ref[pl.ds(144, 16), :]]
+            return jnp.concatenate(parts, axis=0)
         rows = pl.ds(16 * t if t < 9 else 160 + 16 * (t - 9), 16)
         if t < 9:
             inner = [near_ref[j, pl.ds(t * ROWS, ROWS), :] for j in range(8)]
         else:
             inner = [far_ref[:, (t - 9) * 128 : (t - 8) * 128]]
-        return jnp.concatenate([above_ref[rows, :]] + inner + [below_ref[rows, :]], axis=0)
+        if half == 1:
+            inner = [above_ref[rows, :]] + inner + [below_ref[rows, :]]
+        return jnp.concatenate(inner, axis=0)
 
     @pl.when(step == 0)
     def _():
@@ -526,8 +531,9 @@
         for t in range(PER):
             right = column(8 * half + t)
             res = dot(jnp.concatenate([left, right], axis=1), lanes_ref[...])
-            slope[t] = res[:, :128]
-            level[t] = res[:, 128:]
+            rows = pl.ds(16 - 16 * half, 640 + 32 * half)
+            slope[t, rows, :] = res[:, :128]
+            level[t, rows, :] = res[:, 128:]
             left = right
 
     top = pl.multiple_of(step * BAND, BAND)
@@ -540,9 +546,9 @@
                 masked = jnp.where((lane >= 4) | (part > 0), masked, 0.0)
             if half == 1 and t == PER - 1:
                 masked = jnp.where((lane < 4) | (part < 7), masked, 0.0)
-            if k == 0:
+            if half == 1 and k == 0:
                 masked = jnp.where((sub >= 4) | (chan > 0) | (step > 0), masked, 0.0)
-            if k == BAND // 8:
+            if half == 1 and k == BAND // 8:
                 masked = jnp.where((sub < 4) | (chan < 15) | (step < 640 // BAND - 1), masked, 0.0)
             grad_chan = level[t, pl.ds(base + 13, 8), :] - level[t, pl.ds(base + 11, 8), :]
             prod[0, t, pl.ds(k * 8, 8), :] = grad_chan * masked
@@ -579,6 +585,73 @@
             out_ref[:, cols] = res[t * BAND : (t + 1) * BAND]
 
 
+def ahead(parts, count, lane):
+    turned = [pltpu.roll(v, (-count) % 128, 1) for v in parts]
+    out = []
+    for t in range(len(parts)):
+        if count > 0:
+            other = turned[min(t + 1, len(parts) - 1)]
+            out.append(jnp.where(lane < 128 - count, turned[t], other))
+        else:
+            other = turned[max(t - 1, 0)]
+            out.append(jnp.where(lane < -count, other, turned[t]))
+    return out
+
+
+def edge_kernel(place_ref, above_ref, top_ref, bottom_ref, below_ref, _, out_ref, wide, prod):
+    lane = lax.broadcasted_iota(jnp.int32, (8, 128), 1)
+    sub = lax.broadcasted_iota(jnp.int32, (8, 128), 0)
+    step = pl.program_id(0)
+    chan, part = place_ref[0], place_ref[1]
+
+    def spread(start, ref, turned):
+        rows = pl.ds(start, 16)
+        wide[0, rows, :] = pltpu.roll(ref[pl.ds(144, 16), :].astype(F32), turned, 1)
+        for t in range(9):
+            wide[t + 1, rows, :] = ref[pl.ds(16 * t, 16), :].astype(F32)
+
+    @pl.when(step == 0)
+    def _():
+        spread(0, above_ref, 64)
+        spread(16, top_ref, 0)
+
+    @pl.when(step == 1)
+    def _():
+        spread(0, bottom_ref, 64)
+        spread(16, below_ref, 0)
+
+    skip = pl.multiple_of(8 - step * 8, 8)
+    for k in range(2):
+        first = skip + k * 8 + 4
+        row = sub + first
+        keep = ((row >= 16) | (step == 1) | (chan > 0)) & ((row < 16) | (step == 0) | (chan < 15))
+        here = [wide[t, pl.ds(first, 8), :] for t in range(10)]
+        right, left = ahead(here, 1, lane), ahead(here, -1, lane)
+        for t in range(10):
+            grad_time = right[t] - left[t]
+            masked = jnp.where(keep, grad_time, 0.0)
+            if t == 0:
+                masked = jnp.where(part > 0, masked, 0.0)
+            grad_chan = wide[t, pl.ds(first + 1, 8), :] - wide[t, pl.ds(first - 1, 8), :]
+            prod[0, t, pl.ds(k * 8, 8), :] = grad_chan * masked
+            prod[1, t, pl.ds(k * 8, 8), :] = grad_time * masked
+    sums = []
+    for n in range(2):
+        parts = []
+        for t in range(10):
+            total = prod[n, t, pl.ds(0, 8), :]
+            for d in range(1, 9):
+                total = total + prod[n, t, pl.ds(d, 8), :]
+            parts.append(total)
+        near, far = ahead(parts, 1, lane), ahead(parts, -1, lane)
+        three = [v + a + b for v, a, b in zip(parts, near, far)]
+        near, far = ahead(three, 3, lane), ahead(three, -3, lane)
+        sums.append([v + a + b for v, a, b in zip(three, near, far)][1:9])
+    scale = 1.0 / 324.0
+    out = [(c * -scale) / (a * scale + 1e-05) for c, a in zip(*sums)]
+    out_ref[...] = jnp.concatenate(out, axis=1)
+
+
 def call(kernel, out, specs, scratch, flops, *args, smem=0):
     nbytes = sum(a.size * a.dtype.itemsize for a in args) + 3 * 2**20
     return pl.pallas_call(
@@ -650,7 +723,7 @@
     return call(channel_kernel, out, VMEM, scratch, 8 * 10**9, pencil, low, high, packed, *tables)
 
 
-def tensor(half, place, near, above, below, far=None, whole=None):
+def tensor(half, place, near, above=None, below=None, far=None, whole=None):
     lanes, nine = (jnp.asarray(t.astype(ml_dtypes.bfloat16)) for t in slide_tables())
     scratch = [
         pltpu.VMEM((PER, 672, 128), F32),
@@ -660,8 +733,8 @@
         pltpu.VMEM((2, PER, BAND, 256), BF),
     ]
     if half == 0:
-        args = (place, near, above, below, lanes, nine)
-        specs, alias = [SMEM] + [VMEM] * 5, {}
+        args = (place, near, lanes, nine)
+        specs, alias = [SMEM] + [VMEM] * 3, {}
     else:
         args = (place, near, above, below, far, lanes, nine, whole)
         specs, alias = [SMEM] + [VMEM] * 6 + [ANY], {7: 0}
@@ -676,6 +749,20 @@
         compiler_params=pltpu.CompilerParams(vmem_limit_bytes=40 * 2**20),
         cost_estimate=pl.CostEstimate(flops=10**9, bytes_accessed=9 * 2**20, transcendentals=0),
     )(*args)
+
+
+def edges(place, above, top, bottom, below, whole):
+    return pl.pallas_call(
+        edge_kernel,
+        grid=(2,),
+        out_shape=jax.ShapeDtypeStruct((640, 2048), F32),
+        in_specs=[SMEM] + [VMEM] * 4 + [ANY],
+        out_specs=pl.BlockSpec((8, 1024), lambda g: (79 * g, 0)),
+        scratch_shapes=[pltpu.VMEM((10, 32, 128), F32), pltpu.VMEM((2, 10, 16, 128), F32)],
+        input_output_aliases={5: 0},
+        compiler_params=pltpu.CompilerParams(vmem_limit_bytes=16 * 2**20),
+        cost_estimate=pl.CostEstimate(flops=10**7, bytes_accessed=2**19, transcendentals=0),
+    )(place, above, top, bottom, below, whole)
 
 
 def window_bounds(fan_bounds, block):
@@ -733,7 +820,7 @@
     top, bottom = call(outer_kernel, [outer, outer], [VMEM, VMEM], [], 10**6, near)
     above = lax.ppermute(bottom, "chan", down)
     below = lax.ppermute(top, "chan", [(b, a) for a, b in down])
-    whole = tensor(0, place, near, above, below)
+    whole = edges(place, above, top, bottom, below, tensor(0, place, near))
     far = lax.all_to_all(after(far, near), "tm", 0, 0, tiled=True).reshape(640, FAR)
     return tensor(1, place, near, above, below, far, whole)
 

time: 202 us -> 198 us (0.980)
  waiting for transfers between devices: 36.1 us -> 29.8 us
    ppermute x1, waiting for transfers between devices: 3.86 us -> 0.01 us  [per_device(): above = lax.ppermute(bottom, 'chan', down)]
    ppermute x1, waiting for transfers between devices: 4.31 us -> 1.88 us  [per_device(): below = lax.ppermute(top, 'chan', [(b, a) for a, b in down])]
  transfers between devices with their start and end apart: 4 -> 4, of which waited for: 3 -> 2; matrix products, arithmetic and copies ran while one was open for 1% -> 1% of each run, Pallas kernels for 3% -> 4%
where the time goes in v6:
time: 198 us
  blocking collectives  108 us (55%)
  Pallas kernels  37.1 us (19%)
  waiting for transfers between devices  29.8 us (15%)
  starting transfers between devices  18.2 us (9%)
  between operations  2.12 us (1%)
    all_to_all x1, blocking collectives, per_device(): pencil = lax.all_to_all(spectra, ('chan', 'tm'), 0, 0, tiled=True)  43.9 us
    all_to_all x1, blocking collectives, per_device(): back = lax.all_to_all(passed, ('chan', 'tm'), 0, 0, tiled=True)  40.2 us
    all_to_all x1, waiting for transfers between devices, per_device(): lax.all_to_all(record.reshape(8, ROWS, 2048), 'tm', 0, 0, tiled=True)  27.9 us
    all_to_all x1, blocking collectives, per_device(): near = lax.all_to_all(near, 'tm', 0, 0, tiled=True)  24.1 us
    pallas_call x4, Pallas kernels, call(): pl.pallas_call(kernel, out_shape=out, in_specs=[SMEM] * smem + [VMEM] * (...  22.6 us
    pallas_call x2, Pallas kernels, tensor(): pl.pallas_call(functools.partial(tensor_kernel, half), grid=(640 // BAND,...  12.5 us
    all_to_all x1, starting transfers between devices, per_device(): lax.all_to_all(record.reshape(8, ROWS, 2048), 'tm', 0, 0, tiled=True)  7.02 us
    ppermute x1, starting transfers between devices, per_device(): above = lax.ppermute(bottom, 'chan', down)  5.53 us
  transfers between devices with their start and end apart: 4, of which 2 were waited for; matrix products, arithmetic and copies ran while one was open for 1% of the time, Pallas kernels for 4%

profile of v6, /device:TPU:1, one launch (start us, length us, event | category | flops | bytes accessed | tf_op | source)
XLA Modules:
  0.0 197.7 jit_solution(3318840033151630598)
XLA Ops:
  0.0 0.0 copy-start.9
  0.0 0.0 copy-start.12
  0.0 0.0 copy-start.13
  0.0 7.0 %all-to-all-start = ((bf16[8,80,2048]{2,1,0:T(8,128)(2,1)}), bf16[8,80,2048]{2,1,0:T(8,128)(2,1)S(1)}, u32[]{:S(2)}, u32[]{:S(2)}) async-start(bf16[8,80,2048]{2,1,0:T(8,128)(2,1)} %bitcast.15), calls=%async_computation | async-start | bytes 5242880 | tf_op jit(solution)/shard_map/all_to_all | solution.py:806
  7.1 0.0 copy-done.15
  7.1 0.7 dynamic_slice.10
  9.0 0.0 copy-done.14
  9.6 0.1 constant_dynamic-slice_fusion
  9.7 0.1 copy.25
  9.8 0.1 pad_add_fusion.1.place_ref
  9.9 0.8 dynamic-slice_convert_fusion
  10.7 0.1 slice_reduce_fusion
  10.8 0.1 broadcast_in_dim.26
  10.8 0.1 fusion.2
  10.9 27.9 %all-to-all-done.x_ref = bf16[8,80,2048]{2,1,0:T(8,128)(2,1)S(1)} async-done(((bf16[8,80,2048]{2,1,0:T(8,128)(2,1)}), bf16[8,80,2048]{2,1,0:T(8,128)(2,1)S(1)}, u32[]{:S(2)}, u32[]{:S(2)}) %all-to-all-start) | async-done | bytes 2621472 | tf_op jit(solution)/shard_map/all_to_all | solution.py:806
  38.8 0.1 iota.7.packed_ref.first_ref
  38.9 0.1 broadcast_in_dim.24.ok_ref
  39.0 0.1 broadcast_in_dim.30.high_ref
  39.0 0.1 broadcast_in_dim.28.low_ref
  39.1 0.0 copy-done.9
  39.2 6.5 %shard_map.190 = bf16[128,80,128]{2,1,0:T(8,128)(2,1)S(1)} custom-call(s32[2]{0:T(128)S(1)} %pad_add_fusion.1.place_ref, bf16[8,80,2048]{2,1,0:T(8,128)(2,1)S(1)} %all-to-all-done.x_ref, f32[80,128]{1,0:T(8,128)S(1)} %broadcast_in_dim.24.ok_ref, s32[72,128]{1,0:T(8,128)S(1)} %broadcast_in_dim.28.low_ref, s32[72,128]{1,0:T(8,128)S(1)} %broadcast_in_dim.30.high_ref, ...), custom_call_target="tpu_custom_call" | custom-call | flops 4000000000 | bytes 6475784 | tf_op jit(solution)/shard_map/pallas_call | solution.py:657
  45.7 0.0 copy-start.6
  45.7 0.0 copy-start.7
  45.7 0.0 copy-start.10
  45.7 0.0 copy-start.11
  45.7 43.9 %all_to_all.25.in_ref = bf16[128,80,128]{2,1,0:T(8,128)(2,1)S(1)} all-to-all(bf16[128,80,128]{2,1,0:T(8,128)(2,1)S(1)} %shard_map.190), channel_id=1, replica_groups=mesh['chan'=16,'tm'=8] {'chan','tm'}, dimensions={0} | all-to-all | bytes 5242880 | tf_op jit(solution)/shard_map/all_to_all | solution.py:813
  89.7 0.0 copy-done.11
  89.7 11.6 %shard_map.191 = bf16[128,80,128]{2,1,0:T(8,128)(2,1)S(1)} custom-call(bf16[128,80,128]{2,1,0:T(8,128)(2,1)S(1)} %all_to_all.25.in_ref, s32[72,128]{1,0:T(8,128)S(1)} %broadcast_in_dim.28.low_ref, s32[72,128]{1,0:T(8,128)S(1)} %broadcast_in_dim.30.high_ref, f32[8,128]{1,0:T(8,128)S(1)} %iota.7.packed_ref.first_ref, f32[80,128]{1,0:T(8,128)S(1)} %copy-done.11, ...), custom_call_target="tpu_custom_call" | custom-call | flops 8000000000 | bytes 6451200 | tf_op jit(solution)/shard_map/pallas_call | solution.py:657
  101.3 0.0 copy-start.4
  101.3 0.0 copy-start.5
  101.3 40.2 %all_to_all.26.in_ref = bf16[128,80,128]{2,1,0:T(8,128)(2,1)S(1)} all-to-all(bf16[128,80,128]{2,1,0:T(8,128)(2,1)S(1)} %shard_map.191), channel_id=1, replica_groups=mesh['chan'=16,'tm'=8] {'chan','tm'}, dimensions={0} | all-to-all | bytes 5242880 | tf_op jit(solution)/shard_map/all_to_all | solution.py:815
  141.5 0.0 copy-done.4
  141.5 4.4 %shard_map.192 = (bf16[8,848,128]{2,1,0:T(8,128)(2,1)S(1)}, bf16[8,80,896]{2,1,0:T(8,128)(2,1)S(1)}) custom-call(s32[2]{0:T(128)S(1)} %pad_add_fusion.1.place_ref, bf16[128,80,128]{2,1,0:T(8,128)(2,1)S(1)} %all_to_all.26.in_ref, f32[64,128]{1,0:T(8,128)S(1)} %copy-done.13, f32[64,128]{1,0:T(8,128)S(1)} %copy-done.12, bf16[2,256,256]{2,1,0:T(8,128)(2,1)S(1)} %copy-done.5, ...), custom_call_target="tpu_custom_call" | custom-call | flops 4000000000 | bytes 6357000 | tf_op jit(solution)/shard_map/pallas_call | solution.py:657
  145.9 0.0 copy-start.1
  145.9 24.1 %all_to_all.27.near_ref.sign_ref.refs_0_ = bf16[8,848,128]{2,1,0:T(8,128)(2,1)} all-to-all(bf16[8,848,128]{2,1,0:T(8,128)(2,1)S(1)} %get-tuple-element.9), channel_id=1, replica_groups=mesh['chan'=16,'tm'=8] {'tm'}, dimensions={0} | all-to-all | bytes 3473408 | tf_op jit(solution)/shard_map/all_to_all | solution.py:817
  170.1 0.0 copy-done.1
  170.1 0.0 copy-start.3
  170.1 3.7 %all-to-all-start.4 = ((bf16[8,80,896]{2,1,0:T(8,128)(2,1)}), bf16[8,80,896]{2,1,0:T(8,128)(2,1)S(1)}, u32[]{:S(2)}, u32[]{:S(2)}) async-start(bf16[8,80,896]{2,1,0:T(8,128)(2,1)} %shard_map.194), calls=%async_computation.4 | async-start | bytes 2293760 | tf_op jit(solution)/shard_map/all_to_all | solution.py:824
  173.8 5.5 %collective-permute-start = (bf16[272,128]{1,0:T(8,128)(2,1)S(1)}, bf16[272,128]{1,0:T(8,128)(2,1)S(1)}, u32[]{:S(2)}, u32[]{:S(2)}) collective-permute-start(bf16[272,128]{1,0:T(8,128)(2,1)S(1)} %get-tuple-element.10.bottom_ref), channel_id=1, source_target_pairs={{0,8},{8,16},{16,24},{24,32},{32,40},{40,48},{48,56},{56,64},{64,7... | collective-permute-start | bytes 208904 | tf_op jit(solution)/shard_map/ppermute | solution.py:821
  179.4 1.9 collective-permute-start.1
  181.3 0.0 copy-done.2
  181.3 0.0 copy-done.3
  181.3 6.3 %shard_map.195._ = f32[640,2048]{1,0:T(8,128)} custom-call(s32[2]{0:T(128)S(1)} %pad_add_fusion.1.place_ref, bf16[8,848,128]{2,1,0:T(8,128)(2,1)S(1)} %copy-done, bf16[256,256]{1,0:T(8,128)(2,1)S(1)} %copy-done.3, bf16[256,256]{1,0:T(8,128)(2,1)S(1)} %copy-done.2), custom_call_target="tpu_custom_call" | custom-call | flops 1000000000 | bytes 9437184 | tf_op jit(solution)/shard_map/pallas_call | solution.py:741
  187.6 0.0 collective-permute-done.above_ref.refs_1_
  187.6 1.9 collective-permute-done.1.below_ref.refs_2_
  189.5 2.0 %shard_map.196.refs_6_ = f32[640,2048]{1,0:T(8,128)} custom-call(s32[2]{0:T(128)S(1)} %pad_add_fusion.1.place_ref, bf16[272,128]{1,0:T(8,128)(2,1)S(1)} %collective-permute-done.above_ref.refs_1_, bf16[272,128]{1,0:T(8,128)(2,1)S(1)} %get-tuple-element.11.top_ref, bf16[272,128]{1,0:T(8,128)(2,1)S(1)} %get-tuple-element.10.bottom_ref, ...), custom_call_target="tpu_custom_call", output_to_operand_aliasing={{}: (5, {})} | custom-call | flops 10000000 | bytes 524288 | tf_op jit(solution)/shard_map/pallas_call | solution.py:755
  191.5 0.0 all-to-all-done.4
  191.5 6.2 %shard_map.197 = f32[640,2048]{1,0:T(8,128)} custom-call(s32[2]{0:T(128)S(1)} %pad_add_fusion.1.place_ref, bf16[8,848,128]{2,1,0:T(8,128)(2,1)S(1)} %copy-done, bf16[272,128]{1,0:T(8,128)(2,1)S(1)} %collective-permute-done.above_ref.refs_1_, bf16[272,128]{1,0:T(8,128)(2,1)S(1)} %collective-permute-done.1.below_ref.refs_2_, ...), custom_call_target="tpu_custom_call", output_to_operand_aliasing={{}: (7, {})} | custom-call | flops 1000000000 | bytes 9437184 | tf_op jit(solution)/shard_map/pallas_call | solution.py:741
  (18 shorter events, 0.1 us)
Async XLA Ops:
  0.0 7.1 %copy-start.15 = (s32[128]{0:T(128)S(1)}, s32[128]{0:T(128)}, u32[]{:S(2)}) copy-start(s32[128]{0:T(128)} %constant.46.clone) | copy-start | bytes 1540
  0.0 9.0 %copy-start.14 = (s32[2,8193]{1,0:T(2,128)S(1)}, s32[2,8193]{1,0:T(2,128)}, u32[]{:S(2)}) copy-start(s32[2,8193]{1,0:T(2,128)} %param.22) | copy-start | bytes 196636
  0.0 39.1 %copy-start.8 = (bf16[2,256,256]{2,1,0:T(8,128)(2,1)S(1)}, bf16[2,256,256]{2,1,0:T(8,128)(2,1)}, u32[]{:S(2)}) copy-start(bf16[2,256,256]{2,1,0:T(8,128)(2,1)} %constant.50.clone.w0_ref) | copy-start | bytes 786436
  0.0 39.1 %copy-start.9 = (bf16[2,256,256]{2,1,0:T(8,128)(2,1)S(1)}, bf16[2,256,256]{2,1,0:T(8,128)(2,1)}, u32[]{:S(2)}) copy-start(bf16[2,256,256]{2,1,0:T(8,128)(2,1)} %constant.49.clone.w_ref) | copy-start | bytes 786436
  0.0 39.1 %copy-start.12 = (f32[64,128]{1,0:T(8,128)S(1)}, f32[64,128]{1,0:T(8,128)}, u32[]{:S(2)}) copy-start(f32[64,128]{1,0:T(8,128)} %constant.48.clone.ts_ref) | copy-start | bytes 98308
  0.0 39.1 %copy-start.13 = (f32[64,128]{1,0:T(8,128)S(1)}, f32[64,128]{1,0:T(8,128)}, u32[]{:S(2)}) copy-start(f32[64,128]{1,0:T(8,128)} %constant.47.clone.tc_ref) | copy-start | bytes 98308
  0.0 38.8 %all-to-all-start = ((bf16[8,80,2048]{2,1,0:T(8,128)(2,1)}), bf16[8,80,2048]{2,1,0:T(8,128)(2,1)S(1)}, u32[]{:S(2)}, u32[]{:S(2)}) async-start(bf16[8,80,2048]{2,1,0:T(8,128)(2,1)} %bitcast.15), calls=%async_computation | async-start | bytes 5242880 | tf_op jit(solution)/shard_map/all_to_all | solution.py:806
  45.7 44.0 %copy-start.6 = (bf16[2,256,256]{2,1,0:T(8,128)(2,1)S(1)}, bf16[2,256,256]{2,1,0:T(8,128)(2,1)}, u32[]{:S(2)}) copy-start(bf16[2,256,256]{2,1,0:T(8,128)(2,1)} %constant.54.clone.v_ref) | copy-start | bytes 786436
  45.7 44.0 %copy-start.7 = (bf16[2,256,256]{2,1,0:T(8,128)(2,1)S(1)}, bf16[2,256,256]{2,1,0:T(8,128)(2,1)}, u32[]{:S(2)}) copy-start(bf16[2,256,256]{2,1,0:T(8,128)(2,1)} %constant.53.clone.w_ref) | copy-start | bytes 786436
  45.7 43.9 %copy-start.10 = (f32[80,128]{1,0:T(8,128)S(1)}, f32[80,128]{1,0:T(8,128)}, u32[]{:S(2)}) copy-start(f32[80,128]{1,0:T(8,128)} %constant.52.clone.ts_ref) | copy-start | bytes 122884
  45.7 43.9 %copy-start.11 = (f32[80,128]{1,0:T(8,128)S(1)}, f32[80,128]{1,0:T(8,128)}, u32[]{:S(2)}) copy-start(f32[80,128]{1,0:T(8,128)} %constant.51.clone.tc_ref) | copy-start | bytes 122884
  101.3 40.2 %copy-start.4 = (bf16[2,256,256]{2,1,0:T(8,128)(2,1)S(1)}, bf16[2,256,256]{2,1,0:T(8,128)(2,1)}, u32[]{:S(2)}) copy-start(bf16[2,256,256]{2,1,0:T(8,128)(2,1)} %constant.56.clone.w0_ref) | copy-start | bytes 786436
  101.3 40.2 %copy-start.5 = (bf16[2,256,256]{2,1,0:T(8,128)(2,1)S(1)}, bf16[2,256,256]{2,1,0:T(8,128)(2,1)}, u32[]{:S(2)}) copy-start(bf16[2,256,256]{2,1,0:T(8,128)(2,1)} %constant.55.clone.w_ref) | copy-start | bytes 786436
  145.9 24.1 %copy-start.1 = (bf16[8,80,896]{2,1,0:T(8,128)(2,1)}, bf16[8,80,896]{2,1,0:T(8,128)(2,1)S(1)}, u32[]{:S(2)}) copy-start(bf16[8,80,896]{2,1,0:T(8,128)(2,1)S(1)} %get-tuple-element.12.value_ref) | copy-start | bytes 3440644
  170.1 3.7 %copy-start = (bf16[8,848,128]{2,1,0:T(8,128)(2,1)S(1)}, bf16[8,848,128]{2,1,0:T(8,128)(2,1)}, u32[]{:S(2)}) copy-start(bf16[8,848,128]{2,1,0:T(8,128)(2,1)} %all_to_all.27.near_ref.sign_ref.refs_0_) | copy-start | bytes 5210116
  170.1 11.2 %copy-start.2 = (bf16[256,256]{1,0:T(8,128)(2,1)S(1)}, bf16[256,256]{1,0:T(8,128)(2,1)}, u32[]{:S(2)}) copy-start(bf16[256,256]{1,0:T(8,128)(2,1)} %constant.58.clone.refs_2_.refs_5_) | copy-start | bytes 393220
  170.1 11.2 %copy-start.3 = (bf16[256,256]{1,0:T(8,128)(2,1)S(1)}, bf16[256,256]{1,0:T(8,128)(2,1)}, u32[]{:S(2)}) copy-start(bf16[256,256]{1,0:T(8,128)(2,1)} %constant.57.clone.refs_1_.refs_4_) | copy-start | bytes 393220
  170.1 21.4 %all-to-all-start.4 = ((bf16[8,80,896]{2,1,0:T(8,128)(2,1)}), bf16[8,80,896]{2,1,0:T(8,128)(2,1)S(1)}, u32[]{:S(2)}, u32[]{:S(2)}) async-start(bf16[8,80,896]{2,1,0:T(8,128)(2,1)} %shard_map.194), calls=%async_computation.4 | async-start | bytes 2293760 | tf_op jit(solution)/shard_map/all_to_all | solution.py:824
  173.8 13.8 %collective-permute-start = (bf16[272,128]{1,0:T(8,128)(2,1)S(1)}, bf16[272,128]{1,0:T(8,128)(2,1)S(1)}, u32[]{:S(2)}, u32[]{:S(2)}) collective-permute-start(bf16[272,128]{1,0:T(8,128)(2,1)S(1)} %get-tuple-element.10.bottom_ref), channel_id=1, source_target_pairs={{0,8},{8,16},{16,24},{24,32},{32,40},{40,48},{48,56},{56,64},{64,7... | collective-permute-start | bytes 208904 | tf_op jit(solution)/shard_map/ppermute | solution.py:821
  179.4 10.1 %collective-permute-start.1 = (bf16[272,128]{1,0:T(8,128)(2,1)S(1)}, bf16[272,128]{1,0:T(8,128)(2,1)S(1)}, u32[]{:S(2)}, u32[]{:S(2)}) collective-permute-start(bf16[272,128]{1,0:T(8,128)(2,1)S(1)} %get-tuple-element.11.top_ref), channel_id=1, source_target_pairs={{8,0},{16,8},{24,16},{32,24},{40,32},{48,40},{56,48},{64,56},{72,6... | collective-permute-start | bytes 208904 | tf_op jit(solution)/shard_map/ppermute | solution.py:822

commit v7 on v6

--- a/solution.py
+++ b/solution.py
@@ -23,7 +23,6 @@
 BF = jnp.bfloat16
 F32 = jnp.float32
 VMEM = pl.BlockSpec(memory_space=pltpu.VMEM)
-SMEM = pl.BlockSpec(memory_space=pltpu.SMEM)
 ANY = pl.BlockSpec(memory_space=pl.ANY)
 
 WAVES = [0] + [8 * n for n in range(1, 8)] + [4 + 8 * n for n in range(8)]
@@ -235,7 +234,7 @@
 
 
 def forward_kernel(
-    place_ref, x_ref, ok_ref, low_ref, high_ref, packed_ref, tc_ref, ts_ref, w_ref, w0_ref, out_ref,
+    x_ref, ok_ref, low_ref, high_ref, packed_ref, tc_ref, ts_ref, w_ref, w0_ref, out_ref,
     stage, hi_ref, lo_ref
 ):
     def tile_body(tile, carry):
@@ -298,7 +297,7 @@
 
 
 def backward_kernel(
-    place_ref, in_ref, tc_ref, ts_ref, w_ref, w0_ref, near_ref, far_ref, stage, mid_ref
+    in_ref, tc_ref, ts_ref, w_ref, w0_ref, near_ref, far_ref, stage, mid_ref
 ):
     def joined(slot):
         return jnp.concatenate([in_ref[2 * slot], in_ref[2 * slot + 1]], axis=1)
@@ -366,7 +365,7 @@
             both = jnp.where(lane < 64, after.astype(F32), before.astype(F32))
             here = ((lane - 16 * tile + 5) & 127) < 10
             sides[s] = jnp.where(here, pltpu.roll(both, 16 * tile, 1), sides[s])
-    base = pl.multiple_of(jnp.where(place_ref[1] == 7, 64, 0), 16)
+    base = pl.multiple_of(jnp.where(lax.axis_index("tm") == 7, 64, 0), 16)
     for s in range(8):
         near_ref[s, pl.ds(SIDE, 16), :] = sides[s].astype(BF)
         for n in range(7):
@@ -492,7 +491,7 @@
 PER = 9
 
 
-def tensor_kernel(half, place_ref, *refs):
+def tensor_kernel(half, *refs):
     if half == 0:
         near_ref, lanes_ref, nine_ref, out_ref = refs[:4]
         slope, level, prod, trio, both_ref = refs[4:]
@@ -502,7 +501,7 @@
     lane = lax.broadcasted_iota(jnp.int32, (8, 128), 1)
     sub = lax.broadcasted_iota(jnp.int32, (8, 128), 0)
     step = pl.program_id(0)
-    chan, part = place_ref[0], place_ref[1]
+    chan, part = lax.axis_index("chan"), lax.axis_index("tm")
 
     def column(t):
         if t in (-1, 16):
@@ -598,11 +597,11 @@
     return out
 
 
-def edge_kernel(place_ref, above_ref, top_ref, bottom_ref, below_ref, _, out_ref, wide, prod):
+def edge_kernel(above_ref, top_ref, bottom_ref, below_ref, _, out_ref, wide, prod):
     lane = lax.broadcasted_iota(jnp.int32, (8, 128), 1)
     sub = lax.broadcasted_iota(jnp.int32, (8, 128), 0)
     step = pl.program_id(0)
-    chan, part = place_ref[0], place_ref[1]
+    chan, part = lax.axis_index("chan"), lax.axis_index("tm")
 
     def spread(start, ref, turned):
         rows = pl.ds(start, 16)
@@ -652,12 +651,12 @@
     out_ref[...] = jnp.concatenate(out, axis=1)
 
 
-def call(kernel, out, specs, scratch, flops, *args, smem=0):
+def call(kernel, out, specs, scratch, flops, *args):
     nbytes = sum(a.size * a.dtype.itemsize for a in args) + 3 * 2**20
     return pl.pallas_call(
         kernel,
         out_shape=out,
-        in_specs=[SMEM] * smem + [VMEM] * (len(args) - smem),
+        in_specs=[VMEM] * len(args),
         out_specs=specs,
         scratch_shapes=scratch,
         compiler_params=pltpu.CompilerParams(vmem_limit_bytes=48 * 2**20),
@@ -673,7 +672,7 @@
     return jnp.asarray(table.astype(np.float32))
 
 
-def forward(place, series, good, low, high, packed):
+def forward(series, good, low, high, packed):
     fwd, _, first, _, tc, ts = time_tables()
     scratch = [
         pltpu.VMEM((16, 8, 16, 128), F32),
@@ -688,24 +687,22 @@
         VMEM,
         scratch,
         4 * 10**9,
-        place,
         series,
         good,
         low,
         high,
         packed,
         *tables,
-        smem=1,
     )
 
 
-def backward(place, spectra):
+def backward(spectra):
     _, bwd, _, last, tc, ts = time_tables()
     scratch = [pltpu.VMEM((16, 8, 16, 128), F32), pltpu.VMEM((64 * ROWS, 256), F32)]
     out = [jax.ShapeDtypeStruct(s, BF) for s in ((8, NEAR, 128), (8, ROWS, FAR))]
     tables = single(tc), single(ts), pair(bwd), pair(last)
     return call(
-        backward_kernel, out, [VMEM, VMEM], scratch, 4 * 10**9, place, spectra, *tables, smem=1
+        backward_kernel, out, [VMEM, VMEM], scratch, 4 * 10**9, spectra, *tables
     )
 
 
@@ -723,7 +720,7 @@
     return call(channel_kernel, out, VMEM, scratch, 8 * 10**9, pencil, low, high, packed, *tables)
 
 
-def tensor(half, place, near, above=None, below=None, far=None, whole=None):
+def tensor(half, near, above=None, below=None, far=None, whole=None):
     lanes, nine = (jnp.asarray(t.astype(ml_dtypes.bfloat16)) for t in slide_tables())
     scratch = [
         pltpu.VMEM((PER, 672, 128), F32),
@@ -733,11 +730,11 @@
         pltpu.VMEM((2, PER, BAND, 256), BF),
     ]
     if half == 0:
-        args = (place, near, lanes, nine)
-        specs, alias = [SMEM] + [VMEM] * 3, {}
+        args = (near, lanes, nine)
+        specs, alias = [VMEM] * 3, {}
     else:
-        args = (place, near, above, below, far, lanes, nine, whole)
-        specs, alias = [SMEM] + [VMEM] * 6 + [ANY], {7: 0}
+        args = (near, above, below, far, lanes, nine, whole)
+        specs, alias = [VMEM] * 6 + [ANY], {6: 0}
     return pl.pallas_call(
         functools.partial(tensor_kernel, half),
         grid=(640 // BAND,),
@@ -751,18 +748,18 @@
     )(*args)
 
 
-def edges(place, above, top, bottom, below, whole):
+def edges(above, top, bottom, below, whole):
     return pl.pallas_call(
         edge_kernel,
         grid=(2,),
         out_shape=jax.ShapeDtypeStruct((640, 2048), F32),
-        in_specs=[SMEM] + [VMEM] * 4 + [ANY],
+        in_specs=[VMEM] * 4 + [ANY],
         out_specs=pl.BlockSpec((8, 1024), lambda g: (79 * g, 0)),
         scratch_shapes=[pltpu.VMEM((10, 32, 128), F32), pltpu.VMEM((2, 10, 16, 128), F32)],
-        input_output_aliases={5: 0},
+        input_output_aliases={4: 0},
         compiler_params=pltpu.CompilerParams(vmem_limit_bytes=16 * 2**20),
         cost_estimate=pl.CostEstimate(flops=10**7, bytes_accessed=2**19, transcendentals=0),
-    )(place, above, top, bottom, below, whole)
+    )(above, top, bottom, below, whole)
 
 
 def window_bounds(fan_bounds, block):
@@ -802,27 +799,26 @@
 def per_device(record, channel_ok, fan_bounds):
     chan, part = lax.axis_index("chan"), lax.axis_index("tm")
     block = chan * 8 + part
-    place = jnp.stack([chan, part]).astype(jnp.int32)
     series = lax.all_to_all(record.reshape(8, ROWS, 2048), "tm", 0, 0, tiled=True)
     good = lax.dynamic_slice(channel_ok, (part * ROWS,), (ROWS,)).astype(F32)
     good = jnp.broadcast_to(good[:, None], (ROWS, 128))
     low, high = window_bounds(fan_bounds, block)
     corner = lax.broadcasted_iota(jnp.int32, (8, 128), 0) == 0
     packed = (corner & (block == 0)).astype(F32)
-    spectra = forward(place, series, good, low, high, packed)
+    spectra = forward(series, good, low, high, packed)
     pencil = lax.all_to_all(spectra, ("chan", "tm"), 0, 0, tiled=True)
     passed = channels(pencil, low, high, packed)
     back = lax.all_to_all(passed, ("chan", "tm"), 0, 0, tiled=True)
-    near, far = backward(place, back)
+    near, far = backward(back)
     near = lax.all_to_all(near, "tm", 0, 0, tiled=True)
     down = [(i, i + 1) for i in range(15)]
     outer = jax.ShapeDtypeStruct((272, 128), BF)
     top, bottom = call(outer_kernel, [outer, outer], [VMEM, VMEM], [], 10**6, near)
     above = lax.ppermute(bottom, "chan", down)
     below = lax.ppermute(top, "chan", [(b, a) for a, b in down])
-    whole = edges(place, above, top, bottom, below, tensor(0, place, near))
+    whole = edges(above, top, bottom, below, tensor(0, near))
     far = lax.all_to_all(after(far, near), "tm", 0, 0, tiled=True).reshape(640, FAR)
-    return tensor(1, place, near, above, below, far, whole)
+    return tensor(1, near, above, below, far, whole)
 
 
 def solution(mesh):

time: 198 us -> 196 us (0.990)
  Pallas kernels: 37.1 us -> 34.3 us
where the time goes in v7:
time: 196 us
  blocking collectives  108 us (55%)
  Pallas kernels  34.3 us (17%)
  waiting for transfers between devices  30.4 us (16%)
  starting transfers between devices  18.2 us (9%)
  between operations  2.2 us (1%)
    all_to_all x1, blocking collectives, per_device(): pencil = lax.all_to_all(spectra, ('chan', 'tm'), 0, 0, tiled=True)  43.9 us
    all_to_all x1, blocking collectives, per_device(): back = lax.all_to_all(passed, ('chan', 'tm'), 0, 0, tiled=True)  40.2 us
    all_to_all x1, waiting for transfers between devices, per_device(): lax.all_to_all(record.reshape(8, ROWS, 2048), 'tm', 0, 0, tiled=True)  28 us
    all_to_all x1, blocking collectives, per_device(): near = lax.all_to_all(near, 'tm', 0, 0, tiled=True)  24.1 us
    pallas_call x4, Pallas kernels, call(): pl.pallas_call(kernel, out_shape=out, in_specs=[VMEM] * len(args), out_sp...  21.5 us
    pallas_call x2, Pallas kernels, tensor(): pl.pallas_call(functools.partial(tensor_kernel, half), grid=(640 // BAND,...  11.3 us
    all_to_all x1, starting transfers between devices, per_device(): lax.all_to_all(record.reshape(8, ROWS, 2048), 'tm', 0, 0, tiled=True)  7.02 us
    ppermute x1, starting transfers between devices, per_device(): above = lax.ppermute(bottom, 'chan', down)  5.53 us
  transfers between devices with their start and end apart: 4, of which 2 were waited for; matrix products, arithmetic and copies ran while one was open for 1% of the time, Pallas kernels for 4%

profile of v7, /device:TPU:1, one launch (start us, length us, event | category | flops | bytes accessed | tf_op | source)
XLA Modules:
  0.0 195.5 jit_solution(1999158682995377299)
XLA Ops:
  0.0 0.0 copy-start.9
  0.0 0.0 copy-start.12
  0.0 0.0 copy-start.13
  0.0 7.0 %all-to-all-start = ((bf16[8,80,2048]{2,1,0:T(8,128)(2,1)}), bf16[8,80,2048]{2,1,0:T(8,128)(2,1)S(1)}, u32[]{:S(2)}, u32[]{:S(2)}) async-start(bf16[8,80,2048]{2,1,0:T(8,128)(2,1)} %bitcast.13), calls=%async_computation | async-start | bytes 5242880 | tf_op jit(solution)/shard_map/all_to_all | solution.py:802
  7.1 0.0 copy-done.15
  7.1 0.6 dynamic_slice.10
  9.0 0.0 copy-done.14
  9.6 0.1 constant_dynamic-slice_fusion
  9.7 0.1 copy.25
  9.8 0.8 dynamic-slice_convert_fusion
  10.6 0.1 slice_reduce_fusion
  10.7 0.1 broadcast_in_dim.26
  10.8 0.1 fusion.2
  10.9 28.0 %all-to-all-done.x_ref = bf16[8,80,2048]{2,1,0:T(8,128)(2,1)S(1)} async-done(((bf16[8,80,2048]{2,1,0:T(8,128)(2,1)}), bf16[8,80,2048]{2,1,0:T(8,128)(2,1)S(1)}, u32[]{:S(2)}, u32[]{:S(2)}) %all-to-all-start) | async-done | bytes 2621472 | tf_op jit(solution)/shard_map/all_to_all | solution.py:802
  38.8 0.1 iota.7.packed_ref.first_ref
  38.9 0.1 broadcast_in_dim.24.ok_ref
  39.0 0.1 broadcast_in_dim.30.high_ref
  39.0 0.1 broadcast_in_dim.28.low_ref
  39.1 0.0 copy-done.8
  39.1 0.0 copy-done.9
  39.1 0.0 copy-done.12
  39.1 0.0 copy-done.13
  39.2 6.0 %shard_map.190 = bf16[128,80,128]{2,1,0:T(8,128)(2,1)S(1)} custom-call(bf16[8,80,2048]{2,1,0:T(8,128)(2,1)S(1)} %all-to-all-done.x_ref, f32[80,128]{1,0:T(8,128)S(1)} %broadcast_in_dim.24.ok_ref, s32[72,128]{1,0:T(8,128)S(1)} %broadcast_in_dim.28.low_ref, s32[72,128]{1,0:T(8,128)S(1)} %broadcast_in_dim.30.high_ref, f32[8,128]{1,0:T(8,128)S(1)} %iota.7.packed_ref.first_ref, ...), custom_call_target="tpu_custom_call" | custom-call | flops 4000000000 | bytes 6475776 | tf_op jit(solution)/shard_map/pallas_call | solution.py:656
  45.1 0.0 copy-start.6
  45.2 0.0 copy-start.7
  45.2 0.0 copy-start.10
  45.2 0.0 copy-start.11
  45.2 43.9 %all_to_all.25.in_ref = bf16[128,80,128]{2,1,0:T(8,128)(2,1)S(1)} all-to-all(bf16[128,80,128]{2,1,0:T(8,128)(2,1)S(1)} %shard_map.190), channel_id=1, replica_groups=mesh['chan'=16,'tm'=8] {'chan','tm'}, dimensions={0} | all-to-all | bytes 5242880 | tf_op jit(solution)/shard_map/all_to_all | solution.py:809
  89.1 0.0 copy-done.6
  89.1 0.0 copy-done.7
  89.1 11.6 %shard_map.191 = bf16[128,80,128]{2,1,0:T(8,128)(2,1)S(1)} custom-call(bf16[128,80,128]{2,1,0:T(8,128)(2,1)S(1)} %all_to_all.25.in_ref, s32[72,128]{1,0:T(8,128)S(1)} %broadcast_in_dim.28.low_ref, s32[72,128]{1,0:T(8,128)S(1)} %broadcast_in_dim.30.high_ref, f32[8,128]{1,0:T(8,128)S(1)} %iota.7.packed_ref.first_ref, f32[80,128]{1,0:T(8,128)S(1)} %copy-done.11, ...), custom_call_target="tpu_custom_call" | custom-call | flops 8000000000 | bytes 6451200 | tf_op jit(solution)/shard_map/pallas_call | solution.py:656
  100.7 0.0 copy-start.4
  100.8 0.0 copy-start.5
  100.8 40.2 %all_to_all.26.in_ref = bf16[128,80,128]{2,1,0:T(8,128)(2,1)S(1)} all-to-all(bf16[128,80,128]{2,1,0:T(8,128)(2,1)S(1)} %shard_map.191), channel_id=1, replica_groups=mesh['chan'=16,'tm'=8] {'chan','tm'}, dimensions={0} | all-to-all | bytes 5242880 | tf_op jit(solution)/shard_map/all_to_all | solution.py:811
  140.9 0.0 copy-done.5
  140.9 3.9 %shard_map.192 = (bf16[8,848,128]{2,1,0:T(8,128)(2,1)S(1)}, bf16[8,80,896]{2,1,0:T(8,128)(2,1)S(1)}) custom-call(bf16[128,80,128]{2,1,0:T(8,128)(2,1)S(1)} %all_to_all.26.in_ref, f32[64,128]{1,0:T(8,128)S(1)} %copy-done.13, f32[64,128]{1,0:T(8,128)S(1)} %copy-done.12, bf16[2,256,256]{2,1,0:T(8,128)(2,1)S(1)} %copy-done.5, bf16[2,256,256]{2,1,0:T(8,128)(2,1)S(1)} %copy-done.4), custom_call_target="tpu_custom_call" | custom-call | flops 4000000000 | bytes 6356992 | tf_op jit(solution)/shard_map/pallas_call | solution.py:656
  144.9 24.1 %all_to_all.27.near_ref.sign_ref.refs_0_ = bf16[8,848,128]{2,1,0:T(8,128)(2,1)} all-to-all(bf16[8,848,128]{2,1,0:T(8,128)(2,1)S(1)} %get-tuple-element.9), channel_id=1, replica_groups=mesh['chan'=16,'tm'=8] {'tm'}, dimensions={0} | all-to-all | bytes 3473408 | tf_op jit(solution)/shard_map/all_to_all | solution.py:813
  169.0 0.0 copy-done.1
  169.0 0.0 copy-start.3
  169.0 3.7 %all-to-all-start.4 = ((bf16[8,80,896]{2,1,0:T(8,128)(2,1)}), bf16[8,80,896]{2,1,0:T(8,128)(2,1)S(1)}, u32[]{:S(2)}, u32[]{:S(2)}) async-start(bf16[8,80,896]{2,1,0:T(8,128)(2,1)} %shard_map.194), calls=%async_computation.4 | async-start | bytes 2293760 | tf_op jit(solution)/shard_map/all_to_all | solution.py:820
  172.8 5.5 %collective-permute-start = (bf16[272,128]{1,0:T(8,128)(2,1)S(1)}, bf16[272,128]{1,0:T(8,128)(2,1)S(1)}, u32[]{:S(2)}, u32[]{:S(2)}) collective-permute-start(bf16[272,128]{1,0:T(8,128)(2,1)S(1)} %get-tuple-element.10.bottom_ref), channel_id=1, source_target_pairs={{0,8},{8,16},{16,24},{24,32},{32,40},{40,48},{48,56},{56,64},{64,7... | collective-permute-start | bytes 208904 | tf_op jit(solution)/shard_map/ppermute | solution.py:817
  178.3 1.9 collective-permute-start.1
  180.2 5.7 %shard_map.195._ = f32[640,2048]{1,0:T(8,128)} custom-call(bf16[8,848,128]{2,1,0:T(8,128)(2,1)S(1)} %copy-done, bf16[256,256]{1,0:T(8,128)(2,1)S(1)} %copy-done.3, bf16[256,256]{1,0:T(8,128)(2,1)S(1)} %copy-done.2), custom_call_target="tpu_custom_call" | custom-call | flops 1000000000 | bytes 9437184 | tf_op jit(solution)/shard_map/pallas_call | solution.py:738
  185.9 0.0 collective-permute-done.above_ref.refs_1_
  185.9 2.5 %collective-permute-done.1.below_ref.refs_2_ = bf16[272,128]{1,0:T(8,128)(2,1)S(1)} collective-permute-done((bf16[272,128]{1,0:T(8,128)(2,1)S(1)}, bf16[272,128]{1,0:T(8,128)(2,1)S(1)}, u32[]{:S(2)}, u32[]{:S(2)}) %collective-permute-start.1) | collective-permute-done | bytes 69664 | tf_op jit(solution)/shard_map/ppermute | solution.py:818
  188.4 1.5 shard_map.196.refs_6_
  189.9 0.0 all-to-all-done.4
  189.9 5.6 %shard_map.197 = f32[640,2048]{1,0:T(8,128)} custom-call(bf16[8,848,128]{2,1,0:T(8,128)(2,1)S(1)} %copy-done, bf16[272,128]{1,0:T(8,128)(2,1)S(1)} %collective-permute-done.above_ref.refs_1_, bf16[272,128]{1,0:T(8,128)(2,1)S(1)} %collective-permute-done.1.below_ref.refs_2_, bf16[640,896]{1,0:T(8,128)(2,1)S(1)} %bitcast.12, ...), custom_call_target="tpu_custom_call", output_to_operand_aliasing={{}: (6, {})} | custom-call | flops 1000000000 | bytes 9437184 | tf_op jit(solution)/shard_map/pallas_call | solution.py:738
  (17 shorter events, 0.1 us)
Async XLA Ops:
  0.0 7.1 %copy-start.15 = (s32[128]{0:T(128)S(1)}, s32[128]{0:T(128)}, u32[]{:S(2)}) copy-start(s32[128]{0:T(128)} %constant.46.clone) | copy-start | bytes 1540
  0.0 9.0 %copy-start.14 = (s32[2,8193]{1,0:T(2,128)S(1)}, s32[2,8193]{1,0:T(2,128)}, u32[]{:S(2)}) copy-start(s32[2,8193]{1,0:T(2,128)} %param.22) | copy-start | bytes 196636
  0.0 39.1 %copy-start.8 = (bf16[2,256,256]{2,1,0:T(8,128)(2,1)S(1)}, bf16[2,256,256]{2,1,0:T(8,128)(2,1)}, u32[]{:S(2)}) copy-start(bf16[2,256,256]{2,1,0:T(8,128)(2,1)} %constant.50.clone.w0_ref) | copy-start | bytes 786436
  0.0 39.1 %copy-start.9 = (bf16[2,256,256]{2,1,0:T(8,128)(2,1)S(1)}, bf16[2,256,256]{2,1,0:T(8,128)(2,1)}, u32[]{:S(2)}) copy-start(bf16[2,256,256]{2,1,0:T(8,128)(2,1)} %constant.49.clone.w_ref) | copy-start | bytes 786436
  0.0 39.1 %copy-start.12 = (f32[64,128]{1,0:T(8,128)S(1)}, f32[64,128]{1,0:T(8,128)}, u32[]{:S(2)}) copy-start(f32[64,128]{1,0:T(8,128)} %constant.48.clone.ts_ref) | copy-start | bytes 98308
  0.0 39.1 %copy-start.13 = (f32[64,128]{1,0:T(8,128)S(1)}, f32[64,128]{1,0:T(8,128)}, u32[]{:S(2)}) copy-start(f32[64,128]{1,0:T(8,128)} %constant.47.clone.tc_ref) | copy-start | bytes 98308
  0.0 38.8 %all-to-all-start = ((bf16[8,80,2048]{2,1,0:T(8,128)(2,1)}), bf16[8,80,2048]{2,1,0:T(8,128)(2,1)S(1)}, u32[]{:S(2)}, u32[]{:S(2)}) async-start(bf16[8,80,2048]{2,1,0:T(8,128)(2,1)} %bitcast.13), calls=%async_computation | async-start | bytes 5242880 | tf_op jit(solution)/shard_map/all_to_all | solution.py:802
  45.1 44.0 %copy-start.6 = (bf16[2,256,256]{2,1,0:T(8,128)(2,1)S(1)}, bf16[2,256,256]{2,1,0:T(8,128)(2,1)}, u32[]{:S(2)}) copy-start(bf16[2,256,256]{2,1,0:T(8,128)(2,1)} %constant.54.clone.v_ref) | copy-start | bytes 786436
  45.2 44.0 %copy-start.7 = (bf16[2,256,256]{2,1,0:T(8,128)(2,1)S(1)}, bf16[2,256,256]{2,1,0:T(8,128)(2,1)}, u32[]{:S(2)}) copy-start(bf16[2,256,256]{2,1,0:T(8,128)(2,1)} %constant.53.clone.w_ref) | copy-start | bytes 786436
  45.2 43.9 %copy-start.10 = (f32[80,128]{1,0:T(8,128)S(1)}, f32[80,128]{1,0:T(8,128)}, u32[]{:S(2)}) copy-start(f32[80,128]{1,0:T(8,128)} %constant.52.clone.ts_ref) | copy-start | bytes 122884
  45.2 43.9 %copy-start.11 = (f32[80,128]{1,0:T(8,128)S(1)}, f32[80,128]{1,0:T(8,128)}, u32[]{:S(2)}) copy-start(f32[80,128]{1,0:T(8,128)} %constant.51.clone.tc_ref) | copy-start | bytes 122884
  100.7 40.2 %copy-start.4 = (bf16[2,256,256]{2,1,0:T(8,128)(2,1)S(1)}, bf16[2,256,256]{2,1,0:T(8,128)(2,1)}, u32[]{:S(2)}) copy-start(bf16[2,256,256]{2,1,0:T(8,128)(2,1)} %constant.56.clone.w0_ref) | copy-start | bytes 786436
  100.8 40.2 %copy-start.5 = (bf16[2,256,256]{2,1,0:T(8,128)(2,1)S(1)}, bf16[2,256,256]{2,1,0:T(8,128)(2,1)}, u32[]{:S(2)}) copy-start(bf16[2,256,256]{2,1,0:T(8,128)(2,1)} %constant.55.clone.w_ref) | copy-start | bytes 786436
  144.9 24.1 %copy-start.1 = (bf16[8,80,896]{2,1,0:T(8,128)(2,1)}, bf16[8,80,896]{2,1,0:T(8,128)(2,1)S(1)}, u32[]{:S(2)}) copy-start(bf16[8,80,896]{2,1,0:T(8,128)(2,1)S(1)} %get-tuple-element.12.value_ref) | copy-start | bytes 3440644
  169.0 3.7 %copy-start = (bf16[8,848,128]{2,1,0:T(8,128)(2,1)S(1)}, bf16[8,848,128]{2,1,0:T(8,128)(2,1)}, u32[]{:S(2)}) copy-start(bf16[8,848,128]{2,1,0:T(8,128)(2,1)} %all_to_all.27.near_ref.sign_ref.refs_0_) | copy-start | bytes 5210116
  169.0 11.2 %copy-start.2 = (bf16[256,256]{1,0:T(8,128)(2,1)S(1)}, bf16[256,256]{1,0:T(8,128)(2,1)}, u32[]{:S(2)}) copy-start(bf16[256,256]{1,0:T(8,128)(2,1)} %constant.58.clone.refs_2_.refs_5_) | copy-start | bytes 393220
  169.0 11.2 %copy-start.3 = (bf16[256,256]{1,0:T(8,128)(2,1)S(1)}, bf16[256,256]{1,0:T(8,128)(2,1)}, u32[]{:S(2)}) copy-start(bf16[256,256]{1,0:T(8,128)(2,1)} %constant.57.clone.refs_1_.refs_4_) | copy-start | bytes 393220
  169.0 20.9 %all-to-all-start.4 = ((bf16[8,80,896]{2,1,0:T(8,128)(2,1)}), bf16[8,80,896]{2,1,0:T(8,128)(2,1)S(1)}, u32[]{:S(2)}, u32[]{:S(2)}) async-start(bf16[8,80,896]{2,1,0:T(8,128)(2,1)} %shard_map.194), calls=%async_computation.4 | async-start | bytes 2293760 | tf_op jit(solution)/shard_map/all_to_all | solution.py:820
  172.8 13.2 %collective-permute-start = (bf16[272,128]{1,0:T(8,128)(2,1)S(1)}, bf16[272,128]{1,0:T(8,128)(2,1)S(1)}, u32[]{:S(2)}, u32[]{:S(2)}) collective-permute-start(bf16[272,128]{1,0:T(8,128)(2,1)S(1)} %get-tuple-element.10.bottom_ref), channel_id=1, source_target_pairs={{0,8},{8,16},{16,24},{24,32},{32,40},{40,48},{48,56},{56,64},{64,7... | collective-permute-start | bytes 208904 | tf_op jit(solution)/shard_map/ppermute | solution.py:817
  178.3 10.1 %collective-permute-start.1 = (bf16[272,128]{1,0:T(8,128)(2,1)S(1)}, bf16[272,128]{1,0:T(8,128)(2,1)S(1)}, u32[]{:S(2)}, u32[]{:S(2)}) collective-permute-start(bf16[272,128]{1,0:T(8,128)(2,1)S(1)} %get-tuple-element.11.top_ref), channel_id=1, source_target_pairs={{8,0},{16,8},{24,16},{32,24},{40,32},{48,40},{56,48},{64,56},{72,6... | collective-permute-start | bytes 208904 | tf_op jit(solution)/shard_map/ppermute | solution.py:818

commit v8 on v7

--- a/solution.py
+++ b/solution.py
@@ -16,10 +16,10 @@
 TF = 128
 R = 4
 GROUP = 63
-SIDE = 9 * ROWS
+SIDE = 8 * ROWS
 OUTER = SIDE + 16
-NEAR = OUTER + 7 * 16
-FAR = 896
+NEAR = OUTER + 8 * 16
+FAR = 1024
 BF = jnp.bfloat16
 F32 = jnp.float32
 VMEM = pl.BlockSpec(memory_space=pltpu.VMEM)
@@ -352,11 +352,11 @@
         for a in range(16):
             ys = series(a)
             for s in range(8):
-                if a < 9:
+                if a < 8:
                     near_ref[s, pl.ds(a * ROWS + tile * 16, 16), :] = ys[s]
                 else:
-                    far_ref[s, rows, (a - 9) * 128 : (a - 8) * 128] = ys[s]
-            if a in (0, 15):
+                    far_ref[s, rows, (a - 8) * 128 : (a - 7) * 128] = ys[s]
+            if a in (0, 8, 15):
                 ends[a] = ys
         blank = jnp.zeros((16, 128), BF)
         for s in range(8):
@@ -365,10 +365,13 @@
             both = jnp.where(lane < 64, after.astype(F32), before.astype(F32))
             here = ((lane - 16 * tile + 5) & 127) < 10
             sides[s] = jnp.where(here, pltpu.roll(both, 16 * tile, 1), sides[s])
+            here = ((lane - 16 * tile - 5) & 127) < 5
+            middle = pltpu.roll(ends[8][s].astype(F32), 16 * tile + 5, 1)
+            sides[s] = jnp.where(here, middle, sides[s])
     base = pl.multiple_of(jnp.where(lax.axis_index("tm") == 7, 64, 0), 16)
     for s in range(8):
         near_ref[s, pl.ds(SIDE, 16), :] = sides[s].astype(BF)
-        for n in range(7):
+        for n in range(8):
             near_ref[s, pl.ds(OUTER + 16 * n, 16), :] = far_ref[
                 s, pl.ds(base, 16), n * 128 : (n + 1) * 128
             ]
@@ -504,22 +507,22 @@
     chan, part = lax.axis_index("chan"), lax.axis_index("tm")
 
     def column(t):
-        if t in (-1, 16):
+        if t in (-1, 16) or (half == 0 and t == 8):
             parts = []
+            skip = 5 if t == 8 else 0
             for j in range(8):
                 side = near_ref[j, pl.ds(SIDE, 16), :].astype(F32)
-                parts.append(side.astype(BF))
-                for n in range(1, 5):
-                    parts.append(pltpu.roll(side, 128 - 16 * n, 1).astype(BF))
+                for n in range(5):
+                    parts.append(pltpu.roll(side, (-16 * n - skip) % 128, 1).astype(BF))
             if half == 1:
-                first = pltpu.roll(above_ref[pl.ds(144, 16), :].astype(F32), 64, 1).astype(BF)
-                parts = [first] + parts + [below_ref[pl.ds(144, 16), :]]
+                first = pltpu.roll(above_ref[pl.ds(128, 16), :].astype(F32), 64, 1).astype(BF)
+                parts = [first] + parts + [below_ref[pl.ds(128, 16), :]]
             return jnp.concatenate(parts, axis=0)
-        rows = pl.ds(16 * t if t < 9 else 160 + 16 * (t - 9), 16)
-        if t < 9:
+        rows = pl.ds(16 * t if t < 8 else 144 + 16 * (t - 8), 16)
+        if t < 8:
             inner = [near_ref[j, pl.ds(t * ROWS, ROWS), :] for j in range(8)]
         else:
-            inner = [far_ref[:, (t - 9) * 128 : (t - 8) * 128]]
+            inner = [far_ref[:, (t - 8) * 128 : (t - 7) * 128]]
         if half == 1:
             inner = [above_ref[rows, :]] + inner + [below_ref[rows, :]]
         return jnp.concatenate(inner, axis=0)
@@ -605,8 +608,10 @@
 
     def spread(start, ref, turned):
         rows = pl.ds(start, 16)
-        wide[0, rows, :] = pltpu.roll(ref[pl.ds(144, 16), :].astype(F32), turned, 1)
-        for t in range(9):
+        side = ref[pl.ds(128, 16), :].astype(F32)
+        wide[0, rows, :] = pltpu.roll(side, turned, 1)
+        wide[9, rows, :] = pltpu.roll(side, (turned - 5) % 128, 1)
+        for t in range(8):
             wide[t + 1, rows, :] = ref[pl.ds(16 * t, 16), :].astype(F32)
 
     @pl.when(step == 0)
@@ -791,9 +796,9 @@
 
 def outer_kernel(near_ref, top_ref, bottom_ref):
     for ref, source, first in ((top_ref, 0, 0), (bottom_ref, 7, 64)):
-        for t in range(9):
+        for t in range(8):
             ref[pl.ds(16 * t, 16), :] = near_ref[source, pl.ds(t * ROWS + first, 16), :]
-        ref[pl.ds(144, 128), :] = near_ref[source, pl.ds(SIDE, 128), :]
+        ref[pl.ds(128, 144), :] = near_ref[source, pl.ds(SIDE, 144), :]
 
 
 def per_device(record, channel_ok, fan_bounds):

time: 196 us -> 197 us (level)
  transfers between devices with their start and end apart: 4 -> 4, of which waited for: 2 -> 3; matrix products, arithmetic and copies ran while one was open for 1% -> 1% of each run, Pallas kernels for 4% -> 4%
where the time goes in v8:
time: 197 us; the launch traced here: 196 us
  blocking collectives  107 us (54%)
  Pallas kernels  34.4 us (17%)
  waiting for transfers between devices  32.3 us (16%)
  starting transfers between devices  17.7 us (9%)
  between operations  2.2 us (1%)
    all_to_all x1, blocking collectives, per_device(): pencil = lax.all_to_all(spectra, ('chan', 'tm'), 0, 0, tiled=True)  43.9 us
    all_to_all x1, blocking collectives, per_device(): back = lax.all_to_all(passed, ('chan', 'tm'), 0, 0, tiled=True)  40.2 us
    all_to_all x1, waiting for transfers between devices, per_device(): lax.all_to_all(record.reshape(8, ROWS, 2048), 'tm', 0, 0, tiled=True)  28 us
    all_to_all x1, blocking collectives, per_device(): near = lax.all_to_all(near, 'tm', 0, 0, tiled=True)  23.4 us
    pallas_call x4, Pallas kernels, call(): pl.pallas_call(kernel, out_shape=out, in_specs=[VMEM] * len(args), out_sp...  21.5 us
    pallas_call x2, Pallas kernels, tensor(): pl.pallas_call(functools.partial(tensor_kernel, half), grid=(640 // BAND,...  11.3 us
    all_to_all x1, starting transfers between devices, per_device(): lax.all_to_all(record.reshape(8, ROWS, 2048), 'tm', 0, 0, tiled=True)  7.02 us
    ppermute x1, starting transfers between devices, per_device(): above = lax.ppermute(bottom, 'chan', down)  5.05 us
  transfers between devices with their start and end apart: 4, of which 3 were waited for; matrix products, arithmetic and copies ran while one was open for 1% of the time, Pallas kernels for 4%

profile of v8, /device:TPU:1, one launch (start us, length us, event | category | flops | bytes accessed | tf_op | source)
XLA Modules:
  0.0 196.1 jit_solution(7651170685545180069)
XLA Ops:
  0.0 0.0 copy-start.9
  0.0 0.0 copy-start.12
  0.0 0.0 copy-start.13
  0.0 7.0 %all-to-all-start = ((bf16[8,80,2048]{2,1,0:T(8,128)(2,1)}), bf16[8,80,2048]{2,1,0:T(8,128)(2,1)S(1)}, u32[]{:S(2)}, u32[]{:S(2)}) async-start(bf16[8,80,2048]{2,1,0:T(8,128)(2,1)} %bitcast.13), calls=%async_computation | async-start | bytes 5242880 | tf_op jit(solution)/shard_map/all_to_all | solution.py:807
  7.1 0.0 copy-done.15
  7.1 0.6 dynamic_slice.10
  9.0 0.0 copy-done.14
  9.6 0.1 constant_dynamic-slice_fusion
  9.7 0.1 copy.25
  9.8 0.8 dynamic-slice_convert_fusion
  10.6 0.1 slice_reduce_fusion
  10.7 0.1 broadcast_in_dim.26
  10.8 0.1 fusion.2
  10.9 28.0 %all-to-all-done.x_ref = bf16[8,80,2048]{2,1,0:T(8,128)(2,1)S(1)} async-done(((bf16[8,80,2048]{2,1,0:T(8,128)(2,1)}), bf16[8,80,2048]{2,1,0:T(8,128)(2,1)S(1)}, u32[]{:S(2)}, u32[]{:S(2)}) %all-to-all-start) | async-done | bytes 2621472 | tf_op jit(solution)/shard_map/all_to_all | solution.py:807
  38.8 0.1 iota.7.packed_ref.first_ref
  38.9 0.1 broadcast_in_dim.24.ok_ref
  39.0 0.1 broadcast_in_dim.30.high_ref
  39.0 0.1 broadcast_in_dim.28.low_ref
  39.1 0.0 copy-done.8
  39.1 0.0 copy-done.9
  39.1 0.0 copy-done.12
  39.1 0.0 copy-done.13
  39.2 6.0 %shard_map.190 = bf16[128,80,128]{2,1,0:T(8,128)(2,1)S(1)} custom-call(bf16[8,80,2048]{2,1,0:T(8,128)(2,1)S(1)} %all-to-all-done.x_ref, f32[80,128]{1,0:T(8,128)S(1)} %broadcast_in_dim.24.ok_ref, s32[72,128]{1,0:T(8,128)S(1)} %broadcast_in_dim.28.low_ref, s32[72,128]{1,0:T(8,128)S(1)} %broadcast_in_dim.30.high_ref, f32[8,128]{1,0:T(8,128)S(1)} %iota.7.packed_ref.first_ref, ...), custom_call_target="tpu_custom_call" | custom-call | flops 4000000000 | bytes 6475776 | tf_op jit(solution)/shard_map/pallas_call | solution.py:661
  45.1 0.0 copy-start.6
  45.2 0.0 copy-start.7
  45.2 0.0 copy-start.10
  45.2 0.0 copy-start.11
  45.2 43.9 %all_to_all.25.in_ref = bf16[128,80,128]{2,1,0:T(8,128)(2,1)S(1)} all-to-all(bf16[128,80,128]{2,1,0:T(8,128)(2,1)S(1)} %shard_map.190), channel_id=1, replica_groups=mesh['chan'=16,'tm'=8] {'chan','tm'}, dimensions={0} | all-to-all | bytes 5242880 | tf_op jit(solution)/shard_map/all_to_all | solution.py:814
  89.1 0.0 copy-done.6
  89.1 0.0 copy-done.7
  89.1 11.6 %shard_map.191 = bf16[128,80,128]{2,1,0:T(8,128)(2,1)S(1)} custom-call(bf16[128,80,128]{2,1,0:T(8,128)(2,1)S(1)} %all_to_all.25.in_ref, s32[72,128]{1,0:T(8,128)S(1)} %broadcast_in_dim.28.low_ref, s32[72,128]{1,0:T(8,128)S(1)} %broadcast_in_dim.30.high_ref, f32[8,128]{1,0:T(8,128)S(1)} %iota.7.packed_ref.first_ref, f32[80,128]{1,0:T(8,128)S(1)} %copy-done.11, ...), custom_call_target="tpu_custom_call" | custom-call | flops 8000000000 | bytes 6451200 | tf_op jit(solution)/shard_map/pallas_call | solution.py:661
  100.7 0.0 copy-start.4
  100.8 0.0 copy-start.5
  100.8 40.2 %all_to_all.26.in_ref = bf16[128,80,128]{2,1,0:T(8,128)(2,1)S(1)} all-to-all(bf16[128,80,128]{2,1,0:T(8,128)(2,1)S(1)} %shard_map.191), channel_id=1, replica_groups=mesh['chan'=16,'tm'=8] {'chan','tm'}, dimensions={0} | all-to-all | bytes 5242880 | tf_op jit(solution)/shard_map/all_to_all | solution.py:816
  140.9 0.0 copy-done.5
  140.9 3.9 %shard_map.192 = (bf16[8,784,128]{2,1,0:T(8,128)(2,1)S(1)}, bf16[8,80,1024]{2,1,0:T(8,128)(2,1)S(1)}) custom-call(bf16[128,80,128]{2,1,0:T(8,128)(2,1)S(1)} %all_to_all.26.in_ref, f32[64,128]{1,0:T(8,128)S(1)} %copy-done.13, f32[64,128]{1,0:T(8,128)S(1)} %copy-done.12, bf16[2,256,256]{2,1,0:T(8,128)(2,1)S(1)} %copy-done.5, bf16[2,256,256]{2,1,0:T(8,128)(2,1)S(1)} %copy-done.4), custom_call_target="tpu_custom_call" | custom-call | flops 4000000000 | bytes 6356992 | tf_op jit(solution)/shard_map/pallas_call | solution.py:661
  144.9 23.4 %all_to_all.27.near_ref.sign_ref.refs_0_ = bf16[8,784,128]{2,1,0:T(8,128)(2,1)} all-to-all(bf16[8,784,128]{2,1,0:T(8,128)(2,1)S(1)} %get-tuple-element.9), channel_id=1, replica_groups=mesh['chan'=16,'tm'=8] {'tm'}, dimensions={0} | all-to-all | bytes 3211264 | tf_op jit(solution)/shard_map/all_to_all | solution.py:818
  168.3 0.0 copy-done.1
  168.3 0.0 copy-start.3
  168.3 3.7 %all-to-all-start.4 = ((bf16[8,80,1024]{2,1,0:T(8,128)(2,1)}), bf16[8,80,1024]{2,1,0:T(8,128)(2,1)S(1)}, u32[]{:S(2)}, u32[]{:S(2)}) async-start(bf16[8,80,1024]{2,1,0:T(8,128)(2,1)} %shard_map.194), calls=%async_computation.4 | async-start | bytes 2621440 | tf_op jit(solution)/shard_map/all_to_all | solution.py:825
  172.0 5.1 %collective-permute-start = (bf16[272,128]{1,0:T(8,128)(2,1)S(1)}, bf16[272,128]{1,0:T(8,128)(2,1)S(1)}, u32[]{:S(2)}, u32[]{:S(2)}) collective-permute-start(bf16[272,128]{1,0:T(8,128)(2,1)S(1)} %get-tuple-element.10.bottom_ref), channel_id=1, source_target_pairs={{0,8},{8,16},{16,24},{24,32},{32,40},{40,48},{48,56},{56,64},{64,7... | collective-permute-start | bytes 208904 | tf_op jit(solution)/shard_map/ppermute | solution.py:822
  177.1 1.9 collective-permute-start.1
  179.0 5.7 %shard_map.195._ = f32[640,2048]{1,0:T(8,128)} custom-call(bf16[8,784,128]{2,1,0:T(8,128)(2,1)S(1)} %copy-done, bf16[256,256]{1,0:T(8,128)(2,1)S(1)} %copy-done.3, bf16[256,256]{1,0:T(8,128)(2,1)S(1)} %copy-done.2), custom_call_target="tpu_custom_call" | custom-call | flops 1000000000 | bytes 9437184 | tf_op jit(solution)/shard_map/pallas_call | solution.py:743
  184.7 1.5 collective-permute-done.above_ref.refs_1_
  186.2 2.8 %collective-permute-done.1.below_ref.refs_2_ = bf16[272,128]{1,0:T(8,128)(2,1)S(1)} collective-permute-done((bf16[272,128]{1,0:T(8,128)(2,1)S(1)}, bf16[272,128]{1,0:T(8,128)(2,1)S(1)}, u32[]{:S(2)}, u32[]{:S(2)}) %collective-permute-start.1) | collective-permute-done | bytes 69664 | tf_op jit(solution)/shard_map/ppermute | solution.py:823
  189.0 1.5 shard_map.196.refs_6_
  190.5 0.0 all-to-all-done.4
  190.5 5.6 %shard_map.197 = f32[640,2048]{1,0:T(8,128)} custom-call(bf16[8,784,128]{2,1,0:T(8,128)(2,1)S(1)} %copy-done, bf16[272,128]{1,0:T(8,128)(2,1)S(1)} %collective-permute-done.above_ref.refs_1_, bf16[272,128]{1,0:T(8,128)(2,1)S(1)} %collective-permute-done.1.below_ref.refs_2_, bf16[640,1024]{1,0:T(8,128)(2,1)S(1)} %bitcast.12, ...), custom_call_target="tpu_custom_call", output_to_operand_aliasing={{}: (6, {})} | custom-call | flops 1000000000 | bytes 9437184 | tf_op jit(solution)/shard_map/pallas_call | solution.py:743
  (17 shorter events, 0.1 us)
Async XLA Ops:
  0.0 7.1 %copy-start.15 = (s32[128]{0:T(128)S(1)}, s32[128]{0:T(128)}, u32[]{:S(2)}) copy-start(s32[128]{0:T(128)} %constant.46.clone) | copy-start | bytes 1540
  0.0 9.0 %copy-start.14 = (s32[2,8193]{1,0:T(2,128)S(1)}, s32[2,8193]{1,0:T(2,128)}, u32[]{:S(2)}) copy-start(s32[2,8193]{1,0:T(2,128)} %param.22) | copy-start | bytes 196636
  0.0 39.1 %copy-start.8 = (bf16[2,256,256]{2,1,0:T(8,128)(2,1)S(1)}, bf16[2,256,256]{2,1,0:T(8,128)(2,1)}, u32[]{:S(2)}) copy-start(bf16[2,256,256]{2,1,0:T(8,128)(2,1)} %constant.50.clone.w0_ref) | copy-start | bytes 786436
  0.0 39.1 %copy-start.9 = (bf16[2,256,256]{2,1,0:T(8,128)(2,1)S(1)}, bf16[2,256,256]{2,1,0:T(8,128)(2,1)}, u32[]{:S(2)}) copy-start(bf16[2,256,256]{2,1,0:T(8,128)(2,1)} %constant.49.clone.w_ref) | copy-start | bytes 786436
  0.0 39.1 %copy-start.12 = (f32[64,128]{1,0:T(8,128)S(1)}, f32[64,128]{1,0:T(8,128)}, u32[]{:S(2)}) copy-start(f32[64,128]{1,0:T(8,128)} %constant.48.clone.ts_ref) | copy-start | bytes 98308
  0.0 39.1 %copy-start.13 = (f32[64,128]{1,0:T(8,128)S(1)}, f32[64,128]{1,0:T(8,128)}, u32[]{:S(2)}) copy-start(f32[64,128]{1,0:T(8,128)} %constant.47.clone.tc_ref) | copy-start | bytes 98308
  0.0 38.8 %all-to-all-start = ((bf16[8,80,2048]{2,1,0:T(8,128)(2,1)}), bf16[8,80,2048]{2,1,0:T(8,128)(2,1)S(1)}, u32[]{:S(2)}, u32[]{:S(2)}) async-start(bf16[8,80,2048]{2,1,0:T(8,128)(2,1)} %bitcast.13), calls=%async_computation | async-start | bytes 5242880 | tf_op jit(solution)/shard_map/all_to_all | solution.py:807
  45.1 44.0 %copy-start.6 = (bf16[2,256,256]{2,1,0:T(8,128)(2,1)S(1)}, bf16[2,256,256]{2,1,0:T(8,128)(2,1)}, u32[]{:S(2)}) copy-start(bf16[2,256,256]{2,1,0:T(8,128)(2,1)} %constant.54.clone.v_ref) | copy-start | bytes 786436
  45.2 44.0 %copy-start.7 = (bf16[2,256,256]{2,1,0:T(8,128)(2,1)S(1)}, bf16[2,256,256]{2,1,0:T(8,128)(2,1)}, u32[]{:S(2)}) copy-start(bf16[2,256,256]{2,1,0:T(8,128)(2,1)} %constant.53.clone.w_ref) | copy-start | bytes 786436
  45.2 43.9 %copy-start.10 = (f32[80,128]{1,0:T(8,128)S(1)}, f32[80,128]{1,0:T(8,128)}, u32[]{:S(2)}) copy-start(f32[80,128]{1,0:T(8,128)} %constant.52.clone.ts_ref) | copy-start | bytes 122884
  45.2 43.9 %copy-start.11 = (f32[80,128]{1,0:T(8,128)S(1)}, f32[80,128]{1,0:T(8,128)}, u32[]{:S(2)}) copy-start(f32[80,128]{1,0:T(8,128)} %constant.51.clone.tc_ref) | copy-start | bytes 122884
  100.7 40.2 %copy-start.4 = (bf16[2,256,256]{2,1,0:T(8,128)(2,1)S(1)}, bf16[2,256,256]{2,1,0:T(8,128)(2,1)}, u32[]{:S(2)}) copy-start(bf16[2,256,256]{2,1,0:T(8,128)(2,1)} %constant.56.clone.w0_ref) | copy-start | bytes 786436
  100.8 40.2 %copy-start.5 = (bf16[2,256,256]{2,1,0:T(8,128)(2,1)S(1)}, bf16[2,256,256]{2,1,0:T(8,128)(2,1)}, u32[]{:S(2)}) copy-start(bf16[2,256,256]{2,1,0:T(8,128)(2,1)} %constant.55.clone.w_ref) | copy-start | bytes 786436
  144.9 23.4 %copy-start.1 = (bf16[8,80,1024]{2,1,0:T(8,128)(2,1)}, bf16[8,80,1024]{2,1,0:T(8,128)(2,1)S(1)}, u32[]{:S(2)}) copy-start(bf16[8,80,1024]{2,1,0:T(8,128)(2,1)S(1)} %get-tuple-element.12.value_ref) | copy-start | bytes 3932164
  168.3 3.7 %copy-start = (bf16[8,784,128]{2,1,0:T(8,128)(2,1)S(1)}, bf16[8,784,128]{2,1,0:T(8,128)(2,1)}, u32[]{:S(2)}) copy-start(bf16[8,784,128]{2,1,0:T(8,128)(2,1)} %all_to_all.27.near_ref.sign_ref.refs_0_) | copy-start | bytes 4816900
  168.3 10.8 %copy-start.2 = (bf16[256,256]{1,0:T(8,128)(2,1)S(1)}, bf16[256,256]{1,0:T(8,128)(2,1)}, u32[]{:S(2)}) copy-start(bf16[256,256]{1,0:T(8,128)(2,1)} %constant.58.clone.refs_2_.refs_5_) | copy-start | bytes 393220
  168.3 10.8 %copy-start.3 = (bf16[256,256]{1,0:T(8,128)(2,1)S(1)}, bf16[256,256]{1,0:T(8,128)(2,1)}, u32[]{:S(2)}) copy-start(bf16[256,256]{1,0:T(8,128)(2,1)} %constant.57.clone.refs_1_.refs_4_) | copy-start | bytes 393220
  168.3 22.2 %all-to-all-start.4 = ((bf16[8,80,1024]{2,1,0:T(8,128)(2,1)}), bf16[8,80,1024]{2,1,0:T(8,128)(2,1)S(1)}, u32[]{:S(2)}, u32[]{:S(2)}) async-start(bf16[8,80,1024]{2,1,0:T(8,128)(2,1)} %shard_map.194), calls=%async_computation.4 | async-start | bytes 2621440 | tf_op jit(solution)/shard_map/all_to_all | solution.py:825
  172.0 14.2 %collective-permute-start = (bf16[272,128]{1,0:T(8,128)(2,1)S(1)}, bf16[272,128]{1,0:T(8,128)(2,1)S(1)}, u32[]{:S(2)}, u32[]{:S(2)}) collective-permute-start(bf16[272,128]{1,0:T(8,128)(2,1)S(1)} %get-tuple-element.10.bottom_ref), channel_id=1, source_target_pairs={{0,8},{8,16},{16,24},{24,32},{32,40},{40,48},{48,56},{56,64},{64,7... | collective-permute-start | bytes 208904 | tf_op jit(solution)/shard_map/ppermute | solution.py:822
  177.1 11.9 %collective-permute-start.1 = (bf16[272,128]{1,0:T(8,128)(2,1)S(1)}, bf16[272,128]{1,0:T(8,128)(2,1)S(1)}, u32[]{:S(2)}, u32[]{:S(2)}) collective-permute-start(bf16[272,128]{1,0:T(8,128)(2,1)S(1)} %get-tuple-element.11.top_ref), channel_id=1, source_target_pairs={{8,0},{16,8},{24,16},{32,24},{40,32},{48,40},{56,48},{64,56},{72,6... | collective-permute-start | bytes 208904 | tf_op jit(solution)/shard_map/ppermute | solution.py:823
